TPU v7x, 32 devices: a whole 2x2x4 slice. The times are simulated.
32 devices in a mesh: image: 4 (over y, x), crop: 2 (over core), proto: 4 (over z).
Axes of the slice: x: 2, y: 2, z: 4, core: 2. Of those that a mesh axis runs over, the one named last changes fastest.
Arguments:
- teacher_feats: bfloat16 [256, 2, 512], P('image'), may hold values from -4 to 4
- student_feats: bfloat16 [8, 256, 512], P('crop', 'image'), may hold values from -4 to 4
- teacher_protos: bfloat16 [512, 16384], P(None, ('crop', 'proto')), may hold values from -6 to 6
- student_protos: bfloat16 [512, 16384], P(None, ('crop', 'proto')), may hold values from -6 to 6
- pairing: int32 [8, 256], P('crop', 'image'), may hold values from 0 to 1
- row_weight: bfloat16 [8, 256], P('crop', 'image'), may hold values from 0.5 to 4
Outputs:
- feat_grad: float32 [8, 256, 512], P('crop', 'image')
- row_loss: float32 [8, 256], P('crop', 'image')
All inputs are finite; a program needn't handle non-finite values.
Results may differ from a plain program's by a relative error of at most 0.0016.
Values may be sent and summed in bfloat16 or wider, within the bound.
No kernel may reach another device: no remote copies, remote signals or barrier semaphores. Data moves between devices by JAX's collectives and lax.ppermute only.
A program may use at most 64 MiB of HBM per device.

v0:
```python
import jax
import jax.numpy as jnp
from jax import lax
from jax.sharding import PartitionSpec as P

SWEEPS = 3


epsilon = 1e-06
student_softness = 0.1
teacher_softness = 0.04


def unit_rows(raw_rows):
    return raw_rows * lax.rsqrt(jnp.sum(raw_rows * raw_rows, axis=-1, keepdims=True) + epsilon)


def unit_columns(weight_rows):
    entries = weight_rows.astype(jnp.float32)
    return (
        entries * lax.rsqrt(jnp.sum(entries * entries, axis=0, keepdims=True) + epsilon)
    ).astype(jnp.bfloat16)


def finish_rows(raw_rows, back_sum, cross_term, running_sums):
    scales = lax.rsqrt(jnp.sum(raw_rows * raw_rows, axis=-1, keepdims=True) + epsilon)
    along = jnp.sum(raw_rows * back_sum, axis=-1, keepdims=True)
    gradient = scales * back_sum - scales * scales * scales * raw_rows * along
    return (gradient, jnp.log(running_sums) - cross_term)


def column_step(transport_plan):
    return transport_plan / lax.psum(jnp.sum(transport_plan, axis=0), "image")


def row_step(transport_plan):
    return transport_plan / lax.psum(jnp.sum(transport_plan, axis=1), ("crop", "proto"))[:, None]


def shards(teacher_feats, student_feats, teacher_protos, student_protos, pairing, row_weight):
    image_count = teacher_feats.shape[0]
    view_count = teacher_feats.shape[1]
    width = teacher_feats.shape[2]
    local_count = student_feats.shape[0]
    teacher_normalized_rows = (
        unit_rows(teacher_feats.astype(jnp.float32))
        .astype(jnp.bfloat16)
        .reshape(image_count * view_count, width)
    )
    teacher_weight_matrix = unit_columns(teacher_protos)
    student_weight_matrix = unit_columns(student_protos)
    features, picked, weight_rows = (
        lax.all_gather(student_feats, "crop", axis=0, tiled=True),
        lax.all_gather(pairing, "crop", axis=0, tiled=True),
        lax.all_gather(row_weight, "crop", axis=0, tiled=True),
    )
    student_normalized_rows = unit_rows(features.astype(jnp.float32)).astype(jnp.bfloat16)
    score_matrix = (
        jnp.einsum(
            "lbd,dk->lbk",
            student_normalized_rows,
            student_weight_matrix,
            preferred_element_type=jnp.float32,
        )
        / student_softness
    )
    exponent_terms = jnp.exp(score_matrix)
    partial_totals = jnp.sum(exponent_terms, axis=2)
    transport_plan = jnp.exp(
        jnp.dot(teacher_normalized_rows, teacher_weight_matrix, preferred_element_type=jnp.float32)
        / teacher_softness
    )
    running_sums = lax.psum(partial_totals, ("crop", "proto"))
    for sweep_index in range(SWEEPS):
        transport_plan = row_step(column_step(transport_plan))
    targets = transport_plan.astype(jnp.bfloat16).reshape(image_count, view_count, -1)
    selected_entries = jnp.zeros(score_matrix.shape, jnp.float32)
    for view_index in range(view_count):
        selected_entries = jnp.where(
            (picked == view_index)[:, :, None],
            targets[None, :, view_index, :].astype(jnp.float32),
            selected_entries,
        )
    cross_term = jnp.sum(selected_entries * score_matrix, axis=2)
    linear_factors = (
        weight_rows.astype(jnp.float32)[:, :, None]
        * (exponent_terms / running_sums[:, :, None] - selected_entries)
        / student_softness
    ).astype(jnp.bfloat16)
    back_sum = jnp.einsum(
        "lbk,dk->lbd", linear_factors, student_weight_matrix, preferred_element_type=jnp.float32
    )
    raw_rows = student_feats.astype(jnp.float32)
    own_back, own_cross = (
        lax.psum_scatter(back_sum, "crop", scatter_dimension=0, tiled=True),
        lax.psum_scatter(cross_term, "crop", scatter_dimension=0, tiled=True),
    )
    own_back, own_cross = lax.psum((own_back, own_cross), "proto")
    own_totals = lax.dynamic_slice_in_dim(
        running_sums, lax.axis_index("crop") * local_count, local_count, 0
    )
    return finish_rows(raw_rows, own_back, own_cross, own_totals)


def solution(mesh):
    in_specs = (
        P("image", None, None),
        P("crop", "image", None),
        P(None, ("crop", "proto")),
        P(None, ("crop", "proto")),
        P("crop", "image"),
        P("crop", "image"),
    )
    out_specs = (P("crop", "image", None), P("crop", "image"))
    return jax.shard_map(shards, mesh=mesh, in_specs=in_specs, out_specs=out_specs, check_vma=False)
```

profile of v0, /device:TPU:0, one launch (start us, length us, event | category | flops | bytes accessed | tf_op | source)
XLA Modules:
  0.0 182.2 jit_solution(343731333264147463)
XLA Ops:
  7.2 1.1 fusion.33
  8.3 1.1 fusion.34
  9.5 2.0 %fusion.3 = f32[2048]{0:T(1024)S(1)} fusion(bf16[512,2048]{1,0:T(8,128)(2,1)} %param.8), kind=kLoop, calls=%fused_computation.7 | loop fusion | flops 3143680 | bytes 2105344 | tf_op jit(solution)/shard_map/reduce_sum | solution.py:21
  11.5 2.3 %fusion.40 = (f32[2048]{0:T(1024)S(1)}, f32[128,2048]{1,0:T(8,128)S(1)}) fusion(bf16[128,512]{1,0:T(8,128)(2,1)S(1)} %reshape.75, bf16[512,2048]{1,0:T(8,128)(2,1)} %param.8, f32[2048]{0:T(1024)S(1)} %add_rsqrt_fusion.1), kind=kOutput, calls=%fused_computation.67 | convolution fusion | flops 272103424 | bytes 3293184 | tf_op jit(solution)/shard_map/dot_general | solution.py:70
  13.8 11.5 %psum.64 = f32[2048]{0:T(1024)S(1)} all-reduce(f32[2048]{0:T(1024)S(1)} %get-tuple-element.10), channel_id=1, replica_groups=mesh['image'=4,'crop'=2,'proto'=4] {'image'}, use_global_device_ids=true, to_apply=%region_8.0 | all-reduce | flops 2048 | bytes 16384 | tf_op jit(solution)/shard_map/psum | solution.py:33
  25.5 15.4 %psum.65 = f32[128]{0:T(128)S(1)} all-reduce(f32[128]{0:T(128)S(1)} %divide_reduce_fusion), channel_id=1, replica_groups=mesh['image'=4,'crop'=2,'proto'=4] {'crop','proto'}, use_global_device_ids=true, to_apply=%region_10.0 | all-reduce | flops 128 | bytes 1024 | tf_op jit(solution)/shard_map/psum | solution.py:37
  40.9 0.3 fusion.25
  41.2 8.2 %psum.66 = f32[2048]{0:T(1024)S(1)} all-reduce(f32[2048]{0:T(1024)S(1)} %fusion.25), channel_id=1, replica_groups=mesh['image'=4,'crop'=2,'proto'=4] {'image'}, use_global_device_ids=true, to_apply=%region_12.0 | all-reduce | flops 2048 | bytes 16384 | tf_op jit(solution)/shard_map/psum | solution.py:33
  49.4 0.3 fusion.26
  49.7 14.5 %psum.67 = f32[128]{0:T(128)S(1)} all-reduce(f32[128]{0:T(128)S(1)} %fusion.26), channel_id=1, replica_groups=mesh['image'=4,'crop'=2,'proto'=4] {'crop','proto'}, use_global_device_ids=true, to_apply=%region_14.0 | all-reduce | flops 128 | bytes 1024 | tf_op jit(solution)/shard_map/psum | solution.py:37
  64.2 0.3 fusion.27
  64.5 9.2 %psum.68 = f32[2048]{0:T(1024)S(1)} all-reduce(f32[2048]{0:T(1024)S(1)} %fusion.27), channel_id=1, replica_groups=mesh['image'=4,'crop'=2,'proto'=4] {'image'}, use_global_device_ids=true, to_apply=%region_16.0 | all-reduce | flops 2048 | bytes 16384 | tf_op jit(solution)/shard_map/psum | solution.py:33
  73.7 0.4 fusion.28
  74.1 15.3 %psum.69 = f32[128]{0:T(128)S(1)} all-reduce(f32[128]{0:T(128)S(1)} %fusion.28), channel_id=1, replica_groups=mesh['image'=4,'crop'=2,'proto'=4] {'crop','proto'}, use_global_device_ids=true, to_apply=%region_18.19 | all-reduce | flops 128 | bytes 1024 | tf_op jit(solution)/shard_map/psum | solution.py:37
  89.4 0.5 fusion.24
  89.9 0.3 reshape.76
  90.2 0.7 fusion.39
  91.0 1.9 %all-gather.1 = s32[2,4,64]{2,1,0:T(4,128)S(1)} all-gather(s32[1,4,64]{2,1,0:T(4,128)S(1)} %bitcast.25), channel_id=1, replica_groups=mesh['image'=4,'crop'=2,'proto'=4] {'crop'}, dimensions={0}, use_global_device_ids=true | all-gather | bytes 3072 | tf_op jit(solution)/shard_map/all_gather | solution.py:54
  92.8 2.2 %all_gather.10 = bf16[8,64,512]{2,1,0:T(8,128)(2,1)S(1)} all-gather(bf16[4,64,512]{2,1,0:T(8,128)(2,1)S(1)} %copy-done), channel_id=1, replica_groups=mesh['image'=4,'crop'=2,'proto'=4] {'crop'}, dimensions={0}, use_global_device_ids=true | all-gather | bytes 786432 | tf_op jit(solution)/shard_map/all_gather | solution.py:53
  95.0 0.2 fusion.21
  95.2 2.0 %fusion.1 = f32[2048]{0:T(1024)S(1)} fusion(bf16[512,2048]{1,0:T(8,128)(2,1)} %param.9), kind=kLoop, calls=%fused_computation.5 | loop fusion | flops 3143680 | bytes 2105344 | tf_op jit(solution)/shard_map/reduce_sum | solution.py:21
  97.2 0.4 fusion.35
  97.6 3.9 %multiply_reduce_fusion = (f32[8,64]{1,0:T(8,128)S(1)}, f32[8,64]{1,0:T(8,128)S(1)}, f32[8,64,2048]{2,1,0:T(8,128)}) fusion(f32[64,2048]{1,0:T(8,128)S(1)} %get-tuple-element.13, f32[64,2048]{1,0:T(8,128)S(1)} %get-tuple-element.14, pred[8,64]{1,0:T(8,128)(4,1)S(1)} %bitcast.29, pred[8,64]{1,0:T(8,128)(4,1)S(1)} %bitcast.27, ...), kind=kOutput, calls=%fused_computation.9 | convolution fusion | flops 1083964416 | bytes 7879680 | tf_op jit(solution)/shard_map/lbd,dk->lbk/dot_general | solution.py:59
  101.6 14.3 %psum.63 = f32[8,64]{1,0:T(8,128)S(1)} all-reduce(f32[8,64]{1,0:T(8,128)S(1)} %get-tuple-element.3), channel_id=1, replica_groups=mesh['image'=4,'crop'=2,'proto'=4] {'crop','proto'}, use_global_device_ids=true, to_apply=%region_4.0 | all-reduce | flops 512 | bytes 4096 | tf_op jit(solution)/shard_map/psum | solution.py:73
  115.8 1.8 all-gather
  117.6 5.3 %fusion.9 = f32[8,64,512]{2,1,0:T(8,128)} fusion(f32[8,64,2048]{2,1,0:T(8,128)} %get-tuple-element.12, f32[64,2048]{1,0:T(8,128)S(1)} %get-tuple-element.13, f32[64,2048]{1,0:T(8,128)S(1)} %get-tuple-element.14, f32[8,64]{1,0:T(8,128)S(1)} %psum.63, f32[8,64]{1,0:T(8,128)S(1)} %convert.2, pred[8,64]{1,0:T(8,128)(4,1)S(1)} %bitcast.30, ...), kind=kOutput, calls=%fused_computation.17 | convolution fusion | flops 1085276160 | bytes 8401920 | tf_op jit(solution)/shard_map/lbk,dk->lbd/dot_general | solution.py:90
  123.0 0.6 dynamic-slice
  124.2 2.5 %all-reduce = f32[8,64]{1,0:T(8,128)S(1)} all-reduce(f32[8,64]{1,0:T(8,128)S(1)} %get-tuple-element.2), channel_id=3, replica_groups=mesh['image'=4,'crop'=2,'proto'=4] {'crop'}, use_global_device_ids=true, to_apply=%region_23.24.clone | all-reduce | flops 512 | bytes 4096
  126.7 10.6 %psum.71 = f32[4,64]{1,0:T(4,128)S(1)} all-reduce(f32[4,64]{1,0:T(4,128)S(1)} %constant_dynamic-slice_fusion), channel_id=1, replica_groups=mesh['image'=4,'crop'=2,'proto'=4] {'proto'}, use_global_device_ids=true, to_apply=%region_24.25 | all-reduce | flops 256 | bytes 2048 | tf_op jit(solution)/shard_map/psum | solution.py:98
  137.4 0.6 log_subtract_fusion
  138.0 34.8 %all-reduce.3.cloned.1.call-done = f32[4,64,512]{2,1,0:T(8,128)} async-done(((f32[4,64,512]{2,1,0:T(8,128)}), f32[4,64,512]{2,1,0:T(8,128)}) %all-reduce.3.cloned.1.call-update) | async-done | bytes 524304 | tf_op jit(solution)/shard_map/psum | solution.py:98
  172.8 2.5 %fusion.20 = f32[4,64,512]{2,1,0:T(8,128)} fusion(bf16[4,64,512]{2,1,0:T(8,128)(2,1)S(1)} %copy-done, f32[4,64,512]{2,1,0:T(8,128)} %all-reduce.3.cloned.1.call-done, f32[4,64]{1,0:T(4,128)S(1)} %get-tuple-element.9, f32[4,64]{1,0:T(4,128)S(1)} %get-tuple-element.8), kind=kOutput, calls=%fused_computation.30 | output fusion | flops 918271 | bytes 1312768 | tf_op jit(solution)/shard_map/mul | solution.py:28
  (26 shorter events, 0.5 us)
Async XLA Ops:
  7.2 130.1 %reduce-scatter.2.cloned.1.call-start = ((), (), s32[]{:S(2)}) async-start(), calls=%async_computation.1 | async-start | bytes 1572864 | tf_op jit(solution)/shard_map/reduce_scatter | solution.py:95
  41.2 49.8 %copy-start.2 = (s32[4,64]{1,0:T(4,128)S(1)}, s32[4,64]{1,0:T(4,128)}, u32[]{:S(2)}) copy-start(s32[4,64]{1,0:T(4,128)} %param.10) | copy-start | bytes 3076
  41.2 51.7 %copy-start = (bf16[4,64,512]{2,1,0:T(8,128)(2,1)S(1)}, bf16[4,64,512]{2,1,0:T(8,128)(2,1)}, u32[]{:S(2)}) copy-start(bf16[4,64,512]{2,1,0:T(8,128)(2,1)} %param.7) | copy-start | bytes 786436
  90.2 7.4 %copy-start.1 = (bf16[512,2048]{1,0:T(8,128)(2,1)S(1)}, bf16[512,2048]{1,0:T(8,128)(2,1)}, u32[]{:S(2)}) copy-start(bf16[512,2048]{1,0:T(8,128)(2,1)} %param.9) | copy-start | bytes 6291460
  97.6 18.2 %copy-start.3 = (bf16[4,64]{1,0:T(4,128)(2,1)S(1)}, bf16[4,64]{1,0:T(4,128)(2,1)}, u32[]{:S(2)}) copy-start(bf16[4,64]{1,0:T(4,128)(2,1)} %param.11) | copy-start | bytes 1540
  117.6 5.3 %copy-start.4 = (u32[32]{0:T(128)S(1)}, u32[32]{0:T(128)}, u32[]{:S(2)}) copy-start(u32[32]{0:T(128)} %constant.32) | copy-start | bytes 388
  122.9 49.9 %all-reduce.3.cloned.1.call-start = ((), (), s32[]{:S(2)}) async-start(), calls=%async_computation.2 | async-start | bytes 1048576 | tf_op jit(solution)/shard_map/psum | solution.py:98
Sparse Core Ops, SparseCore 0:
  123.0 7.2 reduce-scatter.1
  137.4 35.3 all-reduce.2
where the time goes:
time: 183 us; the launch traced here: 182 us
  blocking collectives  107 us (58%)
  waiting for transfers between devices  34.8 us (19%)
  between operations  14.9 us (8%)
  other arithmetic  12 us (7%)
  matrix products  11.4 us (6%)
    psum x3, blocking collectives, row_step(): lax.psum(jnp.sum(transport_plan, axis=1), ('crop', 'proto'))[:, None]  45.1 us
    psum x1, waiting for transfers between devices, shards(): own_back, own_cross = lax.psum((own_back, own_cross), 'proto')  34.8 us
    psum x3, blocking collectives, column_step(): return transport_plan / lax.psum(jnp.sum(transport_plan, axis=0), 'image')  28.9 us
    psum x1, blocking collectives, shards(): running_sums = lax.psum(partial_totals, ('crop', 'proto'))  14.3 us
    psum x1, blocking collectives, shards(): own_back, own_cross = lax.psum((own_back, own_cross), 'proto')  10.6 us
    dot_general x1, matrix products, shards(): jnp.einsum('lbk,dk->lbd', linear_factors, student_weight_matrix, preferre...  5.26 us
    reduce_sum x2, other arithmetic, unit_columns(): jnp.sum(entries * entries, axis=0, keepdims=True) + epsilon  4.08 us
    dot_general x1, matrix products, shards(): jnp.einsum('lbd,dk->lbk', student_normalized_rows, student_weight_matrix,...  3.92 us
  transfers between devices with their start and end apart: 2, of which 1 were waited for; matrix products, arithmetic and copies ran while one was open for 1% of the time, Pallas kernels for 0%

commit v1 on v0

v1 whole, which is shorter than its diff:
```python
import functools

import jax
import jax.numpy as jnp
from jax import lax
from jax.experimental import pallas as pl
from jax.experimental.pallas import tpu as pltpu
from jax.sharding import PartitionSpec as P

SWEEPS = 3
LANES = 128
VMEM_LIMIT = 40 * 1024 * 1024

epsilon = 1e-06
student_softness = 0.1
teacher_softness = 0.04

F32 = jnp.float32
BF16 = jnp.bfloat16


def unit_rows(raw_rows):
    return raw_rows * lax.rsqrt(jnp.sum(raw_rows * raw_rows, axis=-1, keepdims=True) + epsilon)


def unit_columns(entries):
    return entries * lax.rsqrt(jnp.sum(entries * entries, axis=0, keepdims=True) + epsilon)


def lane_groups(values):
    total = values[:, :LANES]
    for start in range(LANES, values.shape[1], LANES):
        total = total + values[:, start : start + LANES]
    return total


def dot_t(a, b):
    return lax.dot_general(a, b, (((1,), (1,)), ((), ())), preferred_element_type=F32)


def row_vector(partial):
    return jnp.sum(partial.T, axis=0, keepdims=True)


def student_kernel(*refs):
    feats, (protos, unit_protos, back, unit_feats) = refs[:-4], refs[-4:]
    width = protos.shape[0]

    @pl.when(pl.program_id(0) == 0)
    def _():
        start = 0
        for part in feats:
            rows = part.shape[0]
            unit_feats[start : start + rows, :] = unit_rows(part[...].astype(F32)).astype(BF16)
            start += rows
        back[...] = jnp.zeros_like(back)

    weights = unit_columns(protos[...].astype(F32)).astype(BF16)
    unit_protos[...] = weights
    logits = jnp.dot(unit_feats[...], weights, preferred_element_type=F32)
    terms = jnp.exp(logits * (1.0 / student_softness))
    back[:, width:] += lane_groups(terms)
    back[:, :width] += dot_t(terms.astype(BF16), weights)


def student_call(feats, protos, block):
    width, columns = protos.shape
    rows = sum(part.shape[0] for part in feats)
    return pl.pallas_call(
        student_kernel,
        grid=(columns // block,),
        in_specs=[pl.BlockSpec(part.shape, lambda i: (0, 0)) for part in feats]
        + [pl.BlockSpec((width, block), lambda i: (0, i))],
        out_specs=[
            pl.BlockSpec((width, block), lambda i: (0, i)),
            pl.BlockSpec((rows, width + LANES), lambda i: (0, 0)),
        ],
        out_shape=[
            jax.ShapeDtypeStruct((width, columns), BF16),
            jax.ShapeDtypeStruct((rows, width + LANES), F32),
        ],
        scratch_shapes=[pltpu.VMEM((rows, width), BF16)],
        compiler_params=pltpu.CompilerParams(vmem_limit_bytes=VMEM_LIMIT),
        cost_estimate=pl.CostEstimate(
            flops=4 * rows * width * columns, bytes_accessed=4 * width * columns, transcendentals=rows * columns
        ),
        name="student",
    )(*feats, protos)


def first_kernel(*refs):
    parts, (protos, plan, sums, partial) = refs[:-4], refs[-4:]

    @pl.when(pl.program_id(0) == 0)
    def _():
        partial[...] = jnp.zeros_like(partial)

    weights = unit_columns(protos[...].astype(F32)).astype(BF16)
    column_sums = None
    start = 0
    for part in parts:
        rows = part.shape[0]
        values = jnp.exp(
            jnp.dot(part[...], weights, preferred_element_type=F32) * (1.0 / teacher_softness)
        )
        plan[start : start + rows, :] = values
        here = jnp.sum(values, axis=0, keepdims=True)
        column_sums = here if column_sums is None else column_sums + here
        start += rows
    scale = 1.0 / column_sums
    partial[...] += lane_groups(plan[...] * scale)

    @pl.when(pl.program_id(0) == pl.num_programs(0) - 1)
    def _():
        sums[...] = jnp.broadcast_to(row_vector(partial[...]), sums.shape)


def first_call(parts, protos, copies, block):
    width, columns = protos.shape
    rows = sum(part.shape[0] for part in parts)
    return pl.pallas_call(
        first_kernel,
        grid=(columns // block,),
        in_specs=[pl.BlockSpec(part.shape, lambda i: (0, 0)) for part in parts]
        + [pl.BlockSpec((width, block), lambda i: (0, i))],
        out_specs=[
            pl.BlockSpec((rows, block), lambda i: (0, i)),
            pl.BlockSpec((copies, rows), lambda i: (0, 0)),
        ],
        out_shape=[
            jax.ShapeDtypeStruct((rows, columns), F32),
            jax.ShapeDtypeStruct((copies, rows), F32),
        ],
        scratch_shapes=[pltpu.VMEM((rows, LANES), F32)],
        compiler_params=pltpu.CompilerParams(vmem_limit_bytes=VMEM_LIMIT),
        cost_estimate=pl.CostEstimate(
            flops=2 * rows * width * columns, bytes_accessed=6 * rows * columns, transcendentals=rows * columns
        ),
        name="first_sweep",
    )(*parts, protos)


def scale_rows(row_sums, row_scale):
    scale = 1.0 / jnp.sum(row_sums[...], axis=0, keepdims=True)
    row_scale[...] = jnp.broadcast_to(scale, (LANES, scale.shape[1])).T


def column_scale(plan, row_scale):
    scales = []
    for start in range(0, plan.shape[1], LANES):
        weighted = plan[:, start : start + LANES] * row_scale[...]
        scales.append(1.0 / jnp.sum(weighted, axis=0, keepdims=True))
    return scales


def sweep_kernel(row_sums, plan, sums, row_scale, partial):
    @pl.when(pl.program_id(0) == 0)
    def _():
        scale_rows(row_sums, row_scale)
        partial[...] = jnp.zeros_like(partial)

    scales = column_scale(plan, row_scale)
    total = partial[...]
    for j, scale in enumerate(scales):
        total = total + plan[:, j * LANES : (j + 1) * LANES] * scale
    partial[...] = total

    @pl.when(pl.program_id(0) == pl.num_programs(0) - 1)
    def _():
        sums[...] = jnp.broadcast_to(row_vector(partial[...]), sums.shape)


def sweep_call(row_sums, plan, block):
    copies = row_sums.shape[0]
    rows, columns = plan.shape
    return pl.pallas_call(
        sweep_kernel,
        grid=(columns // block,),
        in_specs=[
            pl.BlockSpec((copies, rows), lambda i: (0, 0)),
            pl.BlockSpec((rows, block), lambda i: (0, i)),
        ],
        out_specs=pl.BlockSpec((copies, rows), lambda i: (0, 0)),
        out_shape=jax.ShapeDtypeStruct((copies, rows), F32),
        scratch_shapes=[pltpu.VMEM((rows, LANES), F32)] * 2,
        compiler_params=pltpu.CompilerParams(vmem_limit_bytes=VMEM_LIMIT),
        cost_estimate=pl.CostEstimate(
            flops=4 * rows * columns, bytes_accessed=4 * rows * columns, transcendentals=0
        ),
        name="sweep",
    )(row_sums, plan)


def last_kernel(row_sums, plan, unit_protos, mixed, row_scale):
    own = mixed.shape[0]
    width = unit_protos.shape[0]

    @pl.when(pl.program_id(0) == 0)
    def _():
        scale_rows(row_sums, row_scale)
        mixed[...] = jnp.zeros_like(mixed)

    scales = column_scale(plan, row_scale)
    columns = [
        plan[:own, j * LANES : (j + 1) * LANES] * scale for j, scale in enumerate(scales)
    ]
    values = jnp.concatenate(columns, axis=1)
    mixed[:, width:] += lane_groups(values)
    mixed[:, :width] += dot_t(values.astype(BF16), unit_protos[...])


def last_call(row_sums, plan, unit_protos, own, block):
    copies = row_sums.shape[0]
    rows, columns = plan.shape
    width = unit_protos.shape[0]
    return pl.pallas_call(
        last_kernel,
        grid=(columns // block,),
        in_specs=[
            pl.BlockSpec((copies, rows), lambda i: (0, 0)),
            pl.BlockSpec((rows, block), lambda i: (0, i)),
            pl.BlockSpec((width, block), lambda i: (0, i)),
        ],
        out_specs=pl.BlockSpec((own, width + LANES), lambda i: (0, 0)),
        out_shape=jax.ShapeDtypeStruct((own, width + LANES), F32),
        scratch_shapes=[pltpu.VMEM((rows, LANES), F32)],
        compiler_params=pltpu.CompilerParams(vmem_limit_bytes=VMEM_LIMIT),
        cost_estimate=pl.CostEstimate(
            flops=2 * own * width * columns, bytes_accessed=6 * rows * columns, transcendentals=0
        ),
        name="last_sweep",
    )(row_sums, plan, unit_protos)


def mean_kernel(*refs):
    parts, out = refs[:-1], refs[-1]
    width = out.shape[1]
    total = parts[0][...]
    for part in parts[1:]:
        total = total + part[...]
    out[...] = total[:, :width] / jnp.sum(total[:, width:], axis=1, keepdims=True)


def mean_call(parts, width):
    rows = parts[0].shape[0]
    return pl.pallas_call(
        mean_kernel,
        out_shape=jax.ShapeDtypeStruct((rows, width), F32),
        compiler_params=pltpu.CompilerParams(vmem_limit_bytes=VMEM_LIMIT),
        name="mean_protos",
    )(*parts)


def finish_kernel(views, count, place, feats, picked, weights, back, *refs):
    parts, (gradient, loss, means) = refs[:count], refs[count:]
    width = means.shape[1]
    rows = parts[0].shape[0]
    for k, part in enumerate(parts):
        start = pl.multiple_of(jnp.bitwise_xor(place[0], k) * rows, rows)
        means[pl.ds(start, rows), :] = part[...]
    images = feats.shape[1]
    for crop in range(feats.shape[0]):
        raw = feats[crop].astype(F32)
        chosen = means[:images, :]
        for view in range(1, views):
            chosen = jnp.where(
                picked[:, crop : crop + 1] == view, means[view * images : (view + 1) * images, :], chosen
            )
        here = slice(crop * images, (crop + 1) * images)
        totals = jnp.sum(back[here, width:], axis=1, keepdims=True)
        factor = weights[:, crop : crop + 1] * (1.0 / student_softness)
        back_sum = factor * (back[here, :width] / totals - chosen)
        scales = lax.rsqrt(jnp.sum(raw * raw, axis=1, keepdims=True) + epsilon)
        along = jnp.sum(raw * back_sum, axis=1, keepdims=True)
        gradient[crop] = scales * back_sum - scales * scales * scales * raw * along
        unit = (raw * scales).astype(BF16).astype(F32)
        cross = jnp.sum(unit * chosen, axis=1, keepdims=True) * (1.0 / student_softness)
        column = jnp.log(totals) - cross
        loss[crop : crop + 1, :] = jnp.broadcast_to(column, (images, LANES)).T[:1, :]


def finish_call(views, place, feats, picked, weights, back, parts):
    crops, images, width = feats.shape
    vmem = pl.BlockSpec(memory_space=pltpu.VMEM)
    return pl.pallas_call(
        functools.partial(finish_kernel, views, len(parts)),
        in_specs=[pl.BlockSpec(memory_space=pltpu.SMEM)] + [vmem] * (4 + len(parts)),
        out_specs=[vmem, vmem],
        out_shape=[
            jax.ShapeDtypeStruct((crops, images, width), F32),
            jax.ShapeDtypeStruct((crops, images), F32),
        ],
        scratch_shapes=[pltpu.VMEM((views * images, width), F32)],
        compiler_params=pltpu.CompilerParams(vmem_limit_bytes=VMEM_LIMIT),
        name="finish",
    )(place, feats, picked, weights, back, *parts)


def swap(values, axis, distance):
    count = lax.axis_size(axis)
    return lax.ppermute(values, axis, [(i, i ^ distance) for i in range(count)])


def shards(teacher_feats, student_feats, teacher_protos, student_protos, pairing, row_weight):
    images, views, width = teacher_feats.shape
    crops = student_feats.shape[0]
    image_devices = lax.axis_size("image")
    crop_devices = lax.axis_size("crop")
    proto_devices = lax.axis_size("proto")
    place = lax.axis_index("crop")
    both = ("crop", "proto")
    block = 512

    own_rows = (
        unit_rows(jnp.swapaxes(teacher_feats, 0, 1).astype(F32)).astype(BF16).reshape(views * images, width)
    )
    teacher_parts = [own_rows] + [swap(own_rows, "image", k) for k in range(1, image_devices)]
    feats = student_feats.reshape(crops * images, width)
    student_parts = [feats] + [swap(feats, "crop", k) for k in range(1, crop_devices)]

    unit_protos, partial_back = student_call(student_parts, student_protos, block)
    rows = crops * images
    back = partial_back[:rows]
    for k in range(1, crop_devices):
        back = back + swap(partial_back[k * rows : (k + 1) * rows], "crop", k)
    back = lax.psum(back, "proto")

    plan, sums = first_call(teacher_parts, teacher_protos, crop_devices * proto_devices, block)
    for _ in range(SWEEPS - 2):
        sums = sweep_call(lax.all_to_all(sums, both, 0, 0), plan, block)
    mixed = last_call(lax.all_to_all(sums, both, 0, 0), plan, unit_protos, views * images, block)

    share = views * images // crop_devices
    half = lax.dynamic_slice_in_dim(mixed, place * share, share, 0)
    for k in range(1, crop_devices):
        half = half + swap(lax.dynamic_slice_in_dim(mixed, (place ^ k) * share, share, 0), "crop", k)
    means = mean_call([half] + [swap(half, "proto", k) for k in range(1, proto_devices)], width)
    means = [means] + [swap(means, "crop", k) for k in range(1, crop_devices)]
    return finish_call(
        views, place.reshape(1), student_feats, pairing.T, row_weight.T.astype(F32), back, means
    )


def solution(mesh):
    in_specs = (
        P("image", None, None),
        P("crop", "image", None),
        P(None, ("crop", "proto")),
        P(None, ("crop", "proto")),
        P("crop", "image"),
        P("crop", "image"),
    )
    out_specs = (P("crop", "image", None), P("crop", "image"))
    return jax.shard_map(shards, mesh=mesh, in_specs=in_specs, out_specs=out_specs, check_vma=False)
```

time: 183 us -> 118 us (0.64)
  blocking collectives: 107 us -> 10.3 us
  waiting for transfers between devices: 34.8 us -> 56.4 us
  starting transfers between devices: 0.08 us -> 13.3 us
  Pallas kernels: 0 us -> 13.2 us
  matrix products: 11.4 us -> 0 us
  other arithmetic: 12 us -> 3.15 us
  local copies, waits for them, and re-layouts: 1.75 us -> 6.76 us
    psum x8 -> x0, blocking collectives: 98.9 us -> none  [the longest x3 45.1 us: row_step(): lax.psum(jnp.sum(transport_plan, axis=1), ('crop', 'proto'))[:, None]]
    ppermute x0 -> x10, waiting for transfers between devices: none -> 26.2 us  [swap(): return lax.ppermute(values, axis, [(i, i ^ distance) for i in range(count)])]
    pallas_call x0 -> x6, Pallas kernels: none -> 13.2 us  [the longest x1 3.87 us: student_call(): pl.pallas_call(student_kernel, grid=(columns // block,), in_specs=[pl.Blo...]
    dot_general x3 -> x0, matrix products: 11.4 us -> none  [the longest x1 5.26 us: shards(): jnp.einsum('lbk,dk->lbd', linear_factors, student_weight_matrix, preferre...]
    all_to_all x0 -> x1, blocking collectives: none -> 10.3 us  [shards(): sums = sweep_call(lax.all_to_all(sums, both, 0, 0), plan, block)]
    psum x1, waiting for transfers between devices: 34.8 us -> 24.6 us  [shards(): back = lax.psum(back, 'proto')]
    ppermute x0 -> x10, starting transfers between devices: none -> 9.9 us  [swap(): return lax.ppermute(values, axis, [(i, i ^ distance) for i in range(count)])]
    all_gather x3 -> x0, blocking collectives: 5.82 us -> none  [the longest x1 2.17 us: shards(): lax.all_gather(student_feats, 'crop', axis=0, tiled=True)]
  transfers between devices with their start and end apart: 2 -> 12, of which waited for: 1 -> 8; matrix products, arithmetic and copies ran while one was open for 1% -> 3% of each run, Pallas kernels for 0% -> 6%
where the time goes in v1:
time: 118 us; the launch traced here: 117 us
  waiting for transfers between devices  56.4 us (48%)
  between operations  14.2 us (12%)
  starting transfers between devices  13.3 us (11%)
  Pallas kernels  13.2 us (11%)
  blocking collectives  10.3 us (9%)
  local copies, waits for them, and re-layouts  6.76 us (6%)
  other arithmetic  3.15 us (3%)
    ppermute x10, waiting for transfers between devices, swap(): return lax.ppermute(values, axis, [(i, i ^ distance) for i in range(count)])  26.2 us
    psum x1, waiting for transfers between devices, shards(): back = lax.psum(back, 'proto')  24.6 us
    all_to_all x1, blocking collectives, shards(): sums = sweep_call(lax.all_to_all(sums, both, 0, 0), plan, block)  10.3 us
    ppermute x10, starting transfers between devices, swap(): return lax.ppermute(values, axis, [(i, i ^ distance) for i in range(count)])  9.9 us
    unnamed x27, local copies, waits for them, and re-layouts  5.95 us
    all_to_all x1, waiting for transfers between devices, shards(): lax.all_to_all(sums, both, 0, 0)  5.53 us
    pallas_call x1, Pallas kernels, student_call(): pl.pallas_call(student_kernel, grid=(columns // block,), in_specs=[pl.Blo...  3.87 us
    pallas_call x1, Pallas kernels, first_call(): pl.pallas_call(first_kernel, grid=(columns // block,), in_specs=[pl.Block...  3.86 us
  transfers between devices with their start and end apart: 12, of which 8 were waited for; matrix products, arithmetic and copies ran while one was open for 3% of the time, Pallas kernels for 6%

profile of v1, /device:TPU:0, one launch (start us, length us, event | category | flops | bytes accessed | tf_op | source)
XLA Modules:
  0.0 117.3 jit_solution(8738890396130184515)
XLA Ops:
  7.2 0.5 collective-permute-start
  7.7 1.0 fusion
  8.7 0.4 collective-permute-done.refs_1_
  9.1 0.9 copy-done.5
  10.0 1.6 %copy-done.7 = bf16[512,2048]{1,0:T(8,128)(2,1)S(1)} copy-done((bf16[512,2048]{1,0:T(8,128)(2,1)S(1)}, bf16[512,2048]{1,0:T(8,128)(2,1)}, u32[]{:S(2)}) %copy-start.7) | copy-done | bytes 2097176
  11.6 3.9 %student.1 = (bf16[512,2048]{1,0:T(8,128)(2,1)S(1)}, f32[512,640]{1,0:T(8,128)S(1)}) custom-call(bf16[256,512]{1,0:T(8,128)(2,1)S(1)} %bitcast.21, bf16[256,512]{1,0:T(8,128)(2,1)S(1)} %collective-permute-done.refs_1_, bf16[512,2048]{1,0:T(8,128)(2,1)S(1)} %copy-done.7), custom_call_target="tpu_custom_call" | custom-call | flops 2147483648 | bytes 4194304 | tf_op jit(solution)/shard_map/student/pallas_call | solution.py:69
  15.5 0.4 collective-permute-start.1
  16.1 2.7 %collective-permute-start.2 = (bf16[128,512]{1,0:T(8,128)(2,1)S(1)}, bf16[128,512]{1,0:T(8,128)(2,1)S(1)}, u32[]{:S(2)}, u32[]{:S(2)}) collective-permute-start(bf16[128,512]{1,0:T(8,128)(2,1)S(1)} %bitcast.24), channel_id=1, source_target_pairs={{0,8},{8,0},{16,24},{24,16},{1,9},{9,1},{17,25},{25,17},{2,10},{10... | collective-permute-start | bytes 393224 | tf_op jit(solution)/shard_map/ppermute | solution.py:301
  18.8 1.5 %collective-permute-start.3 = (bf16[128,512]{1,0:T(8,128)(2,1)S(1)}, bf16[128,512]{1,0:T(8,128)(2,1)S(1)}, u32[]{:S(2)}, u32[]{:S(2)}) collective-permute-start(bf16[128,512]{1,0:T(8,128)(2,1)S(1)} %bitcast.25), channel_id=1, source_target_pairs={{0,16},{8,24},{16,0},{24,8},{1,17},{9,25},{17,1},{25,9},{2,18},{10... | collective-permute-start | bytes 393224 | tf_op jit(solution)/shard_map/ppermute | solution.py:301
  20.3 2.6 %collective-permute-done.2.refs_1_ = bf16[128,512]{1,0:T(8,128)(2,1)S(1)} collective-permute-done((bf16[128,512]{1,0:T(8,128)(2,1)S(1)}, bf16[128,512]{1,0:T(8,128)(2,1)S(1)}, u32[]{:S(2)}, u32[]{:S(2)}) %collective-permute-start.2) | collective-permute-done | bytes 131104 | tf_op jit(solution)/shard_map/ppermute | solution.py:301
  22.9 4.2 %collective-permute-done.3.refs_2_ = bf16[128,512]{1,0:T(8,128)(2,1)S(1)} collective-permute-done((bf16[128,512]{1,0:T(8,128)(2,1)S(1)}, bf16[128,512]{1,0:T(8,128)(2,1)S(1)}, u32[]{:S(2)}, u32[]{:S(2)}) %collective-permute-start.3) | collective-permute-done | bytes 131104 | tf_op jit(solution)/shard_map/ppermute | solution.py:301
  27.1 3.9 %first_sweep.1 = (f32[512,2048]{1,0:T(8,128)S(1)}, f32[8,512]{1,0:T(8,128)S(1)}) custom-call(bf16[128,512]{1,0:T(8,128)(2,1)S(1)} %bitcast.27, bf16[128,512]{1,0:T(8,128)(2,1)S(1)} %collective-permute-done.2.refs_1_, bf16[128,512]{1,0:T(8,128)(2,1)S(1)} %collective-permute-done.3.refs_2_, bf16[128,512]{1,0:T(8,128)(2,1)S(1)} %collective-permute-done.4.refs_3_, ...), custom_call_target="tpu_custom_call" | custom-call | flops 1073741824 | bytes 6291456 | tf_op jit(solution)/shard_map/first_sweep/pallas_call | solution.py:121
  31.0 10.3 %all_to_all.22 = f32[8,1,512]{2,1,0:T(1,128)S(1)} all-to-all(f32[8,1,512]{2,1,0:T(1,128)S(1)} %copy.19), channel_id=1, replica_groups=mesh['image'=4,'crop'=2,'proto'=4] {'crop','proto'}, dimensions={0} | all-to-all | bytes 32768 | tf_op jit(solution)/shard_map/all_to_all | solution.py:330
  41.3 1.5 %sweep.1 = f32[8,512]{1,0:T(8,128)S(1)} custom-call(f32[8,512]{1,0:T(8,128)S(1)} %bitcast.29, f32[512,2048]{1,0:T(8,128)S(1)} %get-tuple-element.8.plan), custom_call_target="tpu_custom_call" | custom-call | flops 4194304 | bytes 4194304 | tf_op jit(solution)/shard_map/sweep/pallas_call | solution.py:176
  42.9 0.6 copy.20
  43.5 3.3 %all-to-all-start.1 = ((f32[8,1,512]{2,1,0:T(1,128)}), f32[8,1,512]{2,1,0:T(1,128)S(1)}, u32[]{:S(2)}, u32[]{:S(2)}) async-start(f32[8,1,512]{2,1,0:T(1,128)} %copy.20), calls=%async_computation.1 | async-start | bytes 32768 | tf_op jit(solution)/shard_map/all_to_all | solution.py:331
  46.9 5.5 %all-to-all-done.1 = f32[8,1,512]{2,1,0:T(1,128)S(1)} async-done(((f32[8,1,512]{2,1,0:T(1,128)}), f32[8,1,512]{2,1,0:T(1,128)S(1)}, u32[]{:S(2)}, u32[]{:S(2)}) %all-to-all-start.1) | async-done | bytes 16416 | tf_op jit(solution)/shard_map/all_to_all | solution.py:331
  52.4 2.2 %copy-done.1 = f32[512,2048]{1,0:T(8,128)S(1)} copy-done((f32[512,2048]{1,0:T(8,128)S(1)}, f32[512,2048]{1,0:T(8,128)}, u32[]{:S(2)}) %copy-start.1) | copy-done | bytes 4194328
  54.6 2.1 %last_sweep.1 = f32[128,640]{1,0:T(8,128)S(1)} custom-call(f32[8,512]{1,0:T(8,128)S(1)} %bitcast.28, f32[512,2048]{1,0:T(8,128)S(1)} %copy-done.1, bf16[512,2048]{1,0:T(8,128)(2,1)S(1)} %get-tuple-element.9.unit_protos), custom_call_target="tpu_custom_call" | custom-call | flops 268435456 | bytes 6291456 | tf_op jit(solution)/shard_map/last_sweep/pallas_call | solution.py:216
  56.8 0.2 collective-permute-start.5
  57.0 2.0 %slice_add_fusion = f32[256,640]{1,0:T(8,128)} fusion(f32[256,640]{1,0:T(8,128)} %collective-permute-done.1, f32[512,640]{1,0:T(8,128)S(1)} %copy-done.3), kind=kLoop, calls=%fused_computation | loop fusion | flops 163840 | bytes 1966080 | tf_op jit(solution)/shard_map/add | solution.py:325
  59.1 0.6 collective-permute-start.6
  59.7 0.5 collective-permute-start.7
  60.2 3.3 %collective-permute-start.8 = (f32[64,640]{1,0:T(8,128)S(1)}, f32[64,640]{1,0:T(8,128)S(1)}, u32[]{:S(2)}, u32[]{:S(2)}) collective-permute-start(f32[64,640]{1,0:T(8,128)S(1)} %dynamic-slice_add_fusion.refs_0_), channel_id=1, source_target_pairs={{0,3},{1,2},{2,1},{3,0},{4,7},{5,6},{6,5},{7,4},{8,11},{9,10},{10,... | collective-permute-start | bytes 491528 | tf_op jit(solution)/shard_map/ppermute | solution.py:301
  63.5 8.6 %collective-permute-done.6.refs_1_ = f32[64,640]{1,0:T(8,128)S(1)} collective-permute-done((f32[64,640]{1,0:T(8,128)S(1)}, f32[64,640]{1,0:T(8,128)S(1)}, u32[]{:S(2)}, u32[]{:S(2)}) %collective-permute-start.6) | collective-permute-done | bytes 163872 | tf_op jit(solution)/shard_map/ppermute | solution.py:301
  72.1 9.4 %collective-permute-done.7.refs_2_ = f32[64,640]{1,0:T(8,128)S(1)} collective-permute-done((f32[64,640]{1,0:T(8,128)S(1)}, f32[64,640]{1,0:T(8,128)S(1)}, u32[]{:S(2)}, u32[]{:S(2)}) %collective-permute-start.7) | collective-permute-done | bytes 163872 | tf_op jit(solution)/shard_map/ppermute | solution.py:301
  81.7 0.1 copy.16
  81.8 0.1 copy.17
  81.9 1.1 collective-permute-done.9.refs_1_
  83.0 24.6 %all-reduce.2.cloned.1.call-done.back = f32[256,640]{1,0:T(8,128)} async-done(((f32[256,640]{1,0:T(8,128)}), f32[256,640]{1,0:T(8,128)}) %all-reduce.2.cloned.1.call-update) | async-done | bytes 655376 | tf_op jit(solution)/shard_map/psum | solution.py:326
  107.7 1.1 copy-done.4
  108.7 1.7 %finish.1 = (f32[4,64,512]{2,1,0:T(8,128)}, f32[4,64]{1,0:T(4,128)}) custom-call(s32[1]{0:T(128)} %bitcast.place, bf16[4,64,512]{2,1,0:T(8,128)(2,1)S(1)} %copy-done.6, s32[64,4]{1,0:T(8,128)S(1)} %bitcast.22, f32[64,4]{1,0:T(8,128)S(1)} %bitcast.23, f32[256,640]{1,0:T(8,128)S(1)} %copy-done.4, f32[64,512]{1,0:T(8,128)S(1)} %mean_protos.1.refs_0_, ...), custom_call_target="tpu_custom_call" | custom-call | tf_op jit(solution)/shard_map/finish/pallas_call | solution.py:285
  (37 shorter events, 0.5 us)
Async XLA Ops:
  7.2 1.9 %collective-permute-start = (bf16[256,512]{1,0:T(8,128)(2,1)}, bf16[256,512]{1,0:T(8,128)(2,1)S(1)}, u32[]{:S(2)}, u32[]{:S(2)}) collective-permute-start(bf16[256,512]{1,0:T(8,128)(2,1)} %bitcast.20), channel_id=1, source_target_pairs={{0,4},{4,0},{1,5},{5,1},{2,6},{6,2},{3,7},{7,3},{8,12},{12,8},{9,1... | collective-permute-start | bytes 786440 | tf_op jit(solution)/shard_map/ppermute | solution.py:301
  9.1 0.9 copy-start.5
  10.0 1.6 %copy-start.7 = (bf16[512,2048]{1,0:T(8,128)(2,1)S(1)}, bf16[512,2048]{1,0:T(8,128)(2,1)}, u32[]{:S(2)}) copy-start(bf16[512,2048]{1,0:T(8,128)(2,1)} %refs_2_.1) | copy-start | bytes 6291460
  11.6 4.4 %copy-start.9 = (bf16[64,2,512]{2,1,0:T(2,128)(2,1)S(1)}, bf16[64,2,512]{2,1,0:T(2,128)(2,1)}, u32[]{:S(2)}) copy-start(bf16[64,2,512]{2,1,0:T(2,128)(2,1)} %param.6) | copy-start | bytes 393220
  11.6 15.5 %copy-start.8 = (bf16[512,2048]{1,0:T(8,128)(2,1)S(1)}, bf16[512,2048]{1,0:T(8,128)(2,1)}, u32[]{:S(2)}) copy-start(bf16[512,2048]{1,0:T(8,128)(2,1)} %refs_4_.1) | copy-start | bytes 6291460
  15.5 15.5 %copy-start.2 = (f32[512,640]{1,0:T(8,128)}, f32[512,640]{1,0:T(8,128)S(1)}, u32[]{:S(2)}) copy-start(f32[512,640]{1,0:T(8,128)S(1)} %get-tuple-element.6) | copy-start | bytes 3932164
  15.5 41.4 %collective-permute-start.1 = (f32[256,640]{1,0:T(8,128)S(1)}, f32[256,640]{1,0:T(8,128)}, u32[]{:S(2)}, u32[]{:S(2)}) collective-permute-start(f32[256,640]{1,0:T(8,128)S(1)} %slice.7), channel_id=1, source_target_pairs={{0,4},{4,0},{1,5},{5,1},{2,6},{6,2},{3,7},{7,3},{8,12},{12,8},{9,1... | collective-permute-start | bytes 1966088 | tf_op jit(solution)/shard_map/ppermute | solution.py:301
  16.1 6.8 %collective-permute-start.2 = (bf16[128,512]{1,0:T(8,128)(2,1)S(1)}, bf16[128,512]{1,0:T(8,128)(2,1)S(1)}, u32[]{:S(2)}, u32[]{:S(2)}) collective-permute-start(bf16[128,512]{1,0:T(8,128)(2,1)S(1)} %bitcast.24), channel_id=1, source_target_pairs={{0,8},{8,0},{16,24},{24,16},{1,9},{9,1},{17,25},{25,17},{2,10},{10... | collective-permute-start | bytes 393224 | tf_op jit(solution)/shard_map/ppermute | solution.py:301
  18.8 8.3 %collective-permute-start.3 = (bf16[128,512]{1,0:T(8,128)(2,1)S(1)}, bf16[128,512]{1,0:T(8,128)(2,1)S(1)}, u32[]{:S(2)}, u32[]{:S(2)}) collective-permute-start(bf16[128,512]{1,0:T(8,128)(2,1)S(1)} %bitcast.25), channel_id=1, source_target_pairs={{0,16},{8,24},{16,0},{24,8},{1,17},{9,25},{17,1},{25,9},{2,18},{10... | collective-permute-start | bytes 393224 | tf_op jit(solution)/shard_map/ppermute | solution.py:301
  20.3 6.8 %collective-permute-start.4 = (bf16[128,512]{1,0:T(8,128)(2,1)S(1)}, bf16[128,512]{1,0:T(8,128)(2,1)S(1)}, u32[]{:S(2)}, u32[]{:S(2)}) collective-permute-start(bf16[128,512]{1,0:T(8,128)(2,1)S(1)} %bitcast.26), channel_id=1, source_target_pairs={{0,24},{8,16},{16,8},{24,0},{1,25},{9,17},{17,9},{25,1},{2,26},{10... | collective-permute-start | bytes 393224 | tf_op jit(solution)/shard_map/ppermute | solution.py:301
  30.9 11.9 %copy-start = (f32[512,2048]{1,0:T(8,128)}, f32[512,2048]{1,0:T(8,128)S(1)}, u32[]{:S(2)}) copy-start(f32[512,2048]{1,0:T(8,128)S(1)} %get-tuple-element.8.plan) | copy-start | bytes 12582916
  43.5 8.9 %all-to-all-start.1 = ((f32[8,1,512]{2,1,0:T(1,128)}), f32[8,1,512]{2,1,0:T(1,128)S(1)}, u32[]{:S(2)}, u32[]{:S(2)}) async-start(f32[8,1,512]{2,1,0:T(1,128)} %copy.20), calls=%async_computation.1 | async-start | bytes 32768 | tf_op jit(solution)/shard_map/all_to_all | solution.py:331
  46.8 60.8 %all-reduce.2.cloned.1.call-start = ((), (), s32[]{:S(2)}) async-start(), calls=%async_computation.2 | async-start | bytes 1310720 | tf_op jit(solution)/shard_map/psum | solution.py:326
  52.4 2.2 %copy-start.1 = (f32[512,2048]{1,0:T(8,128)S(1)}, f32[512,2048]{1,0:T(8,128)}, u32[]{:S(2)}) copy-start(f32[512,2048]{1,0:T(8,128)} %copy-done) | copy-start | bytes 12582916
  54.6 2.4 %copy-start.3 = (f32[512,640]{1,0:T(8,128)S(1)}, f32[512,640]{1,0:T(8,128)}, u32[]{:S(2)}) copy-start(f32[512,640]{1,0:T(8,128)} %copy-done.2) | copy-start | bytes 3932164
  56.7 24.9 %copy-start.10 = (s32[4,64]{1,0:T(4,128)S(1)}, s32[4,64]{1,0:T(4,128)}, u32[]{:S(2)}) copy-start(s32[4,64]{1,0:T(4,128)} %param.10) | copy-start | bytes 3076
  56.8 25.0 %copy-start.11 = (bf16[4,64]{1,0:T(4,128)(2,1)S(1)}, bf16[4,64]{1,0:T(4,128)(2,1)}, u32[]{:S(2)}) copy-start(bf16[4,64]{1,0:T(4,128)(2,1)} %param.11) | copy-start | bytes 1540
  56.8 50.9 %copy-start.6 = (bf16[4,64,512]{2,1,0:T(8,128)(2,1)S(1)}, bf16[4,64,512]{2,1,0:T(8,128)(2,1)}, u32[]{:S(2)}) copy-start(bf16[4,64,512]{2,1,0:T(8,128)(2,1)} %feats.1) | copy-start | bytes 786436
  56.8 2.2 %collective-permute-start.5 = (f32[64,640]{1,0:T(8,128)S(1)}, f32[64,640]{1,0:T(8,128)S(1)}, u32[]{:S(2)}, u32[]{:S(2)}) collective-permute-start(f32[64,640]{1,0:T(8,128)S(1)} %constant_dynamic-slice_fusion), channel_id=1, source_target_pairs={{0,4},{4,0},{1,5},{5,1},{2,6},{6,2},{3,7},{7,3},{8,12},{12,8},{9,1... | collective-permute-start | bytes 491528 | tf_op jit(solution)/shard_map/ppermute | solution.py:301
  59.1 13.0 %collective-permute-start.6 = (f32[64,640]{1,0:T(8,128)S(1)}, f32[64,640]{1,0:T(8,128)S(1)}, u32[]{:S(2)}, u32[]{:S(2)}) collective-permute-start(f32[64,640]{1,0:T(8,128)S(1)} %dynamic-slice_add_fusion.refs_0_), channel_id=1, source_target_pairs={{0,1},{1,0},{2,3},{3,2},{4,5},{5,4},{6,7},{7,6},{8,9},{9,8},{10,11... | collective-permute-start | bytes 491528 | tf_op jit(solution)/shard_map/ppermute | solution.py:301
  59.7 21.8 %collective-permute-start.7 = (f32[64,640]{1,0:T(8,128)S(1)}, f32[64,640]{1,0:T(8,128)S(1)}, u32[]{:S(2)}, u32[]{:S(2)}) collective-permute-start(f32[64,640]{1,0:T(8,128)S(1)} %dynamic-slice_add_fusion.refs_0_), channel_id=1, source_target_pairs={{0,2},{1,3},{2,0},{3,1},{4,6},{5,7},{6,4},{7,5},{8,10},{9,11},{10,... | collective-permute-start | bytes 491528 | tf_op jit(solution)/shard_map/ppermute | solution.py:301
  60.2 21.3 %collective-permute-start.8 = (f32[64,640]{1,0:T(8,128)S(1)}, f32[64,640]{1,0:T(8,128)S(1)}, u32[]{:S(2)}, u32[]{:S(2)}) collective-permute-start(f32[64,640]{1,0:T(8,128)S(1)} %dynamic-slice_add_fusion.refs_0_), channel_id=1, source_target_pairs={{0,3},{1,2},{2,1},{3,0},{4,7},{5,6},{6,5},{7,4},{8,11},{9,10},{10,... | collective-permute-start | bytes 491528 | tf_op jit(solution)/shard_map/ppermute | solution.py:301
  81.6 1.4 %collective-permute-start.9 = (f32[64,512]{1,0:T(8,128)S(1)}, f32[64,512]{1,0:T(8,128)S(1)}, u32[]{:S(2)}, u32[]{:S(2)}) collective-permute-start(f32[64,512]{1,0:T(8,128)S(1)} %mean_protos.1.refs_0_), channel_id=1, source_target_pairs={{0,4},{4,0},{1,5},{5,1},{2,6},{6,2},{3,7},{7,3},{8,12},{12,8},{9,1... | collective-permute-start | bytes 393224 | tf_op jit(solution)/shard_map/ppermute | solution.py:301
  107.7 1.1 copy-start.4
Sparse Core Ops, SparseCore 0:
  59.2 48.4 all-reduce.1

commit v2 on v0

v2 whole, which is shorter than its diff:
```python
import functools

import jax
import jax.numpy as jnp
from jax import lax
from jax.experimental import pallas as pl
from jax.experimental.pallas import tpu as pltpu
from jax.sharding import PartitionSpec as P

SWEEPS = 3
LANES = 128
ROW_TILE = 16
LEVELS = 32767.0
PARTS = 32768.0

epsilon = 1e-06
student_softness = 0.1
teacher_softness = 0.04

F32 = jnp.float32
BF16 = jnp.bfloat16
I16 = jnp.int16

IN_VMEM = pl.BlockSpec(memory_space=pltpu.VMEM)
IN_SMEM = pl.BlockSpec(memory_space=pltpu.SMEM)


def call(kernel, name, out_shape, scratch=(), scalars=0, vmem=16, after=(), flops=10**9, aliases=None):
    def run(*operands):
        count = len(operands)

        def body(*refs):
            kernel(*refs[:count], *refs[count + len(after) :])

        return pl.pallas_call(
            body,
            in_specs=[IN_SMEM] * scalars
            + [IN_VMEM] * (count - scalars)
            + [pl.BlockSpec(memory_space=pl.ANY)] * len(after),
            out_specs=jax.tree.map(lambda _: IN_VMEM, out_shape),
            out_shape=out_shape,
            scratch_shapes=list(scratch),
            compiler_params=pltpu.CompilerParams(vmem_limit_bytes=vmem * 1024 * 1024),
            cost_estimate=pl.CostEstimate(flops=flops, bytes_accessed=0, transcendentals=0),
            input_output_aliases=aliases or {},
            name=name,
        )(*operands, *after)

    return run


def shape(dims, dtype=F32):
    return jax.ShapeDtypeStruct(dims, dtype)


def unit_rows(raw_rows):
    return raw_rows * lax.rsqrt(jnp.sum(raw_rows * raw_rows, axis=-1, keepdims=True) + epsilon)


def unit_columns(entries):
    return entries * lax.rsqrt(jnp.sum(entries * entries, axis=0, keepdims=True) + epsilon)


def lane_groups(values):
    total = values[:, :LANES]
    for start in range(LANES, values.shape[1], LANES):
        total = total + values[:, start : start + LANES]
    return total


def dot_t(a, b):
    return lax.dot_general(a, b, (((1,), (1,)), ((), ())), preferred_element_type=F32)


def row_vector(partial):
    return jnp.sum(partial.T, axis=0, keepdims=True)


def tree_sum(terms):
    while len(terms) > 1:
        terms = [terms[i] + terms[i + 1] for i in range(0, len(terms), 2)]
    return terms[0]


def encode(values, extra):
    rows = values.shape[0]
    largest = jnp.maximum(jnp.max(jnp.abs(values), axis=1, keepdims=True), 1e-30)
    power = jnp.floor(jnp.log2(largest)) + 1.0
    whole = jnp.floor(values * (jnp.exp2(-power) * LEVELS) + 0.5)
    coded = jnp.clip(whole, -LEVELS, LEVELS).astype(jnp.int32).astype(I16)
    extra_power = jnp.floor(jnp.log2(jnp.maximum(extra, 1e-30))) + 1.0
    scaled = extra * jnp.exp2(-extra_power) * PARTS
    high = jnp.minimum(jnp.floor(scaled), LEVELS)
    low = jnp.minimum(jnp.floor((scaled - high) * PARTS), LEVELS)
    lane = lax.broadcasted_iota(jnp.int32, (rows, LANES), 1)
    tail = jnp.where(lane == 0, power, jnp.where(lane == 1, extra_power, jnp.where(lane == 2, high, low)))
    return coded, tail.astype(jnp.int32).astype(I16)


def store_code(out, values, extra):
    width = values.shape[1]
    out[:, :width], out[:, width:] = encode(values, extra)


def decode(ref):
    width = ref.shape[1] - LANES
    tail = ref[:, width:].astype(jnp.int32).astype(F32)
    values = ref[:, :width].astype(jnp.int32).astype(F32) * (jnp.exp2(tail[:, 0:1]) * (1.0 / LEVELS))
    extra = (tail[:, 2:3] + tail[:, 3:4] * (1.0 / PARTS)) * (1.0 / PARTS) * jnp.exp2(tail[:, 1:2])
    return values, extra


def decode_sum(refs):
    pairs = [decode(ref) for ref in refs]
    return tree_sum([p[0] for p in pairs]), tree_sum([p[1] for p in pairs])


def swap(values, axis, distance):
    count = lax.axis_size(axis)
    return lax.ppermute(values, axis, [(i, i ^ distance) for i in range(count)])


def student_kernel(count, block, place, feats, teacher_protos, *refs):
    protos, refs = refs[:count], refs[count:]
    unit_protos, unit_teacher = refs[:2]
    outs, (unit_feats, back) = refs[2:-2], refs[-2:]
    width, columns = unit_protos.shape
    unit_feats[...] = unit_rows(feats[...].astype(F32)).astype(BF16)
    for start in range(0, columns, block):
        here = slice(start, start + block)
        unit_teacher[:, here] = unit_columns(teacher_protos[:, here].astype(F32)).astype(BF16)
        for k, part in enumerate(protos):
            weights = unit_columns(part[:, here].astype(F32)).astype(BF16)
            if k == 0:
                unit_protos[:, here] = weights
            logits = jnp.dot(unit_feats[...], weights, preferred_element_type=F32)
            terms = jnp.exp(logits * (1.0 / student_softness))
            sums = lane_groups(terms)
            sides = dot_t(terms.astype(BF16), weights)
            if start == 0 and k == 0:
                back[:, width:] = sums
                back[:, :width] = sides
            else:
                back[:, width:] += sums
                back[:, :width] += sides
    share = outs[0].shape[0]
    for k, out in enumerate(outs):
        first = pl.multiple_of(jnp.bitwise_xor(place[0], k) * share, share)
        total = back[pl.ds(first, share), :]
        store_code(out, total[:, :width], lane_sums(total[:, width:]))


def student_call(place, feats, teacher_protos, protos, pieces, block):
    width, columns = teacher_protos.shape
    rows = feats.shape[0]
    out = call(
        functools.partial(student_kernel, len(protos), block),
        "student",
        [shape((width, columns), BF16)] * 2 + [shape((rows // pieces, width + LANES), I16)] * pieces,
        [pltpu.VMEM((rows, width), BF16), pltpu.VMEM((rows, width + LANES), F32)],
        scalars=1,
        vmem=48 if len(protos) > 2 else 16,
        flops=8 * rows * len(protos) * columns * width,
    )(place, feats, teacher_protos, *protos)
    return out[0], out[1], out[2:]


def first_kernel(count, block, *refs):
    parts, (weights, plan, sums, partial) = refs[:count], refs[count:]
    columns = weights.shape[1]
    for start in range(0, columns, block):
        here = slice(start, start + block)
        column_sums = None
        first = 0
        for part in parts:
            rows = part.shape[0]
            values = jnp.exp(
                jnp.dot(part[...], weights[:, here], preferred_element_type=F32) * (1.0 / teacher_softness)
            )
            plan[first : first + rows, here] = values
            total = jnp.sum(values, axis=0, keepdims=True)
            column_sums = total if column_sums is None else column_sums + total
            first += rows
        terms = lane_groups(plan[:, here] * (1.0 / column_sums))
        if start == 0:
            partial[...] = terms
        else:
            partial[...] += terms
    store_sums(sums, partial)


def store_sums(sums, partial):
    total = row_vector(partial[...])
    for k in range(sums.shape[0]):
        sums[k] = total


def first_call(parts, weights, copies, block, after=()):
    columns = weights.shape[1]
    rows = sum(part.shape[0] for part in parts)
    return call(
        functools.partial(first_kernel, len(parts), block),
        "first_sweep",
        [shape((rows, columns)), shape((copies, 1, rows))],
        [pltpu.VMEM((rows, LANES), F32)],
        after=after,
        flops=8 * rows * columns * weights.shape[0],
    )(*parts, weights)


def scale_rows(row_sums, row_scale):
    total = row_sums[0]
    for k in range(1, row_sums.shape[0]):
        total = total + row_sums[k]
    scale = 1.0 / total
    row_scale[...] = jnp.broadcast_to(scale, (LANES, scale.shape[1])).T


def column_scale(plan, row_scale, start):
    weighted = plan[:, start : start + LANES] * row_scale[...]
    return 1.0 / jnp.sum(weighted, axis=0, keepdims=True)


def sweep_kernel(row_sums, plan, *refs):
    shares, (sums, share, _, row_scale, partial) = refs[:-5], refs[-5:]
    back, totals = decode_sum(shares)
    store_code(share, back / totals, totals)
    scale_rows(row_sums, row_scale)
    for start in range(0, plan.shape[1], LANES):
        terms = plan[:, start : start + LANES] * column_scale(plan, row_scale, start)
        if start == 0:
            partial[...] = terms
        else:
            partial[...] += terms
    store_sums(sums, partial)


def sweep_call(row_sums, plan, shares):
    rows = plan.shape[0]
    return call(
        sweep_kernel,
        "sweep",
        [shape(row_sums.shape), shape(shares[0].shape, I16), shape(plan.shape)],
        [pltpu.VMEM((rows, LANES), F32)] * 2,
        aliases={1: 2},
    )(row_sums, plan, *shares)


def last_kernel(share, block, place, row_sums, plan, unit_protos, *refs):
    outs, (row_scale, scaled, mixed) = refs[:-3], refs[-3:]
    own = scaled.shape[0]
    width, columns = unit_protos.shape
    scale_rows(row_sums, row_scale)
    for start in range(0, columns, block):
        here = slice(start, start + block)
        total = None
        for group in range(start, start + block, LANES):
            terms = plan[:own, group : group + LANES] * column_scale(plan, row_scale, group)
            total = terms if total is None else total + terms
            scaled[:, group - start : group - start + LANES] = terms.astype(BF16)
        sides = dot_t(scaled[...], unit_protos[:, here])
        if start == 0:
            mixed[:, width:] = total
            mixed[:, :width] = sides
        else:
            mixed[:, width:] += total
            mixed[:, :width] += sides
    for k, out in enumerate(outs):
        first = pl.multiple_of(jnp.bitwise_xor(place[0], k) * share, share)
        out[...] = mixed[pl.ds(first, share), :]


def last_call(place, row_sums, plan, unit_protos, own, count, block, after=()):
    rows = plan.shape[0]
    width = unit_protos.shape[0]
    share = own // count
    return call(
        functools.partial(last_kernel, share, block),
        "last_sweep",
        [shape((share, width + LANES))] * count,
        [
            pltpu.VMEM((rows, LANES), F32),
            pltpu.VMEM((own, block), BF16),
            pltpu.VMEM((own, width + LANES), F32),
        ],
        scalars=1,
        after=after,
    )(place, row_sums, plan, unit_protos)


def lane_sums(values):
    return jnp.sum(values, axis=1, keepdims=True)


def code_kernel(*refs):
    parts, out = refs[:-1], refs[-1]
    width = out.shape[1] - LANES
    total = tree_sum([part[...] for part in parts])
    store_code(out, total[:, :width], lane_sums(total[:, width:]))


def code_call(parts, after=()):
    return call(code_kernel, "code_mixed", shape(parts[0].shape, I16), after=after)(*parts)


def mean_kernel(*refs):
    parts, out = refs[:-1], refs[-1]
    mixed, totals = decode_sum(parts)
    out[...] = mixed / totals


def mean_call(parts):
    rows, columns = parts[0].shape
    return call(mean_kernel, "mean_protos", shape((rows, columns - LANES)))(*parts)


def finish_kernel(views, mean_count, crop_place, proto_place, feats, picked, weights, *refs):
    parts, refs = refs[:mean_count], refs[mean_count:]
    shares, (gradient, loss, means, expected, totals) = refs[:-5], refs[-5:]
    rows = parts[0].shape[0]
    for k, part in enumerate(parts):
        first = pl.multiple_of(jnp.bitwise_xor(crop_place[0], k) * rows, rows)
        means[pl.ds(first, rows), :] = part[...]
    rows = shares[0].shape[0]
    for k, part in enumerate(shares):
        first = pl.multiple_of(jnp.bitwise_xor(proto_place[0], k) * rows, rows)
        values, extra = decode(part)
        expected[pl.ds(first, rows), :] = values
        totals[pl.ds(first, rows), :] = jnp.broadcast_to(extra, (rows, LANES))
    images = feats.shape[1]
    for crop in range(feats.shape[0]):
        raw = feats[crop].astype(F32)
        chosen = means[:images, :]
        for view in range(1, views):
            chosen = jnp.where(
                picked[:, crop : crop + 1] == view, means[view * images : (view + 1) * images, :], chosen
            )
        here = slice(crop * images, (crop + 1) * images)
        factor = weights[:, crop : crop + 1] * (1.0 / student_softness)
        back_sum = factor * (expected[here, :] - chosen)
        scales = lax.rsqrt(lane_sums(raw * raw) + epsilon)
        along = lane_sums(raw * back_sum)
        gradient[crop] = scales * back_sum - scales * scales * scales * raw * along
        unit = (raw * scales).astype(BF16).astype(F32)
        cross = lane_sums(unit * chosen) * (1.0 / student_softness)
        column = jnp.log(totals[here, 0:1]) - cross
        loss[crop : crop + 1, :] = jnp.broadcast_to(column, (images, LANES)).T[:1, :]


def finish_call(views, crop_place, proto_place, feats, picked, weights, means, shares):
    crops, images, width = feats.shape
    return call(
        functools.partial(finish_kernel, views, len(means)),
        "finish",
        [shape((crops, images, width)), shape((crops, images))],
        [
            pltpu.VMEM((views * images, width), F32),
            pltpu.VMEM((crops * images, width), F32),
            pltpu.VMEM((crops * images, LANES), F32),
        ],
        scalars=2,
    )(crop_place, proto_place, feats, picked, weights, *means, *shares)


def shards(teacher_feats, student_feats, teacher_protos, student_protos, pairing, row_weight):
    images, views, width = teacher_feats.shape
    crops = student_feats.shape[0]
    image_devices = lax.axis_size("image")
    crop_devices = lax.axis_size("crop")
    proto_devices = lax.axis_size("proto")
    crop_place = lax.axis_index("crop").reshape(1)
    proto_place = lax.axis_index("proto").reshape(1)
    both = ("crop", "proto")
    block = 512

    own_rows = (
        unit_rows(jnp.swapaxes(teacher_feats, 0, 1).astype(F32)).astype(BF16).reshape(views * images, width)
    )
    teacher_parts = [own_rows] + [swap(own_rows, "image", k) for k in range(1, image_devices)]
    feats = student_feats.reshape(crops * images, width)
    protos = [student_protos] + [swap(student_protos, "crop", k) for k in range(1, crop_devices)]

    pieces = proto_devices
    if crops * images % (pieces * ROW_TILE):
        pieces, proto_place = 1, jnp.zeros((1,), jnp.int32)
    unit_protos, unit_teacher, coded = student_call(
        proto_place, feats, teacher_protos, protos, pieces, block
    )
    plan, sums = first_call(teacher_parts, unit_teacher, crop_devices * proto_devices, block)
    shares = [coded[0]] + [swap(coded[k % pieces], "proto", k) for k in range(1, proto_devices)]
    for _ in range(SWEEPS - 2):
        sums, share, plan = sweep_call(lax.all_to_all(sums, both, 0, 0), plan, shares)
    shares = [share] + [swap(share, "proto", k) for k in range(1, pieces)]
    sums = lax.all_to_all(sums, both, 0, 0)
    mixed = last_call(
        crop_place, sums, plan, unit_protos, views * images, crop_devices, block, after=shares[1:]
    )

    mixed = code_call([mixed[0]] + [swap(mixed[k], "crop", k) for k in range(1, crop_devices)])
    means = mean_call([mixed] + [swap(mixed, "proto", k) for k in range(1, proto_devices)])
    means = [means] + [swap(means, "crop", k) for k in range(1, crop_devices)]
    return finish_call(
        views, crop_place, proto_place, student_feats, pairing.T, row_weight.T.astype(F32), means, shares
    )


def solution(mesh):
    in_specs = (
        P("image", None, None),
        P("crop", "image", None),
        P(None, ("crop", "proto")),
        P(None, ("crop", "proto")),
        P("crop", "image"),
        P("crop", "image"),
    )
    out_specs = (P("crop", "image", None), P("crop", "image"))
    return jax.shard_map(shards, mesh=mesh, in_specs=in_specs, out_specs=out_specs, check_vma=False)
```

time: 183 us -> 72.5 us (0.40)
  blocking collectives: 107 us -> 10.5 us
  starting transfers between devices: 0.08 us -> 21.7 us
  waiting for transfers between devices: 34.8 us -> 13.6 us
  between operations: 14.9 us -> 0.78 us
  Pallas kernels: 0 us -> 12 us
  matrix products: 11.4 us -> 0 us
  other arithmetic: 12 us -> 2.01 us
  local copies, waits for them, and re-layouts: 1.75 us -> 11.4 us
    psum x8 -> x0, blocking collectives: 98.9 us -> none  [the longest x3 45.1 us: row_step(): lax.psum(jnp.sum(transport_plan, axis=1), ('crop', 'proto'))[:, None]]
    psum x1 -> x0, waiting for transfers between devices: 34.8 us -> none  [shards(): own_back, own_cross = lax.psum((own_back, own_cross), 'proto')]
    ppermute x0 -> x15, starting transfers between devices: none -> 18.4 us  [swap(): return lax.ppermute(values, axis, [(i, i ^ distance) for i in range(count)])]
    pallas_call x0 -> x7, Pallas kernels: none -> 12 us  [run(): pl.pallas_call(body, in_specs=[IN_SMEM] * scalars + [IN_VMEM] * (count -...]
    dot_general x3 -> x0, matrix products: 11.4 us -> none  [the longest x1 5.26 us: shards(): jnp.einsum('lbk,dk->lbd', linear_factors, student_weight_matrix, preferre...]
    unnamed x12 -> x21, local copies, waits for them, and re-layouts: 0.62 us -> 11.3 us
    all_to_all x0 -> x1, blocking collectives: none -> 10.5 us  [shards(): lax.all_to_all(sums, both, 0, 0)]
    ppermute x0 -> x15, waiting for transfers between devices: none -> 8.06 us  [swap(): return lax.ppermute(values, axis, [(i, i ^ distance) for i in range(count)])]
  transfers between devices with their start and end apart: 2 -> 16, of which waited for: 1 -> 5; matrix products, arithmetic and copies ran while one was open for 1% -> 3% of each run, Pallas kernels for 0% -> 9%
where the time goes in v2:
time: 72.5 us; the launch traced here: 72.1 us
  starting transfers between devices  21.7 us (30%)
  waiting for transfers between devices  13.6 us (19%)
  Pallas kernels  12 us (17%)
  local copies, waits for them, and re-layouts  11.4 us (16%)
  blocking collectives  10.5 us (14%)
  other arithmetic  2.01 us (3%)
  between operations  0.78 us (1%)
    ppermute x15, starting transfers between devices, swap(): return lax.ppermute(values, axis, [(i, i ^ distance) for i in range(count)])  18.4 us
    pallas_call x7, Pallas kernels, run(): pl.pallas_call(body, in_specs=[IN_SMEM] * scalars + [IN_VMEM] * (count -...  12 us
    unnamed x21, local copies, waits for them, and re-layouts  11.3 us
    all_to_all x1, blocking collectives, shards(): lax.all_to_all(sums, both, 0, 0)  10.5 us
    ppermute x15, waiting for transfers between devices, swap(): return lax.ppermute(values, axis, [(i, i ^ distance) for i in range(count)])  8.06 us
    all_to_all x1, waiting for transfers between devices, shards(): sums = lax.all_to_all(sums, both, 0, 0)  5.58 us
    all_to_all x1, starting transfers between devices, shards(): sums = lax.all_to_all(sums, both, 0, 0)  3.34 us
  transfers between devices with their start and end apart: 16, of which 5 were waited for; matrix products, arithmetic and copies ran while one was open for 3% of the time, Pallas kernels for 9%

profile of v2, /device:TPU:0, one launch (start us, length us, event | category | flops | bytes accessed | tf_op | source)
XLA Modules:
  0.0 72.1 jit_solution(3872534641098627480)
XLA Ops:
  0.6 0.5 collective-permute-start.3
  1.1 1.0 %fusion = f32[2,64]{1,0:T(2,128)S(1)} fusion(bf16[64,2,512]{2,1,0:T(2,128)(2,1)} %param.6), kind=kLoop, calls=%fused_computation.2 | loop fusion | flops 196480 | bytes 131584 | tf_op jit(solution)/shard_map/reduce_sum | solution.py:57
  2.2 1.0 %fusion.1 = bf16[2,64,512]{2,1,0:T(8,128)(2,1)S(1)} fusion(f32[2,64]{1,0:T(2,128)S(1)} %add_rsqrt_fusion, bf16[64,2,512]{2,1,0:T(2,128)(2,1)} %param.6), kind=kLoop, calls=%fused_computation.3 | loop fusion | flops 196608 | bytes 262656 | tf_op jit(solution)/shard_map/convert_element_type | solution.py:377
  3.2 2.6 %collective-permute-start = (bf16[128,512]{1,0:T(8,128)(2,1)S(1)}, bf16[128,512]{1,0:T(8,128)(2,1)S(1)}, u32[]{:S(2)}, u32[]{:S(2)}) collective-permute-start(bf16[128,512]{1,0:T(8,128)(2,1)S(1)} %bitcast.13), channel_id=1, source_target_pairs={{0,8},{8,0},{16,24},{24,16},{1,9},{9,1},{17,25},{25,17},{2,10},{10... | collective-permute-start | bytes 393224 | tf_op jit(solution)/shard_map/ppermute | solution.py:120
  5.7 1.5 %collective-permute-start.1 = (bf16[128,512]{1,0:T(8,128)(2,1)S(1)}, bf16[128,512]{1,0:T(8,128)(2,1)S(1)}, u32[]{:S(2)}, u32[]{:S(2)}) collective-permute-start(bf16[128,512]{1,0:T(8,128)(2,1)S(1)} %bitcast.14), channel_id=1, source_target_pairs={{0,16},{8,24},{16,0},{24,8},{1,17},{9,25},{17,1},{25,9},{2,18},{10... | collective-permute-start | bytes 393224 | tf_op jit(solution)/shard_map/ppermute | solution.py:120
  7.3 1.3 %copy-done.4 = bf16[512,2048]{1,0:T(8,128)(2,1)} copy-done((bf16[512,2048]{1,0:T(8,128)(2,1)}, bf16[512,2048]{1,0:T(8,128)(2,1)S(1)}, u32[]{:S(2)}) %copy-start.4) | copy-done | bytes 2097176
  8.6 1.6 %copy-done.2 = bf16[512,2048]{1,0:T(8,128)(2,1)S(1)} copy-done((bf16[512,2048]{1,0:T(8,128)(2,1)S(1)}, bf16[512,2048]{1,0:T(8,128)(2,1)}, u32[]{:S(2)}) %copy-start.2) | copy-done | bytes 2097176
  10.2 1.6 %copy-done.3 = bf16[512,2048]{1,0:T(8,128)(2,1)S(1)} copy-done((bf16[512,2048]{1,0:T(8,128)(2,1)S(1)}, bf16[512,2048]{1,0:T(8,128)(2,1)}, u32[]{:S(2)}) %copy-start.3) | copy-done | bytes 2097176
  11.8 1.6 %copy-done.5 = bf16[512,2048]{1,0:T(8,128)(2,1)S(1)} copy-done((bf16[512,2048]{1,0:T(8,128)(2,1)S(1)}, bf16[512,2048]{1,0:T(8,128)(2,1)}, u32[]{:S(2)}) %copy-start.5) | copy-done | bytes 2097176
  13.4 0.9 %copy-done.6 = bf16[4,64,512]{2,1,0:T(8,128)(2,1)S(1)} copy-done((bf16[4,64,512]{2,1,0:T(8,128)(2,1)S(1)}, bf16[4,64,512]{2,1,0:T(8,128)(2,1)}, u32[]{:S(2)}) %copy-start.6) | copy-done | bytes 262168
  14.4 5.0 %student.1 = (bf16[512,2048]{1,0:T(8,128)(2,1)S(1)}, bf16[512,2048]{1,0:T(8,128)(2,1)S(1)}, s16[64,640]{1,0:T(8,128)(2,1)S(1)}, s16[64,640]{1,0:T(8,128)(2,1)S(1...) custom-call(s32[1]{0:T(128)} %bitcast.1.refs_0_.refs_1_, bf16[256,512]{1,0:T(8,128)(2,1)S(1)} %bitcast.19, ...), custom_call_target="tpu_custom_call" | custom-call | flops 4294967296 | tf_op jit(solution)/shard_map/student/pallas_call | solution.py:35
  19.4 2.1 %collective-permute-start.4 = (s16[64,640]{1,0:T(8,128)(2,1)S(1)}, s16[64,640]{1,0:T(8,128)(2,1)S(1)}, u32[]{:S(2)}, u32[]{:S(2)}) collective-permute-start(s16[64,640]{1,0:T(8,128)(2,1)S(1)} %get-tuple-element.19), channel_id=1, source_target_pairs={{0,1},{1,0},{2,3},{3,2},{4,5},{5,4},{6,7},{7,6},{8,9},{9,8},{10,11... | collective-permute-start | bytes 245768 | tf_op jit(solution)/shard_map/ppermute | solution.py:120
  21.5 2.6 %collective-permute-start.5 = (s16[64,640]{1,0:T(8,128)(2,1)S(1)}, s16[64,640]{1,0:T(8,128)(2,1)S(1)}, u32[]{:S(2)}, u32[]{:S(2)}) collective-permute-start(s16[64,640]{1,0:T(8,128)(2,1)S(1)} %get-tuple-element.20), channel_id=1, source_target_pairs={{0,2},{1,3},{2,0},{3,1},{4,6},{5,7},{6,4},{7,5},{8,10},{9,11},{10,... | collective-permute-start | bytes 245768 | tf_op jit(solution)/shard_map/ppermute | solution.py:120
  24.1 1.6 %first_sweep.1 = (f32[512,2048]{1,0:T(8,128)S(1)}, f32[8,1,512]{2,1,0:T(1,128)S(1)}) custom-call(bf16[128,512]{1,0:T(8,128)(2,1)S(1)} %bitcast.16, bf16[128,512]{1,0:T(8,128)(2,1)S(1)} %collective-permute-done.refs_1_, bf16[128,512]{1,0:T(8,128)(2,1)S(1)} %collective-permute-done.1.refs_2_, bf16[128,512]{1,0:T(8,128)(2,1)S(1)} %collective-permute-done.2.refs_3_, ...), custom_call_target="tpu_custom_call" | custom-call | flops 4294967296 | tf_op jit(solution)/shard_map/first_sweep/pallas_call | solution.py:35
  25.7 10.5 %all_to_all.10.refs_0_ = f32[8,1,512]{2,1,0:T(1,128)S(1)} all-to-all(f32[8,1,512]{2,1,0:T(1,128)S(1)} %get-tuple-element.16), channel_id=1, replica_groups=mesh['image'=4,'crop'=2,'proto'=4] {'crop','proto'}, dimensions={0} | all-to-all | bytes 32768 | tf_op jit(solution)/shard_map/all_to_all | solution.py:392
  36.3 1.7 %sweep.1 = (f32[8,1,512]{2,1,0:T(1,128)}, s16[64,640]{1,0:T(8,128)(2,1)S(1)}, f32[512,2048]{1,0:T(8,128)S(1)}) custom-call(f32[8,1,512]{2,1,0:T(1,128)S(1)} %all_to_all.10.refs_0_, f32[512,2048]{1,0:T(8,128)S(1)} %get-tuple-element.17.refs_1_, s16[64,640]{1,0:T(8,128)(2,1)S(1)} %get-tuple-element.18.refs_2_, ...), custom_call_target="tpu_custom_call", output_to_operand_aliasing={{2}: (1, {})} | custom-call | flops 1000000000 | tf_op jit(solution)/shard_map/sweep/pallas_call | solution.py:35
  38.0 1.9 %copy-done = f32[512,2048]{1,0:T(8,128)} copy-done((f32[512,2048]{1,0:T(8,128)}, f32[512,2048]{1,0:T(8,128)S(1)}, u32[]{:S(2)}) %copy-start) | copy-done | bytes 4194328
  39.9 0.5 collective-permute-start.7
  40.4 0.6 collective-permute-start.8
  41.0 3.3 %collective-permute-start.9 = (s16[64,640]{1,0:T(8,128)(2,1)S(1)}, s16[64,640]{1,0:T(8,128)(2,1)S(1)}, u32[]{:S(2)}, u32[]{:S(2)}) collective-permute-start(s16[64,640]{1,0:T(8,128)(2,1)S(1)} %get-tuple-element.25.refs_7_), channel_id=1, source_target_pairs={{0,3},{1,2},{2,1},{3,0},{4,7},{5,6},{6,5},{7,4},{8,11},{9,10},{10,... | collective-permute-start | bytes 245768 | tf_op jit(solution)/shard_map/ppermute | solution.py:120
  44.3 3.3 %all-to-all-start.1 = ((f32[8,1,512]{2,1,0:T(1,128)}), f32[8,1,512]{2,1,0:T(1,128)S(1)}, u32[]{:S(2)}, u32[]{:S(2)}) async-start(f32[8,1,512]{2,1,0:T(1,128)} %get-tuple-element.22), calls=%async_computation.1 | async-start | bytes 32768 | tf_op jit(solution)/shard_map/all_to_all | solution.py:394
  47.7 5.6 %all-to-all-done.1.refs_1_ = f32[8,1,512]{2,1,0:T(1,128)S(1)} async-done(((f32[8,1,512]{2,1,0:T(1,128)}), f32[8,1,512]{2,1,0:T(1,128)S(1)}, u32[]{:S(2)}, u32[]{:S(2)}) %all-to-all-start.1) | async-done | bytes 16416 | tf_op jit(solution)/shard_map/all_to_all | solution.py:394
  53.3 2.2 %copy-done.1 = f32[512,2048]{1,0:T(8,128)S(1)} copy-done((f32[512,2048]{1,0:T(8,128)S(1)}, f32[512,2048]{1,0:T(8,128)}, u32[]{:S(2)}) %copy-start.1) | copy-done | bytes 4194328
  55.4 1.2 %last_sweep.1 = (f32[64,640]{1,0:T(8,128)S(1)}, f32[64,640]{1,0:T(8,128)S(1)}) custom-call(s32[1]{0:T(128)} %bitcast.refs_0_, f32[8,1,512]{2,1,0:T(1,128)S(1)} %all-to-all-done.1.refs_1_, f32[512,2048]{1,0:T(8,128)S(1)} %copy-done.1, bf16[512,2048]{1,0:T(8,128)(2,1)S(1)} %get-tuple-element.24.refs_3_, ...), custom_call_target="tpu_custom_call" | custom-call | flops 1000000000 | tf_op jit(solution)/shard_map/last_sweep/pallas_call | solution.py:35
  56.9 1.3 %collective-permute-done.10.refs_1_ = f32[64,640]{1,0:T(8,128)S(1)} collective-permute-done((f32[64,640]{1,0:T(8,128)S(1)}, f32[64,640]{1,0:T(8,128)S(1)}, u32[]{:S(2)}, u32[]{:S(2)}) %collective-permute-start.10) | collective-permute-done | bytes 163872 | tf_op jit(solution)/shard_map/ppermute | solution.py:120
  58.3 0.6 collective-permute-start.11
  58.9 0.6 collective-permute-start.12
  59.5 3.3 %collective-permute-start.13 = (s16[64,640]{1,0:T(8,128)(2,1)S(1)}, s16[64,640]{1,0:T(8,128)(2,1)S(1)}, u32[]{:S(2)}, u32[]{:S(2)}) collective-permute-start(s16[64,640]{1,0:T(8,128)(2,1)S(1)} %code_mixed.1.refs_0_), channel_id=1, source_target_pairs={{0,3},{1,2},{2,1},{3,0},{4,7},{5,6},{6,5},{7,4},{8,11},{9,10},{10,... | collective-permute-start | bytes 245768 | tf_op jit(solution)/shard_map/ppermute | solution.py:120
  62.8 1.0 %collective-permute-done.11.refs_1_ = s16[64,640]{1,0:T(8,128)(2,1)S(1)} collective-permute-done((s16[64,640]{1,0:T(8,128)(2,1)S(1)}, s16[64,640]{1,0:T(8,128)(2,1)S(1)}, u32[]{:S(2)}, u32[]{:S(2)}) %collective-permute-start.11) | collective-permute-done | bytes 81952 | tf_op jit(solution)/shard_map/ppermute | solution.py:120
  63.8 4.6 %collective-permute-done.12.refs_2_ = s16[64,640]{1,0:T(8,128)(2,1)S(1)} collective-permute-done((s16[64,640]{1,0:T(8,128)(2,1)S(1)}, s16[64,640]{1,0:T(8,128)(2,1)S(1)}, u32[]{:S(2)}, u32[]{:S(2)}) %collective-permute-start.12) | collective-permute-done | bytes 81952 | tf_op jit(solution)/shard_map/ppermute | solution.py:120
  69.0 1.1 %collective-permute-done.14.refs_6_ = f32[64,512]{1,0:T(8,128)S(1)} collective-permute-done((f32[64,512]{1,0:T(8,128)S(1)}, f32[64,512]{1,0:T(8,128)S(1)}, u32[]{:S(2)}, u32[]{:S(2)}) %collective-permute-start.14) | collective-permute-done | bytes 131104 | tf_op jit(solution)/shard_map/ppermute | solution.py:120
  70.1 2.0 %finish.1 = (f32[4,64,512]{2,1,0:T(8,128)}, f32[4,64]{1,0:T(4,128)}) custom-call(s32[1]{0:T(128)} %bitcast.refs_0_, s32[1]{0:T(128)} %bitcast.1.refs_0_.refs_1_, bf16[4,64,512]{2,1,0:T(8,128)(2,1)S(1)} %copy-done.7, s32[64,4]{1,0:T(8,128)S(1)} %bitcast.17, f32[64,4]{1,0:T(8,128)S(1)} %bitcast.18, f32[64,512]{1,0:T(8,128)S(1)} %mean_protos.1.refs_5_, ...), custom_call_target="tpu_custom_call" | custom-call | flops 1000000000 | tf_op jit(solution)/shard_map/finish/pallas_call | solution.py:35
  (33 shorter events, 1.0 us)
Async XLA Ops:
  0.6 6.7 %collective-permute-start.3 = (bf16[512,2048]{1,0:T(8,128)(2,1)}, bf16[512,2048]{1,0:T(8,128)(2,1)S(1)}, u32[]{:S(2)}, u32[]{:S(2)}) collective-permute-start(bf16[512,2048]{1,0:T(8,128)(2,1)} %refs_3_.1), channel_id=1, source_target_pairs={{0,4},{4,0},{1,5},{5,1},{2,6},{6,2},{3,7},{7,3},{8,12},{12,8},{9,1... | collective-permute-start | bytes 6291464 | tf_op jit(solution)/shard_map/ppermute | solution.py:120
  3.2 20.9 %collective-permute-start = (bf16[128,512]{1,0:T(8,128)(2,1)S(1)}, bf16[128,512]{1,0:T(8,128)(2,1)S(1)}, u32[]{:S(2)}, u32[]{:S(2)}) collective-permute-start(bf16[128,512]{1,0:T(8,128)(2,1)S(1)} %bitcast.13), channel_id=1, source_target_pairs={{0,8},{8,0},{16,24},{24,16},{1,9},{9,1},{17,25},{25,17},{2,10},{10... | collective-permute-start | bytes 393224 | tf_op jit(solution)/shard_map/ppermute | solution.py:120
  5.7 18.4 %collective-permute-start.1 = (bf16[128,512]{1,0:T(8,128)(2,1)S(1)}, bf16[128,512]{1,0:T(8,128)(2,1)S(1)}, u32[]{:S(2)}, u32[]{:S(2)}) collective-permute-start(bf16[128,512]{1,0:T(8,128)(2,1)S(1)} %bitcast.14), channel_id=1, source_target_pairs={{0,16},{8,24},{16,0},{24,8},{1,17},{9,25},{17,1},{25,9},{2,18},{10... | collective-permute-start | bytes 393224 | tf_op jit(solution)/shard_map/ppermute | solution.py:120
  7.3 16.8 %collective-permute-start.2 = (bf16[128,512]{1,0:T(8,128)(2,1)S(1)}, bf16[128,512]{1,0:T(8,128)(2,1)S(1)}, u32[]{:S(2)}, u32[]{:S(2)}) collective-permute-start(bf16[128,512]{1,0:T(8,128)(2,1)S(1)} %bitcast.15), channel_id=1, source_target_pairs={{0,24},{8,16},{16,8},{24,0},{1,25},{9,17},{17,9},{25,1},{2,26},{10... | collective-permute-start | bytes 393224 | tf_op jit(solution)/shard_map/ppermute | solution.py:120
  7.3 1.3 %copy-start.4 = (bf16[512,2048]{1,0:T(8,128)(2,1)}, bf16[512,2048]{1,0:T(8,128)(2,1)S(1)}, u32[]{:S(2)}) copy-start(bf16[512,2048]{1,0:T(8,128)(2,1)S(1)} %collective-permute-done.3.refs_4_) | copy-start | bytes 6291460
  8.6 1.6 %copy-start.2 = (bf16[512,2048]{1,0:T(8,128)(2,1)S(1)}, bf16[512,2048]{1,0:T(8,128)(2,1)}, u32[]{:S(2)}) copy-start(bf16[512,2048]{1,0:T(8,128)(2,1)} %refs_2_.2) | copy-start | bytes 6291460
  10.2 1.6 %copy-start.3 = (bf16[512,2048]{1,0:T(8,128)(2,1)S(1)}, bf16[512,2048]{1,0:T(8,128)(2,1)}, u32[]{:S(2)}) copy-start(bf16[512,2048]{1,0:T(8,128)(2,1)} %refs_3_.1) | copy-start | bytes 6291460
  11.8 1.6 %copy-start.5 = (bf16[512,2048]{1,0:T(8,128)(2,1)S(1)}, bf16[512,2048]{1,0:T(8,128)(2,1)}, u32[]{:S(2)}) copy-start(bf16[512,2048]{1,0:T(8,128)(2,1)} %copy-done.4) | copy-start | bytes 6291460
  13.4 0.9 %copy-start.6 = (bf16[4,64,512]{2,1,0:T(8,128)(2,1)S(1)}, bf16[4,64,512]{2,1,0:T(8,128)(2,1)}, u32[]{:S(2)}) copy-start(bf16[4,64,512]{2,1,0:T(8,128)(2,1)} %refs_2_.3) | copy-start | bytes 786436
  19.4 16.9 %collective-permute-start.4 = (s16[64,640]{1,0:T(8,128)(2,1)S(1)}, s16[64,640]{1,0:T(8,128)(2,1)S(1)}, u32[]{:S(2)}, u32[]{:S(2)}) collective-permute-start(s16[64,640]{1,0:T(8,128)(2,1)S(1)} %get-tuple-element.19), channel_id=1, source_target_pairs={{0,1},{1,0},{2,3},{3,2},{4,5},{5,4},{6,7},{7,6},{8,9},{9,8},{10,11... | collective-permute-start | bytes 245768 | tf_op jit(solution)/shard_map/ppermute | solution.py:120
  21.5 14.8 %collective-permute-start.5 = (s16[64,640]{1,0:T(8,128)(2,1)S(1)}, s16[64,640]{1,0:T(8,128)(2,1)S(1)}, u32[]{:S(2)}, u32[]{:S(2)}) collective-permute-start(s16[64,640]{1,0:T(8,128)(2,1)S(1)} %get-tuple-element.20), channel_id=1, source_target_pairs={{0,2},{1,3},{2,0},{3,1},{4,6},{5,7},{6,4},{7,5},{8,10},{9,11},{10,... | collective-permute-start | bytes 245768 | tf_op jit(solution)/shard_map/ppermute | solution.py:120
  24.1 12.2 %collective-permute-start.6 = (s16[64,640]{1,0:T(8,128)(2,1)S(1)}, s16[64,640]{1,0:T(8,128)(2,1)S(1)}, u32[]{:S(2)}, u32[]{:S(2)}) collective-permute-start(s16[64,640]{1,0:T(8,128)(2,1)S(1)} %get-tuple-element.21), channel_id=1, source_target_pairs={{0,3},{1,2},{2,1},{3,0},{4,7},{5,6},{6,5},{7,4},{8,11},{9,10},{10,... | collective-permute-start | bytes 245768 | tf_op jit(solution)/shard_map/ppermute | solution.py:120
  38.0 1.9 %copy-start = (f32[512,2048]{1,0:T(8,128)}, f32[512,2048]{1,0:T(8,128)S(1)}, u32[]{:S(2)}) copy-start(f32[512,2048]{1,0:T(8,128)S(1)} %get-tuple-element.23.refs_2_) | copy-start | bytes 12582916
  39.9 13.3 %collective-permute-start.7 = (s16[64,640]{1,0:T(8,128)(2,1)S(1)}, s16[64,640]{1,0:T(8,128)(2,1)S(1)}, u32[]{:S(2)}, u32[]{:S(2)}) collective-permute-start(s16[64,640]{1,0:T(8,128)(2,1)S(1)} %get-tuple-element.25.refs_7_), channel_id=1, source_target_pairs={{0,1},{1,0},{2,3},{3,2},{4,5},{5,4},{6,7},{7,6},{8,9},{9,8},{10,11... | collective-permute-start | bytes 245768 | tf_op jit(solution)/shard_map/ppermute | solution.py:120
  40.4 12.8 %collective-permute-start.8 = (s16[64,640]{1,0:T(8,128)(2,1)S(1)}, s16[64,640]{1,0:T(8,128)(2,1)S(1)}, u32[]{:S(2)}, u32[]{:S(2)}) collective-permute-start(s16[64,640]{1,0:T(8,128)(2,1)S(1)} %get-tuple-element.25.refs_7_), channel_id=1, source_target_pairs={{0,2},{1,3},{2,0},{3,1},{4,6},{5,7},{6,4},{7,5},{8,10},{9,11},{10,... | collective-permute-start | bytes 245768 | tf_op jit(solution)/shard_map/ppermute | solution.py:120
  41.0 12.2 %collective-permute-start.9 = (s16[64,640]{1,0:T(8,128)(2,1)S(1)}, s16[64,640]{1,0:T(8,128)(2,1)S(1)}, u32[]{:S(2)}, u32[]{:S(2)}) collective-permute-start(s16[64,640]{1,0:T(8,128)(2,1)S(1)} %get-tuple-element.25.refs_7_), channel_id=1, source_target_pairs={{0,3},{1,2},{2,1},{3,0},{4,7},{5,6},{6,5},{7,4},{8,11},{9,10},{10,... | collective-permute-start | bytes 245768 | tf_op jit(solution)/shard_map/ppermute | solution.py:120
  44.3 8.9 %all-to-all-start.1 = ((f32[8,1,512]{2,1,0:T(1,128)}), f32[8,1,512]{2,1,0:T(1,128)S(1)}, u32[]{:S(2)}, u32[]{:S(2)}) async-start(f32[8,1,512]{2,1,0:T(1,128)} %get-tuple-element.22), calls=%async_computation.1 | async-start | bytes 32768 | tf_op jit(solution)/shard_map/all_to_all | solution.py:394
  53.2 2.2 %copy-start.1 = (f32[512,2048]{1,0:T(8,128)S(1)}, f32[512,2048]{1,0:T(8,128)}, u32[]{:S(2)}) copy-start(f32[512,2048]{1,0:T(8,128)} %copy-done) | copy-start | bytes 12582916
  56.7 1.5 %collective-permute-start.10 = (f32[64,640]{1,0:T(8,128)S(1)}, f32[64,640]{1,0:T(8,128)S(1)}, u32[]{:S(2)}, u32[]{:S(2)}) collective-permute-start(f32[64,640]{1,0:T(8,128)S(1)} %get-tuple-element.27), channel_id=1, source_target_pairs={{0,4},{4,0},{1,5},{5,1},{2,6},{6,2},{3,7},{7,3},{8,12},{12,8},{9,1... | collective-permute-start | bytes 491528 | tf_op jit(solution)/shard_map/ppermute | solution.py:120
  58.3 10.5 %copy-start.8 = (s32[4,64]{1,0:T(4,128)S(1)}, s32[4,64]{1,0:T(4,128)}, u32[]{:S(2)}) copy-start(s32[4,64]{1,0:T(4,128)} %param.10) | copy-start | bytes 3076
  58.3 10.6 %copy-start.9 = (bf16[4,64]{1,0:T(4,128)(2,1)S(1)}, bf16[4,64]{1,0:T(4,128)(2,1)}, u32[]{:S(2)}) copy-start(bf16[4,64]{1,0:T(4,128)(2,1)} %param.11) | copy-start | bytes 1540
  58.3 11.8 %copy-start.7 = (bf16[4,64,512]{2,1,0:T(8,128)(2,1)S(1)}, bf16[4,64,512]{2,1,0:T(8,128)(2,1)}, u32[]{:S(2)}) copy-start(bf16[4,64,512]{2,1,0:T(8,128)(2,1)} %refs_2_.3) | copy-start | bytes 786436
  58.3 5.4 %collective-permute-start.11 = (s16[64,640]{1,0:T(8,128)(2,1)S(1)}, s16[64,640]{1,0:T(8,128)(2,1)S(1)}, u32[]{:S(2)}, u32[]{:S(2)}) collective-permute-start(s16[64,640]{1,0:T(8,128)(2,1)S(1)} %code_mixed.1.refs_0_), channel_id=1, source_target_pairs={{0,1},{1,0},{2,3},{3,2},{4,5},{5,4},{6,7},{7,6},{8,9},{9,8},{10,11... | collective-permute-start | bytes 245768 | tf_op jit(solution)/shard_map/ppermute | solution.py:120
  58.9 9.5 %collective-permute-start.12 = (s16[64,640]{1,0:T(8,128)(2,1)S(1)}, s16[64,640]{1,0:T(8,128)(2,1)S(1)}, u32[]{:S(2)}, u32[]{:S(2)}) collective-permute-start(s16[64,640]{1,0:T(8,128)(2,1)S(1)} %code_mixed.1.refs_0_), channel_id=1, source_target_pairs={{0,2},{1,3},{2,0},{3,1},{4,6},{5,7},{6,4},{7,5},{8,10},{9,11},{10,... | collective-permute-start | bytes 245768 | tf_op jit(solution)/shard_map/ppermute | solution.py:120
  59.5 8.9 %collective-permute-start.13 = (s16[64,640]{1,0:T(8,128)(2,1)S(1)}, s16[64,640]{1,0:T(8,128)(2,1)S(1)}, u32[]{:S(2)}, u32[]{:S(2)}) collective-permute-start(s16[64,640]{1,0:T(8,128)(2,1)S(1)} %code_mixed.1.refs_0_), channel_id=1, source_target_pairs={{0,3},{1,2},{2,1},{3,0},{4,7},{5,6},{6,5},{7,4},{8,11},{9,10},{10,... | collective-permute-start | bytes 245768 | tf_op jit(solution)/shard_map/ppermute | solution.py:120
  68.7 1.4 %collective-permute-start.14 = (f32[64,512]{1,0:T(8,128)S(1)}, f32[64,512]{1,0:T(8,128)S(1)}, u32[]{:S(2)}, u32[]{:S(2)}) collective-permute-start(f32[64,512]{1,0:T(8,128)S(1)} %mean_protos.1.refs_5_), channel_id=1, source_target_pairs={{0,4},{4,0},{1,5},{5,1},{2,6},{6,2},{3,7},{7,3},{8,12},{12,8},{9,1... | collective-permute-start | bytes 393224 | tf_op jit(solution)/shard_map/ppermute | solution.py:120

commit v3 on v2

--- a/solution.py
+++ b/solution.py
@@ -22,10 +22,11 @@
 I16 = jnp.int16
 
 IN_VMEM = pl.BlockSpec(memory_space=pltpu.VMEM)
+IN_HBM = pl.BlockSpec(memory_space=pltpu.HBM)
 IN_SMEM = pl.BlockSpec(memory_space=pltpu.SMEM)
 
 
-def call(kernel, name, out_shape, scratch=(), scalars=0, vmem=16, after=(), flops=10**9, aliases=None):
+def call(kernel, name, out_shape, scratch=(), scalars=0, vmem=16, after=(), flops=10**9, aliases=None, far=()):
     def run(*operands):
         count = len(operands)
 
@@ -35,7 +36,7 @@
         return pl.pallas_call(
             body,
             in_specs=[IN_SMEM] * scalars
-            + [IN_VMEM] * (count - scalars)
+            + [IN_HBM if i in far else IN_VMEM for i in range(scalars, count)]
             + [pl.BlockSpec(memory_space=pl.ANY)] * len(after),
             out_specs=jax.tree.map(lambda _: IN_VMEM, out_shape),
             out_shape=out_shape,
@@ -120,29 +121,84 @@
     return lax.ppermute(values, axis, [(i, i ^ distance) for i in range(count)])
 
 
-def student_kernel(count, block, place, feats, teacher_protos, *refs):
-    protos, refs = refs[:count], refs[count:]
-    unit_protos, unit_teacher = refs[:2]
-    outs, (unit_feats, back) = refs[2:-2], refs[-2:]
-    width, columns = unit_protos.shape
-    unit_feats[...] = unit_rows(feats[...].astype(F32)).astype(BF16)
-    for start in range(0, columns, block):
-        here = slice(start, start + block)
-        unit_teacher[:, here] = unit_columns(teacher_protos[:, here].astype(F32)).astype(BF16)
-        for k, part in enumerate(protos):
-            weights = unit_columns(part[:, here].astype(F32)).astype(BF16)
-            if k == 0:
-                unit_protos[:, here] = weights
-            logits = jnp.dot(unit_feats[...], weights, preferred_element_type=F32)
-            terms = jnp.exp(logits * (1.0 / student_softness))
-            sums = lane_groups(terms)
-            sides = dot_t(terms.astype(BF16), weights)
-            if start == 0 and k == 0:
-                back[:, width:] = sums
-                back[:, :width] = sides
-            else:
-                back[:, width:] += sums
-                back[:, :width] += sides
+def fetch(sources, buffers, sems, block):
+    columns = buffers[0].shape[1]
+    copies = []
+    for j, start in enumerate(range(0, columns, block)):
+        here = pl.ds(start, block)
+        copies.append(
+            [
+                pltpu.make_async_copy(source.at[:, here], buffer.at[:, here], sems.at[i, j])
+                for i, (source, buffer) in enumerate(zip(sources, buffers))
+            ]
+        )
+    for group in copies:
+        for copy in group:
+            copy.start()
+    return copies
+
+
+def add_side(back, unit_feats, weights, fresh):
+    width = weights.shape[0]
+    logits = jnp.dot(unit_feats[...], weights, preferred_element_type=F32)
+    terms = jnp.exp(logits * (1.0 / student_softness))
+    sums = lane_groups(terms)
+    sides = dot_t(terms.astype(BF16), weights)
+    if fresh:
+        back[:, width:] = sums
+        back[:, :width] = sides
+    else:
+        back[:, width:] += sums
+        back[:, :width] += sides
+
+
+def own_kernel(block, crop_place, proto_place, feats, protos, teacher_protos, unit_protos, unit_teacher, unit_feats, back, *refs):
+    raw, buffers, raw_sem, sems = refs[0], refs[1:3], refs[3], refs[4]
+    raw_copy = pltpu.make_async_copy(feats, raw, raw_sem)
+    raw_copy.start()
+    copies = fetch([protos, teacher_protos], buffers, sems, block)
+    raw_copy.wait()
+    unit_feats[...] = unit_rows(raw[...].astype(F32)).astype(BF16)
+    for j, group in enumerate(copies):
+        here = slice(j * block, (j + 1) * block)
+        group[0].wait()
+        weights = unit_columns(buffers[0][:, here].astype(F32)).astype(BF16)
+        unit_protos[:, here] = weights
+        add_side(back, unit_feats, weights, j == 0)
+        group[1].wait()
+        unit_teacher[:, here] = unit_columns(buffers[1][:, here].astype(F32)).astype(BF16)
+
+
+def own_call(crop_place, proto_place, feats, protos, teacher_protos, block):
+    width, columns = protos.shape
+    rows = feats.shape[0]
+    return call(
+        functools.partial(own_kernel, block),
+        "student_own",
+        [shape((width, columns), BF16)] * 2 + [shape((rows, width), BF16), shape((rows, width + LANES))],
+        [pltpu.VMEM((rows, width), BF16)]
+        + [pltpu.VMEM((width, columns), BF16)] * 2
+        + [pltpu.SemaphoreType.DMA, pltpu.SemaphoreType.DMA((2, columns // block))],
+        scalars=2,
+        vmem=47,
+        far=[2, 3, 4],
+        flops=4 * rows * columns * width,
+    )(crop_place, proto_place, feats, protos, teacher_protos)
+
+
+def other_kernel(count, block, place, unit_feats, partial, *refs):
+    sources, refs = refs[:count], refs[count:]
+    outs, refs = refs[: -count - 2], refs[-count - 2 :]
+    back, buffers, sems = refs[0], refs[1:-1], refs[-1]
+    width = unit_feats.shape[1]
+    copies = fetch(sources, buffers, sems, block)
+    back[...] = partial[...]
+    for j, group in enumerate(copies):
+        here = slice(j * block, (j + 1) * block)
+        for copy, buffer in zip(group, buffers):
+            copy.wait()
+            weights = unit_columns(buffer[:, here].astype(F32)).astype(BF16)
+            add_side(back, unit_feats, weights, False)
     share = outs[0].shape[0]
     for k, out in enumerate(outs):
         first = pl.multiple_of(jnp.bitwise_xor(place[0], k) * share, share)
@@ -150,37 +206,44 @@
         store_code(out, total[:, :width], lane_sums(total[:, width:]))
 
 
-def student_call(place, feats, teacher_protos, protos, pieces, block):
-    width, columns = teacher_protos.shape
-    rows = feats.shape[0]
-    out = call(
-        functools.partial(student_kernel, len(protos), block),
-        "student",
-        [shape((width, columns), BF16)] * 2 + [shape((rows // pieces, width + LANES), I16)] * pieces,
-        [pltpu.VMEM((rows, width), BF16), pltpu.VMEM((rows, width + LANES), F32)],
+def other_call(place, unit_feats, back, protos, pieces, block):
+    width, columns = protos[0].shape
+    rows = unit_feats.shape[0]
+    count = len(protos)
+    return call(
+        functools.partial(other_kernel, count, block),
+        "student_other",
+        [shape((rows // pieces, width + LANES), I16)] * pieces,
+        [pltpu.VMEM((rows, width + LANES), F32)]
+        + [pltpu.VMEM((width, columns), BF16)] * count
+        + [pltpu.SemaphoreType.DMA((count, columns // block))],
         scalars=1,
-        vmem=48 if len(protos) > 2 else 16,
-        flops=8 * rows * len(protos) * columns * width,
-    )(place, feats, teacher_protos, *protos)
-    return out[0], out[1], out[2:]
+        vmem=48 if count > 1 else 16,
+        far=range(3, 3 + count),
+        flops=4 * rows * count * columns * width,
+    )(place, unit_feats, back, *protos)
 
 
 def first_kernel(count, block, *refs):
-    parts, (weights, plan, sums, partial) = refs[:count], refs[count:]
+    parts, (weights, plan, sums, unit, partial) = refs[:count], refs[count:]
     columns = weights.shape[1]
+    first = 0
+    for part in parts:
+        images, views, _ = part.shape
+        for view in range(views):
+            unit[first : first + images, :] = unit_rows(part[:, view, :].astype(F32)).astype(BF16)
+            first += images
     for start in range(0, columns, block):
         here = slice(start, start + block)
         column_sums = None
-        first = 0
-        for part in parts:
-            rows = part.shape[0]
+        for first in range(0, unit.shape[0], LANES):
             values = jnp.exp(
-                jnp.dot(part[...], weights[:, here], preferred_element_type=F32) * (1.0 / teacher_softness)
+                jnp.dot(unit[first : first + LANES, :], weights[:, here], preferred_element_type=F32)
+                * (1.0 / teacher_softness)
             )
-            plan[first : first + rows, here] = values
+            plan[first : first + LANES, here] = values
             total = jnp.sum(values, axis=0, keepdims=True)
             column_sums = total if column_sums is None else column_sums + total
-            first += rows
         terms = lane_groups(plan[:, here] * (1.0 / column_sums))
         if start == 0:
             partial[...] = terms
@@ -197,12 +260,12 @@
 
 def first_call(parts, weights, copies, block, after=()):
     columns = weights.shape[1]
-    rows = sum(part.shape[0] for part in parts)
+    rows = sum(part.shape[0] * part.shape[1] for part in parts)
     return call(
         functools.partial(first_kernel, len(parts), block),
         "first_sweep",
         [shape((rows, columns)), shape((copies, 1, rows))],
-        [pltpu.VMEM((rows, LANES), F32)],
+        [pltpu.VMEM((rows, weights.shape[0]), BF16), pltpu.VMEM((rows, LANES), F32)],
         after=after,
         flops=8 * rows * columns * weights.shape[0],
     )(*parts, weights)
@@ -288,6 +351,10 @@
     )(place, row_sums, plan, unit_protos)
 
 
+def as_column(row):
+    return jnp.broadcast_to(row, (LANES, row.shape[1])).T[:, :1]
+
+
 def lane_sums(values):
     return jnp.sum(values, axis=1, keepdims=True)
 
@@ -329,14 +396,16 @@
         totals[pl.ds(first, rows), :] = jnp.broadcast_to(extra, (rows, LANES))
     images = feats.shape[1]
     for crop in range(feats.shape[0]):
+        picked_column = as_column(picked[crop : crop + 1, :].astype(F32))
+        weight_column = as_column(weights[crop : crop + 1, :].astype(F32))
         raw = feats[crop].astype(F32)
         chosen = means[:images, :]
         for view in range(1, views):
             chosen = jnp.where(
-                picked[:, crop : crop + 1] == view, means[view * images : (view + 1) * images, :], chosen
+                picked_column == view, means[view * images : (view + 1) * images, :], chosen
             )
         here = slice(crop * images, (crop + 1) * images)
-        factor = weights[:, crop : crop + 1] * (1.0 / student_softness)
+        factor = weight_column * (1.0 / student_softness)
         back_sum = factor * (expected[here, :] - chosen)
         scales = lax.rsqrt(lane_sums(raw * raw) + epsilon)
         along = lane_sums(raw * back_sum)
@@ -373,19 +442,17 @@
     both = ("crop", "proto")
     block = 512
 
-    own_rows = (
-        unit_rows(jnp.swapaxes(teacher_feats, 0, 1).astype(F32)).astype(BF16).reshape(views * images, width)
-    )
-    teacher_parts = [own_rows] + [swap(own_rows, "image", k) for k in range(1, image_devices)]
+    teacher_parts = [teacher_feats] + [swap(teacher_feats, "image", k) for k in range(1, image_devices)]
     feats = student_feats.reshape(crops * images, width)
     protos = [student_protos] + [swap(student_protos, "crop", k) for k in range(1, crop_devices)]
 
     pieces = proto_devices
     if crops * images % (pieces * ROW_TILE):
         pieces, proto_place = 1, jnp.zeros((1,), jnp.int32)
-    unit_protos, unit_teacher, coded = student_call(
-        proto_place, feats, teacher_protos, protos, pieces, block
+    unit_protos, unit_teacher, unit_feats, back = own_call(
+        crop_place, proto_place, feats, student_protos, teacher_protos, block
     )
+    coded = other_call(proto_place, unit_feats, back, protos[1:], pieces, block)
     plan, sums = first_call(teacher_parts, unit_teacher, crop_devices * proto_devices, block)
     shares = [coded[0]] + [swap(coded[k % pieces], "proto", k) for k in range(1, proto_devices)]
     for _ in range(SWEEPS - 2):
@@ -400,7 +467,7 @@
     means = mean_call([mixed] + [swap(mixed, "proto", k) for k in range(1, proto_devices)])
     means = [means] + [swap(means, "crop", k) for k in range(1, crop_devices)]
     return finish_call(
-        views, crop_place, proto_place, student_feats, pairing.T, row_weight.T.astype(F32), means, shares
+        views, crop_place, proto_place, student_feats, pairing, row_weight, means, shares
     )
 
 

time: 72.5 us -> 61.8 us (0.85)
  local copies, waits for them, and re-layouts: 11.4 us -> 0.97 us
  blocking collectives: 10.5 us -> 18.6 us
  waiting for transfers between devices: 13.6 us -> 7.97 us
  starting transfers between devices: 21.7 us -> 18.5 us
  Pallas kernels: 12 us -> 14.9 us
  other arithmetic: 2.01 us -> 0 us
    unnamed x21 -> x8, local copies, waits for them, and re-layouts: 11.3 us -> 0.97 us
    all_to_all x0 -> x1, blocking collectives: none -> 8.02 us  [shards(): sums = lax.all_to_all(sums, both, 0, 0)]
    all_to_all x1 -> x0, waiting for transfers between devices: 5.58 us -> none  [shards(): sums = lax.all_to_all(sums, both, 0, 0)]
    all_to_all x1 -> x0, starting transfers between devices: 3.34 us -> none  [shards(): sums = lax.all_to_all(sums, both, 0, 0)]
    pallas_call x7 -> x8, Pallas kernels: 12 us -> 14.9 us  [run(): pl.pallas_call(body, in_specs=[IN_SMEM] * scalars + [IN_HBM if i in far e...]
    reduce_sum x1 -> x0, other arithmetic: 1.01 us -> none  [unit_rows(): jnp.sum(raw_rows * raw_rows, axis=-1, keepdims=True) + epsilon]
    convert_element_type x1 -> x0, other arithmetic: 0.99 us -> none  [shards(): unit_rows(jnp.swapaxes(teacher_feats, 0, 1).astype(F32)).astype(BF16)]
  transfers between devices with their start and end apart: 16 -> 15, of which waited for: 5 -> 4; matrix products, arithmetic and copies ran while one was open for 3% -> 0% of each run, Pallas kernels for 9% -> 15%
where the time goes in v3:
time: 61.8 us; the launch traced here: 61.6 us
  blocking collectives  18.6 us (30%)
  starting transfers between devices  18.5 us (30%)
  Pallas kernels  14.9 us (24%)
  waiting for transfers between devices  7.97 us (13%)
  local copies, waits for them, and re-layouts  0.97 us (2%)
  between operations  0.75 us (1%)
    ppermute x15, starting transfers between devices, swap(): return lax.ppermute(values, axis, [(i, i ^ distance) for i in range(count)])  18.5 us
    pallas_call x8, Pallas kernels, run(): pl.pallas_call(body, in_specs=[IN_SMEM] * scalars + [IN_HBM if i in far e...  14.9 us
    all_to_all x1, blocking collectives, shards(): lax.all_to_all(sums, both, 0, 0)  10.6 us
    all_to_all x1, blocking collectives, shards(): sums = lax.all_to_all(sums, both, 0, 0)  8.02 us
    ppermute x15, waiting for transfers between devices, swap(): return lax.ppermute(values, axis, [(i, i ^ distance) for i in range(count)])  7.97 us
  transfers between devices with their start and end apart: 15, of which 4 were waited for; matrix products, arithmetic and copies ran while one was open for 0% of the time, Pallas kernels for 15%

profile of v3, /device:TPU:0, one launch (start us, length us, event | category | flops | bytes accessed | tf_op | source)
XLA Modules:
  0.0 61.6 jit_solution(9536303599609305193)
XLA Ops:
  0.6 0.5 collective-permute-start.3
  1.1 2.6 %collective-permute-start.1 = (bf16[64,2,512]{2,1,0:T(2,128)(2,1)}, bf16[64,2,512]{2,1,0:T(2,128)(2,1)S(1)}, u32[]{:S(2)}, u32[]{:S(2)}) collective-permute-start(bf16[64,2,512]{2,1,0:T(2,128)(2,1)} %refs_0_.1), channel_id=1, source_target_pairs={{0,16},{8,24},{16,0},{24,8},{1,17},{9,25},{17,1},{25,9},{2,18},{10... | collective-permute-start | bytes 393224 | tf_op jit(solution)/shard_map/ppermute | solution.py:121
  3.7 1.5 %collective-permute-start = (bf16[64,2,512]{2,1,0:T(2,128)(2,1)}, bf16[64,2,512]{2,1,0:T(2,128)(2,1)S(1)}, u32[]{:S(2)}, u32[]{:S(2)}) collective-permute-start(bf16[64,2,512]{2,1,0:T(2,128)(2,1)} %refs_0_.1), channel_id=1, source_target_pairs={{0,8},{8,0},{16,24},{24,16},{1,9},{9,1},{17,25},{25,17},{2,10},{10... | collective-permute-start | bytes 393224 | tf_op jit(solution)/shard_map/ppermute | solution.py:121
  5.2 0.1 collective-permute-start.2
  5.3 0.9 %copy-done = bf16[4,64,512]{2,1,0:T(8,128)(2,1)S(1)} copy-done((bf16[4,64,512]{2,1,0:T(8,128)(2,1)S(1)}, bf16[4,64,512]{2,1,0:T(8,128)(2,1)}, u32[]{:S(2)}) %copy-start) | copy-done | bytes 262168
  6.2 4.2 %student_own.1 = (bf16[512,2048]{1,0:T(8,128)(2,1)S(1)}, bf16[512,2048]{1,0:T(8,128)(2,1)S(1)}, bf16[256,512]{1,0:T(8,128)(2,1)S(1)}, f32[256,640]{1,0:T(8,128)S(1)}) custom-call(s32[1]{0:T(128)} %bitcast.refs_0_, s32[1]{0:T(128)} %bitcast.1.refs_1_.refs_0_, bf16[256,512]{1,0:T(8,128)(2,1)S(1)} %bitcast.3, bf16[512,2048]{1,0:T(8,128)(2,1)} %refs_3_.2, ...), custom_call_target="tpu_custom_call" | custom-call | flops 1073741824 | tf_op jit(solution)/shard_map/student_own/pallas_call | solution.py:36
  10.4 0.0 copy-start.1
  10.5 2.9 %student_other.1 = (s16[64,640]{1,0:T(8,128)(2,1)S(1)}, s16[64,640]{1,0:T(8,128)(2,1)S(1)}, s16[64,640]{1,0:T(8,128)(2,1)S(1)}, s16[64,640]{1,0:T(8,128)(2,1)S(1)}) custom-call(s32[1]{0:T(128)} %bitcast.1.refs_1_.refs_0_, bf16[256,512]{1,0:T(8,128)(2,1)S(1)} %get-tuple-element.20.refs_1_, f32[256,640]{1,0:T(8,128)S(1)} %get-tuple-element.21.refs_2_, ...), custom_call_target="tpu_custom_call" | custom-call | flops 1073741824 | tf_op jit(solution)/shard_map/student_other/pallas_call | solution.py:36
  13.3 2.1 %collective-permute-start.4 = (s16[64,640]{1,0:T(8,128)(2,1)S(1)}, s16[64,640]{1,0:T(8,128)(2,1)S(1)}, u32[]{:S(2)}, u32[]{:S(2)}) collective-permute-start(s16[64,640]{1,0:T(8,128)(2,1)S(1)} %get-tuple-element.23), channel_id=1, source_target_pairs={{0,1},{1,0},{2,3},{3,2},{4,5},{5,4},{6,7},{7,6},{8,9},{9,8},{10,11... | collective-permute-start | bytes 245768 | tf_op jit(solution)/shard_map/ppermute | solution.py:121
  15.4 2.6 %collective-permute-start.5 = (s16[64,640]{1,0:T(8,128)(2,1)S(1)}, s16[64,640]{1,0:T(8,128)(2,1)S(1)}, u32[]{:S(2)}, u32[]{:S(2)}) collective-permute-start(s16[64,640]{1,0:T(8,128)(2,1)S(1)} %get-tuple-element.24), channel_id=1, source_target_pairs={{0,2},{1,3},{2,0},{3,1},{4,6},{5,7},{6,4},{7,5},{8,10},{9,11},{10,... | collective-permute-start | bytes 245768 | tf_op jit(solution)/shard_map/ppermute | solution.py:121
  18.0 2.4 %first_sweep.1 = (f32[512,2048]{1,0:T(8,128)S(1)}, f32[8,1,512]{2,1,0:T(1,128)S(1)}) custom-call(bf16[64,2,512]{2,1,0:T(2,128)(2,1)S(1)} %copy-done.1, bf16[64,2,512]{2,1,0:T(2,128)(2,1)S(1)} %collective-permute-done.refs_1_, bf16[64,2,512]{2,1,0:T(2,128)(2,1)S(1)} %collective-permute-done.1.refs_2_, bf16[64,2,512]{2,1,0:T(2,128)(2,1)S(1)} %collective-permute-done.2.refs_3_, ...), custom_call_target="tpu_custom_call" | custom-call | flops 4294967296 | tf_op jit(solution)/shard_map/first_sweep/pallas_call | solution.py:36
  20.4 10.6 %all_to_all.10.refs_0_ = f32[8,1,512]{2,1,0:T(1,128)S(1)} all-to-all(f32[8,1,512]{2,1,0:T(1,128)S(1)} %get-tuple-element.18), channel_id=1, replica_groups=mesh['image'=4,'crop'=2,'proto'=4] {'crop','proto'}, dimensions={0} | all-to-all | bytes 32768 | tf_op jit(solution)/shard_map/all_to_all | solution.py:459
  31.0 1.2 %sweep.1 = (f32[8,1,512]{2,1,0:T(1,128)S(1)}, s16[64,640]{1,0:T(8,128)(2,1)S(1)}, f32[512,2048]{1,0:T(8,128)S(1)}) custom-call(f32[8,1,512]{2,1,0:T(1,128)S(1)} %all_to_all.10.refs_0_, f32[512,2048]{1,0:T(8,128)S(1)} %get-tuple-element.19.refs_1_, s16[64,640]{1,0:T(8,128)(2,1)S(1)} %get-tuple-element.22.refs_2_, ...), custom_call_target="tpu_custom_call", output_to_operand_aliasing={{2}: (1, {})} | custom-call | flops 1000000000 | tf_op jit(solution)/shard_map/sweep/pallas_call | solution.py:36
  32.2 0.6 collective-permute-start.9
  32.8 1.4 %collective-permute-start.8 = (s16[64,640]{1,0:T(8,128)(2,1)S(1)}, s16[64,640]{1,0:T(8,128)(2,1)S(1)}, u32[]{:S(2)}, u32[]{:S(2)}) collective-permute-start(s16[64,640]{1,0:T(8,128)(2,1)S(1)} %get-tuple-element.29.refs_7_), channel_id=1, source_target_pairs={{0,2},{1,3},{2,0},{3,1},{4,6},{5,7},{6,4},{7,5},{8,10},{9,11},{10,... | collective-permute-start | bytes 245768 | tf_op jit(solution)/shard_map/ppermute | solution.py:121
  34.2 2.4 %collective-permute-start.7 = (s16[64,640]{1,0:T(8,128)(2,1)S(1)}, s16[64,640]{1,0:T(8,128)(2,1)S(1)}, u32[]{:S(2)}, u32[]{:S(2)}) collective-permute-start(s16[64,640]{1,0:T(8,128)(2,1)S(1)} %get-tuple-element.29.refs_7_), channel_id=1, source_target_pairs={{0,1},{1,0},{2,3},{3,2},{4,5},{5,4},{6,7},{7,6},{8,9},{9,8},{10,11... | collective-permute-start | bytes 245768 | tf_op jit(solution)/shard_map/ppermute | solution.py:121
  36.6 8.0 %all_to_all.11.refs_1_ = f32[8,1,512]{2,1,0:T(1,128)S(1)} all-to-all(f32[8,1,512]{2,1,0:T(1,128)S(1)} %get-tuple-element.26), channel_id=1, replica_groups=mesh['image'=4,'crop'=2,'proto'=4] {'crop','proto'}, dimensions={0} | all-to-all | bytes 32768 | tf_op jit(solution)/shard_map/all_to_all | solution.py:461
  44.7 1.3 %last_sweep.1 = (f32[64,640]{1,0:T(8,128)S(1)}, f32[64,640]{1,0:T(8,128)S(1)}) custom-call(s32[1]{0:T(128)} %bitcast.refs_0_, f32[8,1,512]{2,1,0:T(1,128)S(1)} %all_to_all.11.refs_1_, f32[512,2048]{1,0:T(8,128)S(1)} %get-tuple-element.27.refs_2_, bf16[512,2048]{1,0:T(8,128)(2,1)S(1)} %get-tuple-element.28.refs_3_, ...), custom_call_target="tpu_custom_call" | custom-call | flops 1000000000 | tf_op jit(solution)/shard_map/last_sweep/pallas_call | solution.py:36
  46.0 0.2 collective-permute-start.10
  46.2 1.3 %collective-permute-done.10.refs_1_ = f32[64,640]{1,0:T(8,128)S(1)} collective-permute-done((f32[64,640]{1,0:T(8,128)S(1)}, f32[64,640]{1,0:T(8,128)S(1)}, u32[]{:S(2)}, u32[]{:S(2)}) %collective-permute-start.10) | collective-permute-done | bytes 163872 | tf_op jit(solution)/shard_map/ppermute | solution.py:121
  47.5 0.2 code_mixed.1.refs_0_
  47.6 0.0 copy-start.2
  47.6 0.0 copy-start.3
  47.6 0.6 collective-permute-start.13
  48.2 1.5 %collective-permute-start.12 = (s16[64,640]{1,0:T(8,128)(2,1)S(1)}, s16[64,640]{1,0:T(8,128)(2,1)S(1)}, u32[]{:S(2)}, u32[]{:S(2)}) collective-permute-start(s16[64,640]{1,0:T(8,128)(2,1)S(1)} %code_mixed.1.refs_0_), channel_id=1, source_target_pairs={{0,2},{1,3},{2,0},{3,1},{4,6},{5,7},{6,4},{7,5},{8,10},{9,11},{10,... | collective-permute-start | bytes 245768 | tf_op jit(solution)/shard_map/ppermute | solution.py:121
  49.7 2.4 %collective-permute-start.11 = (s16[64,640]{1,0:T(8,128)(2,1)S(1)}, s16[64,640]{1,0:T(8,128)(2,1)S(1)}, u32[]{:S(2)}, u32[]{:S(2)}) collective-permute-start(s16[64,640]{1,0:T(8,128)(2,1)S(1)} %code_mixed.1.refs_0_), channel_id=1, source_target_pairs={{0,1},{1,0},{2,3},{3,2},{4,5},{5,4},{6,7},{7,6},{8,9},{9,8},{10,11... | collective-permute-start | bytes 245768 | tf_op jit(solution)/shard_map/ppermute | solution.py:121
  52.1 2.8 %collective-permute-done.13.refs_3_ = s16[64,640]{1,0:T(8,128)(2,1)S(1)} collective-permute-done((s16[64,640]{1,0:T(8,128)(2,1)S(1)}, s16[64,640]{1,0:T(8,128)(2,1)S(1)}, u32[]{:S(2)}, u32[]{:S(2)}) %collective-permute-start.13) | collective-permute-done | bytes 81952 | tf_op jit(solution)/shard_map/ppermute | solution.py:121
  54.9 2.5 %collective-permute-done.12.refs_2_ = s16[64,640]{1,0:T(8,128)(2,1)S(1)} collective-permute-done((s16[64,640]{1,0:T(8,128)(2,1)S(1)}, s16[64,640]{1,0:T(8,128)(2,1)S(1)}, u32[]{:S(2)}, u32[]{:S(2)}) %collective-permute-start.12) | collective-permute-done | bytes 81952 | tf_op jit(solution)/shard_map/ppermute | solution.py:121
  57.4 0.3 mean_protos.1.refs_5_
  57.7 0.1 collective-permute-start.14
  57.8 1.3 %collective-permute-done.14.refs_6_ = f32[64,512]{1,0:T(8,128)S(1)} collective-permute-done((f32[64,512]{1,0:T(8,128)S(1)}, f32[64,512]{1,0:T(8,128)S(1)}, u32[]{:S(2)}, u32[]{:S(2)}) %collective-permute-start.14) | collective-permute-done | bytes 131104 | tf_op jit(solution)/shard_map/ppermute | solution.py:121
  59.1 2.5 %finish.1 = (f32[4,64,512]{2,1,0:T(8,128)}, f32[4,64]{1,0:T(4,128)}) custom-call(s32[1]{0:T(128)} %bitcast.refs_0_, s32[1]{0:T(128)} %bitcast.1.refs_1_.refs_0_, bf16[4,64,512]{2,1,0:T(8,128)(2,1)S(1)} %copy-done, s32[4,64]{1,0:T(4,128)S(1)} %copy-done.2, bf16[4,64]{1,0:T(4,128)(2,1)S(1)} %copy-done.3, f32[64,512]{1,0:T(8,128)S(1)} %mean_protos.1.refs_5_, ...), custom_call_target="tpu_custom_call" | custom-call | flops 1000000000 | tf_op jit(solution)/shard_map/finish/pallas_call | solution.py:36
  (16 shorter events, 0.0 us)
Async XLA Ops:
  0.6 9.8 %collective-permute-start.3 = (bf16[512,2048]{1,0:T(8,128)(2,1)}, bf16[512,2048]{1,0:T(8,128)(2,1)S(1)}, u32[]{:S(2)}, u32[]{:S(2)}) collective-permute-start(bf16[512,2048]{1,0:T(8,128)(2,1)} %refs_3_.2), channel_id=1, source_target_pairs={{0,4},{4,0},{1,5},{5,1},{2,6},{6,2},{3,7},{7,3},{8,12},{12,8},{9,1... | collective-permute-start | bytes 6291464 | tf_op jit(solution)/shard_map/ppermute | solution.py:121
  1.1 16.8 %collective-permute-start.1 = (bf16[64,2,512]{2,1,0:T(2,128)(2,1)}, bf16[64,2,512]{2,1,0:T(2,128)(2,1)S(1)}, u32[]{:S(2)}, u32[]{:S(2)}) collective-permute-start(bf16[64,2,512]{2,1,0:T(2,128)(2,1)} %refs_0_.1), channel_id=1, source_target_pairs={{0,16},{8,24},{16,0},{24,8},{1,17},{9,25},{17,1},{25,9},{2,18},{10... | collective-permute-start | bytes 393224 | tf_op jit(solution)/shard_map/ppermute | solution.py:121
  3.7 14.3 %collective-permute-start = (bf16[64,2,512]{2,1,0:T(2,128)(2,1)}, bf16[64,2,512]{2,1,0:T(2,128)(2,1)S(1)}, u32[]{:S(2)}, u32[]{:S(2)}) collective-permute-start(bf16[64,2,512]{2,1,0:T(2,128)(2,1)} %refs_0_.1), channel_id=1, source_target_pairs={{0,8},{8,0},{16,24},{24,16},{1,9},{9,1},{17,25},{25,17},{2,10},{10... | collective-permute-start | bytes 393224 | tf_op jit(solution)/shard_map/ppermute | solution.py:121
  5.2 12.8 %collective-permute-start.2 = (bf16[64,2,512]{2,1,0:T(2,128)(2,1)}, bf16[64,2,512]{2,1,0:T(2,128)(2,1)S(1)}, u32[]{:S(2)}, u32[]{:S(2)}) collective-permute-start(bf16[64,2,512]{2,1,0:T(2,128)(2,1)} %refs_0_.1), channel_id=1, source_target_pairs={{0,24},{8,16},{16,8},{24,0},{1,25},{9,17},{17,9},{25,1},{2,26},{10... | collective-permute-start | bytes 393224 | tf_op jit(solution)/shard_map/ppermute | solution.py:121
  5.3 0.9 %copy-start = (bf16[4,64,512]{2,1,0:T(8,128)(2,1)S(1)}, bf16[4,64,512]{2,1,0:T(8,128)(2,1)}, u32[]{:S(2)}) copy-start(bf16[4,64,512]{2,1,0:T(8,128)(2,1)} %refs_2_.1) | copy-start | bytes 786436
  10.4 7.6 %copy-start.1 = (bf16[64,2,512]{2,1,0:T(2,128)(2,1)S(1)}, bf16[64,2,512]{2,1,0:T(2,128)(2,1)}, u32[]{:S(2)}) copy-start(bf16[64,2,512]{2,1,0:T(2,128)(2,1)} %refs_0_.1) | copy-start | bytes 393220
  13.3 17.7 %collective-permute-start.4 = (s16[64,640]{1,0:T(8,128)(2,1)S(1)}, s16[64,640]{1,0:T(8,128)(2,1)S(1)}, u32[]{:S(2)}, u32[]{:S(2)}) collective-permute-start(s16[64,640]{1,0:T(8,128)(2,1)S(1)} %get-tuple-element.23), channel_id=1, source_target_pairs={{0,1},{1,0},{2,3},{3,2},{4,5},{5,4},{6,7},{7,6},{8,9},{9,8},{10,11... | collective-permute-start | bytes 245768 | tf_op jit(solution)/shard_map/ppermute | solution.py:121
  15.4 15.6 %collective-permute-start.5 = (s16[64,640]{1,0:T(8,128)(2,1)S(1)}, s16[64,640]{1,0:T(8,128)(2,1)S(1)}, u32[]{:S(2)}, u32[]{:S(2)}) collective-permute-start(s16[64,640]{1,0:T(8,128)(2,1)S(1)} %get-tuple-element.24), channel_id=1, source_target_pairs={{0,2},{1,3},{2,0},{3,1},{4,6},{5,7},{6,4},{7,5},{8,10},{9,11},{10,... | collective-permute-start | bytes 245768 | tf_op jit(solution)/shard_map/ppermute | solution.py:121
  18.0 13.0 %collective-permute-start.6 = (s16[64,640]{1,0:T(8,128)(2,1)S(1)}, s16[64,640]{1,0:T(8,128)(2,1)S(1)}, u32[]{:S(2)}, u32[]{:S(2)}) collective-permute-start(s16[64,640]{1,0:T(8,128)(2,1)S(1)} %get-tuple-element.25), channel_id=1, source_target_pairs={{0,3},{1,2},{2,1},{3,0},{4,7},{5,6},{6,5},{7,4},{8,11},{9,10},{10,... | collective-permute-start | bytes 245768 | tf_op jit(solution)/shard_map/ppermute | solution.py:121
  32.2 12.5 %collective-permute-start.9 = (s16[64,640]{1,0:T(8,128)(2,1)S(1)}, s16[64,640]{1,0:T(8,128)(2,1)S(1)}, u32[]{:S(2)}, u32[]{:S(2)}) collective-permute-start(s16[64,640]{1,0:T(8,128)(2,1)S(1)} %get-tuple-element.29.refs_7_), channel_id=1, source_target_pairs={{0,3},{1,2},{2,1},{3,0},{4,7},{5,6},{6,5},{7,4},{8,11},{9,10},{10,... | collective-permute-start | bytes 245768 | tf_op jit(solution)/shard_map/ppermute | solution.py:121
  32.8 11.9 %collective-permute-start.8 = (s16[64,640]{1,0:T(8,128)(2,1)S(1)}, s16[64,640]{1,0:T(8,128)(2,1)S(1)}, u32[]{:S(2)}, u32[]{:S(2)}) collective-permute-start(s16[64,640]{1,0:T(8,128)(2,1)S(1)} %get-tuple-element.29.refs_7_), channel_id=1, source_target_pairs={{0,2},{1,3},{2,0},{3,1},{4,6},{5,7},{6,4},{7,5},{8,10},{9,11},{10,... | collective-permute-start | bytes 245768 | tf_op jit(solution)/shard_map/ppermute | solution.py:121
  34.2 10.4 %collective-permute-start.7 = (s16[64,640]{1,0:T(8,128)(2,1)S(1)}, s16[64,640]{1,0:T(8,128)(2,1)S(1)}, u32[]{:S(2)}, u32[]{:S(2)}) collective-permute-start(s16[64,640]{1,0:T(8,128)(2,1)S(1)} %get-tuple-element.29.refs_7_), channel_id=1, source_target_pairs={{0,1},{1,0},{2,3},{3,2},{4,5},{5,4},{6,7},{7,6},{8,9},{9,8},{10,11... | collective-permute-start | bytes 245768 | tf_op jit(solution)/shard_map/ppermute | solution.py:121
  46.0 1.5 %collective-permute-start.10 = (f32[64,640]{1,0:T(8,128)S(1)}, f32[64,640]{1,0:T(8,128)S(1)}, u32[]{:S(2)}, u32[]{:S(2)}) collective-permute-start(f32[64,640]{1,0:T(8,128)S(1)} %get-tuple-element.31), channel_id=1, source_target_pairs={{0,4},{4,0},{1,5},{5,1},{2,6},{6,2},{3,7},{7,3},{8,12},{12,8},{9,1... | collective-permute-start | bytes 491528 | tf_op jit(solution)/shard_map/ppermute | solution.py:121
  47.6 11.5 %copy-start.2 = (s32[4,64]{1,0:T(4,128)S(1)}, s32[4,64]{1,0:T(4,128)}, u32[]{:S(2)}) copy-start(s32[4,64]{1,0:T(4,128)} %refs_3_.3) | copy-start | bytes 3076
  47.6 11.5 %copy-start.3 = (bf16[4,64]{1,0:T(4,128)(2,1)S(1)}, bf16[4,64]{1,0:T(4,128)(2,1)}, u32[]{:S(2)}) copy-start(bf16[4,64]{1,0:T(4,128)(2,1)} %refs_4_.3) | copy-start | bytes 1540
  47.6 7.3 %collective-permute-start.13 = (s16[64,640]{1,0:T(8,128)(2,1)S(1)}, s16[64,640]{1,0:T(8,128)(2,1)S(1)}, u32[]{:S(2)}, u32[]{:S(2)}) collective-permute-start(s16[64,640]{1,0:T(8,128)(2,1)S(1)} %code_mixed.1.refs_0_), channel_id=1, source_target_pairs={{0,3},{1,2},{2,1},{3,0},{4,7},{5,6},{6,5},{7,4},{8,11},{9,10},{10,... | collective-permute-start | bytes 245768 | tf_op jit(solution)/shard_map/ppermute | solution.py:121
  48.2 9.2 %collective-permute-start.12 = (s16[64,640]{1,0:T(8,128)(2,1)S(1)}, s16[64,640]{1,0:T(8,128)(2,1)S(1)}, u32[]{:S(2)}, u32[]{:S(2)}) collective-permute-start(s16[64,640]{1,0:T(8,128)(2,1)S(1)} %code_mixed.1.refs_0_), channel_id=1, source_target_pairs={{0,2},{1,3},{2,0},{3,1},{4,6},{5,7},{6,4},{7,5},{8,10},{9,11},{10,... | collective-permute-start | bytes 245768 | tf_op jit(solution)/shard_map/ppermute | solution.py:121
  49.7 7.7 %collective-permute-start.11 = (s16[64,640]{1,0:T(8,128)(2,1)S(1)}, s16[64,640]{1,0:T(8,128)(2,1)S(1)}, u32[]{:S(2)}, u32[]{:S(2)}) collective-permute-start(s16[64,640]{1,0:T(8,128)(2,1)S(1)} %code_mixed.1.refs_0_), channel_id=1, source_target_pairs={{0,1},{1,0},{2,3},{3,2},{4,5},{5,4},{6,7},{7,6},{8,9},{9,8},{10,11... | collective-permute-start | bytes 245768 | tf_op jit(solution)/shard_map/ppermute | solution.py:121
  57.7 1.4 %collective-permute-start.14 = (f32[64,512]{1,0:T(8,128)S(1)}, f32[64,512]{1,0:T(8,128)S(1)}, u32[]{:S(2)}, u32[]{:S(2)}) collective-permute-start(f32[64,512]{1,0:T(8,128)S(1)} %mean_protos.1.refs_5_), channel_id=1, source_target_pairs={{0,4},{4,0},{1,5},{5,1},{2,6},{6,2},{3,7},{7,3},{8,12},{12,8},{9,1... | collective-permute-start | bytes 393224 | tf_op jit(solution)/shard_map/ppermute | solution.py:121

commit v4 on v3

--- a/solution.py
+++ b/solution.py
@@ -83,37 +83,90 @@
     return terms[0]
 
 
-def encode(values, extra):
-    rows = values.shape[0]
+def split_positive(values):
+    power = jnp.floor(jnp.log2(jnp.maximum(values, 1e-30))) + 1.0
+    scaled = values * jnp.exp2(-power) * PARTS
+    high = jnp.minimum(jnp.floor(scaled), LEVELS)
+    low = jnp.minimum(jnp.floor((scaled - high) * PARTS), LEVELS)
+    return power, high, low
+
+
+def join_positive(power, high, low):
+    return (high + low * (1.0 / PARTS)) * (1.0 / PARTS) * jnp.exp2(power)
+
+
+def to_i16(values):
+    return values.astype(jnp.int32).astype(I16)
+
+
+def to_f32(values):
+    return values.astype(jnp.int32).astype(F32)
+
+
+def store_code(out, values, extra):
+    rows, width = values.shape
     largest = jnp.maximum(jnp.max(jnp.abs(values), axis=1, keepdims=True), 1e-30)
     power = jnp.floor(jnp.log2(largest)) + 1.0
     whole = jnp.floor(values * (jnp.exp2(-power) * LEVELS) + 0.5)
-    coded = jnp.clip(whole, -LEVELS, LEVELS).astype(jnp.int32).astype(I16)
-    extra_power = jnp.floor(jnp.log2(jnp.maximum(extra, 1e-30))) + 1.0
-    scaled = extra * jnp.exp2(-extra_power) * PARTS
-    high = jnp.minimum(jnp.floor(scaled), LEVELS)
-    low = jnp.minimum(jnp.floor((scaled - high) * PARTS), LEVELS)
+    out[:rows, :] = to_i16(jnp.clip(whole, -LEVELS, LEVELS))
+    extra_power, high, low = split_positive(extra)
     lane = lax.broadcasted_iota(jnp.int32, (rows, LANES), 1)
     tail = jnp.where(lane == 0, power, jnp.where(lane == 1, extra_power, jnp.where(lane == 2, high, low)))
-    return coded, tail.astype(jnp.int32).astype(I16)
-
-
-def store_code(out, values, extra):
-    width = values.shape[1]
-    out[:, :width], out[:, width:] = encode(values, extra)
+    if rows < LANES:
+        tail = jnp.concatenate([tail, jnp.zeros((LANES - rows, LANES), F32)], axis=0)
+    block = tail.T[:ROW_TILE, :]
+    out[rows:, :] = to_i16(jnp.concatenate([block, jnp.zeros((ROW_TILE, width - LANES), F32)], axis=1))
 
 
 def decode(ref):
-    width = ref.shape[1] - LANES
-    tail = ref[:, width:].astype(jnp.int32).astype(F32)
-    values = ref[:, :width].astype(jnp.int32).astype(F32) * (jnp.exp2(tail[:, 0:1]) * (1.0 / LEVELS))
-    extra = (tail[:, 2:3] + tail[:, 3:4] * (1.0 / PARTS)) * (1.0 / PARTS) * jnp.exp2(tail[:, 1:2])
-    return values, extra
+    rows = ref.shape[0] - ROW_TILE
+    block = to_f32(ref[rows:, :LANES])
+    tail = jnp.concatenate([block, jnp.zeros((LANES - ROW_TILE, LANES), F32)], axis=0).T[:rows, :]
+    values = to_f32(ref[:rows, :]) * (jnp.exp2(tail[:, 0:1]) * (1.0 / LEVELS))
+    return values, join_positive(tail[:, 1:2], tail[:, 2:3], tail[:, 3:4])
 
 
 def decode_sum(refs):
     pairs = [decode(ref) for ref in refs]
     return tree_sum([p[0] for p in pairs]), tree_sum([p[1] for p in pairs])
+
+
+SUMS_AT = 4
+
+
+def pack_kernel(count, *refs):
+    parts, refs = refs[:count], refs[count:]
+    shares, outs = refs[: len(refs) // 2], refs[len(refs) // 2 :]
+    power, high, low = split_positive(tree_sum([part[0] for part in parts]))
+    for share, out in zip(shares, outs):
+        rows = share.shape[0] - ROW_TILE
+        out[:rows, :] = share[:rows, :]
+        at = lax.broadcasted_iota(jnp.int32, (ROW_TILE, share.shape[1]), 0)
+        under = to_f32(share[rows:, :])
+        for k, row in enumerate((power, high, low)):
+            under = jnp.where(at == SUMS_AT + k, row, under)
+        out[rows:, :] = to_i16(under)
+
+
+def pack_call(parts, shares):
+    return call(
+        functools.partial(pack_kernel, len(parts)),
+        "pack_sums",
+        [shape(share.shape, I16) for share in shares],
+    )(*parts, *shares)
+
+
+def read_sums(refs):
+    if refs[0].dtype == I16:
+        terms = []
+        for ref in refs:
+            under = to_f32(ref[ref.shape[0] - ROW_TILE :, :])
+            terms.append(join_positive(*(under[SUMS_AT + k : SUMS_AT + k + 1, :] for k in range(3))))
+        return tree_sum(terms)
+    total = refs[0][0]
+    for k in range(1, refs[0].shape[0]):
+        total = total + refs[0][k]
+    return total
 
 
 def swap(values, axis, distance):
@@ -199,7 +252,7 @@
             copy.wait()
             weights = unit_columns(buffer[:, here].astype(F32)).astype(BF16)
             add_side(back, unit_feats, weights, False)
-    share = outs[0].shape[0]
+    share = outs[0].shape[0] - ROW_TILE
     for k, out in enumerate(outs):
         first = pl.multiple_of(jnp.bitwise_xor(place[0], k) * share, share)
         total = back[pl.ds(first, share), :]
@@ -213,7 +266,7 @@
     return call(
         functools.partial(other_kernel, count, block),
         "student_other",
-        [shape((rows // pieces, width + LANES), I16)] * pieces,
+        [shape((rows // pieces + ROW_TILE, width), I16)] * pieces,
         [pltpu.VMEM((rows, width + LANES), F32)]
         + [pltpu.VMEM((width, columns), BF16)] * count
         + [pltpu.SemaphoreType.DMA((count, columns // block))],
@@ -271,11 +324,8 @@
     )(*parts, weights)
 
 
-def scale_rows(row_sums, row_scale):
-    total = row_sums[0]
-    for k in range(1, row_sums.shape[0]):
-        total = total + row_sums[k]
-    scale = 1.0 / total
+def scale_rows(sum_refs, row_scale):
+    scale = 1.0 / read_sums(sum_refs)
     row_scale[...] = jnp.broadcast_to(scale, (LANES, scale.shape[1])).T
 
 
@@ -284,11 +334,10 @@
     return 1.0 / jnp.sum(weighted, axis=0, keepdims=True)
 
 
-def sweep_kernel(row_sums, plan, *refs):
-    shares, (sums, share, _, row_scale, partial) = refs[:-5], refs[-5:]
-    back, totals = decode_sum(shares)
-    store_code(share, back / totals, totals)
-    scale_rows(row_sums, row_scale)
+def sweep_kernel(count, plan, *refs):
+    shares, refs = refs[:count], refs[count:]
+    sum_refs, (sums, share, _, row_scale, partial) = refs[:-5] or shares, refs[-5:]
+    scale_rows(sum_refs, row_scale)
     for start in range(0, plan.shape[1], LANES):
         terms = plan[:, start : start + LANES] * column_scale(plan, row_scale, start)
         if start == 0:
@@ -296,24 +345,27 @@
         else:
             partial[...] += terms
     store_sums(sums, partial)
-
-
-def sweep_call(row_sums, plan, shares):
+    back, totals = decode_sum(shares)
+    store_code(share, back / totals, totals)
+
+
+def sweep_call(plan, copies, shares, row_sums):
     rows = plan.shape[0]
     return call(
-        sweep_kernel,
+        functools.partial(sweep_kernel, len(shares)),
         "sweep",
-        [shape(row_sums.shape), shape(shares[0].shape, I16), shape(plan.shape)],
+        [shape((copies, 1, rows)), shape(shares[0].shape, I16), shape(plan.shape)],
         [pltpu.VMEM((rows, LANES), F32)] * 2,
-        aliases={1: 2},
-    )(row_sums, plan, *shares)
-
-
-def last_kernel(share, block, place, row_sums, plan, unit_protos, *refs):
+        aliases={0: 2},
+    )(plan, *shares, *row_sums)
+
+
+def last_kernel(share, count, block, place, plan, unit_protos, *refs):
+    sum_refs, refs = refs[:count], refs[count:]
     outs, (row_scale, scaled, mixed) = refs[:-3], refs[-3:]
     own = scaled.shape[0]
     width, columns = unit_protos.shape
-    scale_rows(row_sums, row_scale)
+    scale_rows(sum_refs, row_scale)
     for start in range(0, columns, block):
         here = slice(start, start + block)
         total = None
@@ -333,12 +385,12 @@
         out[...] = mixed[pl.ds(first, share), :]
 
 
-def last_call(place, row_sums, plan, unit_protos, own, count, block, after=()):
+def last_call(place, plan, unit_protos, sums, own, count, block, after=()):
     rows = plan.shape[0]
     width = unit_protos.shape[0]
     share = own // count
     return call(
-        functools.partial(last_kernel, share, block),
+        functools.partial(last_kernel, share, len(sums), block),
         "last_sweep",
         [shape((share, width + LANES))] * count,
         [
@@ -348,7 +400,7 @@
         ],
         scalars=1,
         after=after,
-    )(place, row_sums, plan, unit_protos)
+    )(place, plan, unit_protos, *sums)
 
 
 def as_column(row):
@@ -361,13 +413,15 @@
 
 def code_kernel(*refs):
     parts, out = refs[:-1], refs[-1]
-    width = out.shape[1] - LANES
+    width = out.shape[1]
     total = tree_sum([part[...] for part in parts])
     store_code(out, total[:, :width], lane_sums(total[:, width:]))
 
 
 def code_call(parts, after=()):
-    return call(code_kernel, "code_mixed", shape(parts[0].shape, I16), after=after)(*parts)
+    rows, columns = parts[0].shape
+    out = shape((rows + ROW_TILE, columns - LANES), I16)
+    return call(code_kernel, "code_mixed", out, after=after)(*parts)
 
 
 def mean_kernel(*refs):
@@ -376,59 +430,84 @@
     out[...] = mixed / totals
 
 
-def mean_call(parts):
-    rows, columns = parts[0].shape
-    return call(mean_kernel, "mean_protos", shape((rows, columns - LANES)))(*parts)
-
-
-def finish_kernel(views, mean_count, crop_place, proto_place, feats, picked, weights, *refs):
-    parts, refs = refs[:mean_count], refs[mean_count:]
-    shares, (gradient, loss, means, expected, totals) = refs[:-5], refs[-5:]
-    rows = parts[0].shape[0]
-    for k, part in enumerate(parts):
-        first = pl.multiple_of(jnp.bitwise_xor(crop_place[0], k) * rows, rows)
-        means[pl.ds(first, rows), :] = part[...]
-    rows = shares[0].shape[0]
+def mean_call(parts, after=()):
+    rows, width = parts[0].shape
+    return call(mean_kernel, "mean_protos", shape((rows - ROW_TILE, width)), after=after)(*parts)
+
+
+FIELDS = 4
+
+
+def prepare_kernel(place, feats, picked, weights, *refs):
+    shares, (base, fields, expected, totals) = refs[:-4], refs[-4:]
+    rows = shares[0].shape[0] - ROW_TILE
     for k, part in enumerate(shares):
-        first = pl.multiple_of(jnp.bitwise_xor(proto_place[0], k) * rows, rows)
+        first = pl.multiple_of(jnp.bitwise_xor(place[0], k) * rows, rows)
         values, extra = decode(part)
         expected[pl.ds(first, rows), :] = values
         totals[pl.ds(first, rows), :] = jnp.broadcast_to(extra, (rows, LANES))
     images = feats.shape[1]
+    lane = lax.broadcasted_iota(jnp.int32, (images, LANES), 1)
     for crop in range(feats.shape[0]):
-        picked_column = as_column(picked[crop : crop + 1, :].astype(F32))
-        weight_column = as_column(weights[crop : crop + 1, :].astype(F32))
+        here = slice(crop * images, (crop + 1) * images)
         raw = feats[crop].astype(F32)
+        scales = lax.rsqrt(lane_sums(raw * raw) + epsilon)
+        factor = as_column(weights[crop : crop + 1, :].astype(F32)) * (scales * (1.0 / student_softness))
+        cubic = factor * scales * scales
+        mean = expected[here, :]
+        base[here, :] = factor * mean - (cubic * lane_sums(raw * mean)) * raw
+        logs = jnp.log(totals[here, :])
+        view = as_column(picked[crop : crop + 1, :].astype(F32))
+        fields[here, :] = jnp.where(
+            lane == 0, factor, jnp.where(lane == 1, cubic, jnp.where(lane == 2, scales, logs))
+        )
+        fields[here, :] = jnp.where(lane == FIELDS, view, fields[here, :])
+
+
+def prepare_call(place, feats, picked, weights, shares, after=()):
+    crops, images, width = feats.shape
+    rows = crops * images
+    return call(
+        prepare_kernel,
+        "prepare",
+        [shape((rows, width)), shape((rows, LANES))],
+        [pltpu.VMEM((rows, width), F32), pltpu.VMEM((rows, LANES), F32)],
+        scalars=1,
+        after=after,
+    )(place, feats, picked, weights, *shares)
+
+
+def finish_kernel(views, place, feats, base, fields, *refs):
+    parts, (gradient, loss, means) = refs[:-3], refs[-3:]
+    rows = parts[0].shape[0]
+    for k, part in enumerate(parts):
+        first = pl.multiple_of(jnp.bitwise_xor(place[0], k) * rows, rows)
+        means[pl.ds(first, rows), :] = part[...]
+    images = feats.shape[1]
+    for crop in range(feats.shape[0]):
+        here = slice(crop * images, (crop + 1) * images)
+        raw = feats[crop].astype(F32)
+        factor, cubic, scales = (fields[here, k : k + 1] for k in range(3))
+        view_column = fields[here, FIELDS : FIELDS + 1]
         chosen = means[:images, :]
         for view in range(1, views):
-            chosen = jnp.where(
-                picked_column == view, means[view * images : (view + 1) * images, :], chosen
-            )
-        here = slice(crop * images, (crop + 1) * images)
-        factor = weight_column * (1.0 / student_softness)
-        back_sum = factor * (expected[here, :] - chosen)
-        scales = lax.rsqrt(lane_sums(raw * raw) + epsilon)
-        along = lane_sums(raw * back_sum)
-        gradient[crop] = scales * back_sum - scales * scales * scales * raw * along
+            chosen = jnp.where(view_column == view, means[view * images : (view + 1) * images, :], chosen)
+        along = cubic * lane_sums(raw * chosen)
+        gradient[crop] = base[here, :] - factor * chosen + along * raw
         unit = (raw * scales).astype(BF16).astype(F32)
-        cross = lane_sums(unit * chosen) * (1.0 / student_softness)
-        column = jnp.log(totals[here, 0:1]) - cross
+        column = fields[here, FIELDS - 1 : FIELDS] - lane_sums(unit * chosen) * (1.0 / student_softness)
         loss[crop : crop + 1, :] = jnp.broadcast_to(column, (images, LANES)).T[:1, :]
 
 
-def finish_call(views, crop_place, proto_place, feats, picked, weights, means, shares):
+def finish_call(views, place, feats, base, fields, means):
     crops, images, width = feats.shape
     return call(
-        functools.partial(finish_kernel, views, len(means)),
+        functools.partial(finish_kernel, views),
         "finish",
         [shape((crops, images, width)), shape((crops, images))],
-        [
-            pltpu.VMEM((views * images, width), F32),
-            pltpu.VMEM((crops * images, width), F32),
-            pltpu.VMEM((crops * images, LANES), F32),
-        ],
-        scalars=2,
-    )(crop_place, proto_place, feats, picked, weights, *means, *shares)
+        [pltpu.VMEM((views * images, width), F32)],
+        scalars=1,
+    )(place, feats, base, fields, *means)
 
 
 def shards(teacher_feats, student_feats, teacher_protos, student_protos, pairing, row_weight):
@@ -439,36 +518,49 @@
     proto_devices = lax.axis_size("proto")
     crop_place = lax.axis_index("crop").reshape(1)
     proto_place = lax.axis_index("proto").reshape(1)
-    both = ("crop", "proto")
     block = 512
 
     teacher_parts = [teacher_feats] + [swap(teacher_feats, "image", k) for k in range(1, image_devices)]
     feats = student_feats.reshape(crops * images, width)
     protos = [student_protos] + [swap(student_protos, "crop", k) for k in range(1, crop_devices)]
 
-    pieces = proto_devices
-    if crops * images % (pieces * ROW_TILE):
-        pieces, proto_place = 1, jnp.zeros((1,), jnp.int32)
+    teacher_rows = image_devices * images * views
+    joint = crops * images % (proto_devices * ROW_TILE) == 0 and teacher_rows == width
+    pieces, copies = (proto_devices, 1) if joint else (1, crop_devices * proto_devices)
+    if not joint:
+        proto_place = jnp.zeros((1,), jnp.int32)
+
+    def from_all(shares):
+        return [shares[0]] + [swap(shares[k % len(shares)], "proto", k) for k in range(1, proto_devices)]
+
+    def exchange(sums, shares):
+        if joint:
+            parts = [sums] + [swap(sums, "crop", k) for k in range(1, crop_devices)]
+            return from_all(pack_call(parts, shares)), []
+        return from_all(shares), [lax.all_to_all(sums, ("crop", "proto"), 0, 0)]
+
     unit_protos, unit_teacher, unit_feats, back = own_call(
         crop_place, proto_place, feats, student_protos, teacher_protos, block
     )
-    coded = other_call(proto_place, unit_feats, back, protos[1:], pieces, block)
-    plan, sums = first_call(teacher_parts, unit_teacher, crop_devices * proto_devices, block)
-    shares = [coded[0]] + [swap(coded[k % pieces], "proto", k) for k in range(1, proto_devices)]
+    shares = other_call(proto_place, unit_feats, back, protos[1:], pieces, block)
+    plan, sums = first_call(teacher_parts, unit_teacher, copies, block)
     for _ in range(SWEEPS - 2):
-        sums, share, plan = sweep_call(lax.all_to_all(sums, both, 0, 0), plan, shares)
-    shares = [share] + [swap(share, "proto", k) for k in range(1, pieces)]
-    sums = lax.all_to_all(sums, both, 0, 0)
+        shares, row_sums = exchange(sums, shares)
+        sums, share, plan = sweep_call(plan, copies, shares, row_sums)
+        shares = [share]
+    if joint:
+        shares, row_sums = exchange(sums, shares)
+    else:
+        row_sums = [lax.all_to_all(sums, ("crop", "proto"), 0, 0)]
     mixed = last_call(
-        crop_place, sums, plan, unit_protos, views * images, crop_devices, block, after=shares[1:]
+        crop_place, plan, unit_protos, row_sums or shares, views * images, crop_devices, block
     )
 
-    mixed = code_call([mixed[0]] + [swap(mixed[k], "crop", k) for k in range(1, crop_devices)])
-    means = mean_call([mixed] + [swap(mixed, "proto", k) for k in range(1, proto_devices)])
+    coded = code_call([mixed[0]] + [swap(mixed[k], "crop", k) for k in range(1, crop_devices)])
+    base, fields = prepare_call(proto_place, student_feats, pairing, row_weight, shares, after=[coded])
+    means = mean_call(from_all([coded]), after=[base])
     means = [means] + [swap(means, "crop", k) for k in range(1, crop_devices)]
-    return finish_call(
-        views, crop_place, proto_place, student_feats, pairing, row_weight, means, shares
-    )
+    return finish_call(views, crop_place, student_feats, base, fields, means)
 
 
 def solution(mesh):

time: 61.8 us -> 59 us (0.955)
  blocking collectives: 18.6 us -> 0 us
  waiting for transfers between devices: 7.97 us -> 23.3 us
  Pallas kernels: 14.9 us -> 15.6 us
    all_to_all x2 -> x0, blocking collectives: 18.6 us -> none  [the longest x1 10.6 us: shards(): lax.all_to_all(sums, both, 0, 0)]
    ppermute x15 -> x17, waiting for transfers between devices: 7.97 us -> 23.3 us  [swap(): return lax.ppermute(values, axis, [(i, i ^ distance) for i in range(count)])]
    pallas_call x8 -> x11, Pallas kernels: 14.9 us -> 15.6 us  [run(): pl.pallas_call(body, in_specs=[IN_SMEM] * scalars + [IN_HBM if i in far e...]
    ppermute x15 -> x17, starting transfers between devices: 18.5 us -> 18.2 us  [swap(): return lax.ppermute(values, axis, [(i, i ^ distance) for i in range(count)])]
  transfers between devices with their start and end apart: 15 -> 17, of which waited for: 4 -> 10; matrix products, arithmetic and copies ran while one was open for 0% -> 0% of each run, Pallas kernels for 15% -> 18%
where the time goes in v4:
time: 59 us; the launch traced here: 58.9 us
  waiting for transfers between devices  23.3 us (39%)
  starting transfers between devices  18.2 us (31%)
  Pallas kernels  15.6 us (26%)
  local copies, waits for them, and re-layouts  0.97 us (2%)
  between operations  0.77 us (1%)
    ppermute x17, waiting for transfers between devices, swap(): return lax.ppermute(values, axis, [(i, i ^ distance) for i in range(count)])  23.3 us
    ppermute x17, starting transfers between devices, swap(): return lax.ppermute(values, axis, [(i, i ^ distance) for i in range(count)])  18.2 us
    pallas_call x11, Pallas kernels, run(): pl.pallas_call(body, in_specs=[IN_SMEM] * scalars + [IN_HBM if i in far e...  15.6 us
  transfers between devices with their start and end apart: 17, of which 10 were waited for; matrix products, arithmetic and copies ran while one was open for 0% of the time, Pallas kernels for 18%

profile of v4, /device:TPU:0, one launch (start us, length us, event | category | flops | bytes accessed | tf_op | source)
XLA Modules:
  0.0 58.9 jit_solution(16277093139527768921)
XLA Ops:
  0.6 0.5 collective-permute-start.4
  1.1 2.6 %collective-permute-start.1 = (bf16[64,2,512]{2,1,0:T(2,128)(2,1)}, bf16[64,2,512]{2,1,0:T(2,128)(2,1)S(1)}, u32[]{:S(2)}, u32[]{:S(2)}) collective-permute-start(bf16[64,2,512]{2,1,0:T(2,128)(2,1)} %refs_0_.1), channel_id=1, source_target_pairs={{0,16},{8,24},{16,0},{24,8},{1,17},{9,25},{17,1},{25,9},{2,18},{10... | collective-permute-start | bytes 393224 | tf_op jit(solution)/shard_map/ppermute | solution.py:174
  3.7 1.5 %collective-permute-start = (bf16[64,2,512]{2,1,0:T(2,128)(2,1)}, bf16[64,2,512]{2,1,0:T(2,128)(2,1)S(1)}, u32[]{:S(2)}, u32[]{:S(2)}) collective-permute-start(bf16[64,2,512]{2,1,0:T(2,128)(2,1)} %refs_0_.1), channel_id=1, source_target_pairs={{0,8},{8,0},{16,24},{24,16},{1,9},{9,1},{17,25},{25,17},{2,10},{10... | collective-permute-start | bytes 393224 | tf_op jit(solution)/shard_map/ppermute | solution.py:174
  5.3 0.9 %copy-done = bf16[4,64,512]{2,1,0:T(8,128)(2,1)S(1)} copy-done((bf16[4,64,512]{2,1,0:T(8,128)(2,1)S(1)}, bf16[4,64,512]{2,1,0:T(8,128)(2,1)}, u32[]{:S(2)}) %copy-start) | copy-done | bytes 262168
  6.2 4.2 %student_own.1 = (bf16[512,2048]{1,0:T(8,128)(2,1)S(1)}, bf16[512,2048]{1,0:T(8,128)(2,1)S(1)}, bf16[256,512]{1,0:T(8,128)(2,1)S(1)}, f32[256,640]{1,0:T(8,128)S(1)}) custom-call(s32[1]{0:T(128)} %bitcast.refs_0_, s32[1]{0:T(128)} %bitcast.1.refs_1_.refs_0_, bf16[256,512]{1,0:T(8,128)(2,1)S(1)} %bitcast.3, bf16[512,2048]{1,0:T(8,128)(2,1)} %refs_3_.2, ...), custom_call_target="tpu_custom_call" | custom-call | flops 1073741824 | tf_op jit(solution)/shard_map/student_own/pallas_call | solution.py:36
  10.5 1.5 %collective-permute-done.2.refs_3_ = bf16[64,2,512]{2,1,0:T(2,128)(2,1)S(1)} collective-permute-done((bf16[64,2,512]{2,1,0:T(2,128)(2,1)}, bf16[64,2,512]{2,1,0:T(2,128)(2,1)S(1)}, u32[]{:S(2)}, u32[]{:S(2)}) %collective-permute-start.2) | collective-permute-done | bytes 131104 | tf_op jit(solution)/shard_map/ppermute | solution.py:174
  12.1 2.4 %first_sweep.1 = (f32[512,2048]{1,0:T(8,128)S(1)}, f32[1,1,512]{2,1,0:T(1,128)S(1)}) custom-call(bf16[64,2,512]{2,1,0:T(2,128)(2,1)S(1)} %copy-done.1, bf16[64,2,512]{2,1,0:T(2,128)(2,1)S(1)} %collective-permute-done.refs_1_, bf16[64,2,512]{2,1,0:T(2,128)(2,1)S(1)} %collective-permute-done.1.refs_2_, bf16[64,2,512]{2,1,0:T(2,128)(2,1)S(1)} %collective-permute-done.2.refs_3_, ...), custom_call_target="tpu_custom_call" | custom-call | flops 4294967296 | tf_op jit(solution)/shard_map/first_sweep/pallas_call | solution.py:36
  14.5 0.1 collective-permute-start.3
  14.6 2.9 %student_other.1 = (s16[80,512]{1,0:T(8,128)(2,1)S(1)}, s16[80,512]{1,0:T(8,128)(2,1)S(1)}, s16[80,512]{1,0:T(8,128)(2,1)S(1)}, s16[80,512]{1,0:T(8,128)(2,1)S(1)}) custom-call(s32[1]{0:T(128)} %bitcast.1.refs_1_.refs_0_, bf16[256,512]{1,0:T(8,128)(2,1)S(1)} %get-tuple-element.26.refs_1_, f32[256,640]{1,0:T(8,128)S(1)} %get-tuple-element.27.refs_2_, ...), custom_call_target="tpu_custom_call" | custom-call | flops 1073741824 | tf_op jit(solution)/shard_map/student_other/pallas_call | solution.py:36
  17.5 1.9 %collective-permute-start.5 = (s16[80,512]{1,0:T(8,128)(2,1)S(1)}, s16[80,512]{1,0:T(8,128)(2,1)S(1)}, u32[]{:S(2)}, u32[]{:S(2)}) collective-permute-start(s16[80,512]{1,0:T(8,128)(2,1)S(1)} %get-tuple-element.33), channel_id=1, source_target_pairs={{0,1},{1,0},{2,3},{3,2},{4,5},{5,4},{6,7},{7,6},{8,9},{9,8},{10,11... | collective-permute-start | bytes 245768 | tf_op jit(solution)/shard_map/ppermute | solution.py:174
  19.4 2.6 %collective-permute-start.6 = (s16[80,512]{1,0:T(8,128)(2,1)S(1)}, s16[80,512]{1,0:T(8,128)(2,1)S(1)}, u32[]{:S(2)}, u32[]{:S(2)}) collective-permute-start(s16[80,512]{1,0:T(8,128)(2,1)S(1)} %get-tuple-element.34), channel_id=1, source_target_pairs={{0,2},{1,3},{2,0},{3,1},{4,6},{5,7},{6,4},{7,5},{8,10},{9,11},{10,... | collective-permute-start | bytes 245768 | tf_op jit(solution)/shard_map/ppermute | solution.py:174
  22.0 0.5 collective-permute-done.5.refs_2_
  22.5 6.4 %collective-permute-done.6.refs_3_ = s16[80,512]{1,0:T(8,128)(2,1)S(1)} collective-permute-done((s16[80,512]{1,0:T(8,128)(2,1)S(1)}, s16[80,512]{1,0:T(8,128)(2,1)S(1)}, u32[]{:S(2)}, u32[]{:S(2)}) %collective-permute-start.6) | collective-permute-done | bytes 81952 | tf_op jit(solution)/shard_map/ppermute | solution.py:174
  28.9 1.3 %sweep.1 = (f32[1,1,512]{2,1,0:T(1,128)S(1)}, s16[80,512]{1,0:T(8,128)(2,1)S(1)}, f32[512,2048]{1,0:T(8,128)S(1)}) custom-call(f32[512,2048]{1,0:T(8,128)S(1)} %get-tuple-element.24.refs_0_, s16[80,512]{1,0:T(8,128)(2,1)S(1)} %get-tuple-element.32.refs_1_, s16[80,512]{1,0:T(8,128)(2,1)S(1)} %collective-permute-done.5.refs_2_, ...), custom_call_target="tpu_custom_call", output_to_operand_aliasing={{2}: (0, {})} | custom-call | flops 1000000000 | tf_op jit(solution)/shard_map/sweep/pallas_call | solution.py:36
  30.2 1.1 %collective-permute-done.8.refs_1_ = f32[1,1,512]{2,1,0:T(1,128)S(1)} collective-permute-done((f32[1,1,512]{2,1,0:T(1,128)S(1)}, f32[1,1,512]{2,1,0:T(1,128)S(1)}, u32[]{:S(2)}, u32[]{:S(2)}) %collective-permute-start.8) | collective-permute-done | bytes 2080 | tf_op jit(solution)/shard_map/ppermute | solution.py:174
  31.4 2.7 %collective-permute-start.11 = (s16[80,512]{1,0:T(8,128)(2,1)S(1)}, s16[80,512]{1,0:T(8,128)(2,1)S(1)}, u32[]{:S(2)}, u32[]{:S(2)}) collective-permute-start(s16[80,512]{1,0:T(8,128)(2,1)S(1)} %pack_sums.3.refs_3_.refs_4_), channel_id=1, source_target_pairs={{0,3},{1,2},{2,1},{3,0},{4,7},{5,6},{6,5},{7,4},{8,11},{9,10},{10,... | collective-permute-start | bytes 245768 | tf_op jit(solution)/shard_map/ppermute | solution.py:174
  34.2 0.5 collective-permute-start.10
  34.7 1.2 %collective-permute-start.9 = (s16[80,512]{1,0:T(8,128)(2,1)S(1)}, s16[80,512]{1,0:T(8,128)(2,1)S(1)}, u32[]{:S(2)}, u32[]{:S(2)}) collective-permute-start(s16[80,512]{1,0:T(8,128)(2,1)S(1)} %pack_sums.3.refs_3_.refs_4_), channel_id=1, source_target_pairs={{0,1},{1,0},{2,3},{3,2},{4,5},{5,4},{6,7},{7,6},{8,9},{9,8},{10,11... | collective-permute-start | bytes 245768 | tf_op jit(solution)/shard_map/ppermute | solution.py:174
  35.9 2.2 %collective-permute-done.11.refs_6_.refs_7_ = s16[80,512]{1,0:T(8,128)(2,1)S(1)} collective-permute-done((s16[80,512]{1,0:T(8,128)(2,1)S(1)}, s16[80,512]{1,0:T(8,128)(2,1)S(1)}, u32[]{:S(2)}, u32[]{:S(2)}) %collective-permute-start.11) | collective-permute-done | bytes 81952 | tf_op jit(solution)/shard_map/ppermute | solution.py:174
  38.1 4.3 %collective-permute-done.10.refs_5_.refs_6_ = s16[80,512]{1,0:T(8,128)(2,1)S(1)} collective-permute-done((s16[80,512]{1,0:T(8,128)(2,1)S(1)}, s16[80,512]{1,0:T(8,128)(2,1)S(1)}, u32[]{:S(2)}, u32[]{:S(2)}) %collective-permute-start.10) | collective-permute-done | bytes 81952 | tf_op jit(solution)/shard_map/ppermute | solution.py:174
  42.5 1.3 %last_sweep.1 = (f32[64,640]{1,0:T(8,128)S(1)}, f32[64,640]{1,0:T(8,128)S(1)}) custom-call(s32[1]{0:T(128)} %bitcast.refs_0_, f32[512,2048]{1,0:T(8,128)S(1)} %get-tuple-element.38.refs_1_, bf16[512,2048]{1,0:T(8,128)(2,1)S(1)} %get-tuple-element.39.refs_2_, s16[80,512]{1,0:T(8,128)(2,1)S(1)} %pack_sums.3.refs_3_.refs_4_, ...), custom_call_target="tpu_custom_call" | custom-call | flops 1000000000 | tf_op jit(solution)/shard_map/last_sweep/pallas_call | solution.py:36
  43.9 1.4 %collective-permute-done.12.refs_1_ = f32[64,640]{1,0:T(8,128)S(1)} collective-permute-done((f32[64,640]{1,0:T(8,128)S(1)}, f32[64,640]{1,0:T(8,128)S(1)}, u32[]{:S(2)}, u32[]{:S(2)}) %collective-permute-start.12) | collective-permute-done | bytes 163872 | tf_op jit(solution)/shard_map/ppermute | solution.py:174
  45.3 0.2 code_mixed.1.refs_8_.refs_0_
  45.5 2.5 %collective-permute-start.15 = (s16[80,512]{1,0:T(8,128)(2,1)S(1)}, s16[80,512]{1,0:T(8,128)(2,1)S(1)}, u32[]{:S(2)}, u32[]{:S(2)}) collective-permute-start(s16[80,512]{1,0:T(8,128)(2,1)S(1)} %code_mixed.1.refs_8_.refs_0_), channel_id=1, source_target_pairs={{0,3},{1,2},{2,1},{3,0},{4,7},{5,6},{6,5},{7,4},{8,11},{9,10},{10,... | collective-permute-start | bytes 245768 | tf_op jit(solution)/shard_map/ppermute | solution.py:174
  48.0 1.9 %collective-permute-start.13 = (s16[80,512]{1,0:T(8,128)(2,1)S(1)}, s16[80,512]{1,0:T(8,128)(2,1)S(1)}, u32[]{:S(2)}, u32[]{:S(2)}) collective-permute-start(s16[80,512]{1,0:T(8,128)(2,1)S(1)} %code_mixed.1.refs_8_.refs_0_), channel_id=1, source_target_pairs={{0,1},{1,0},{2,3},{3,2},{4,5},{5,4},{6,7},{7,6},{8,9},{9,8},{10,11... | collective-permute-start | bytes 245768 | tf_op jit(solution)/shard_map/ppermute | solution.py:174
  49.9 1.0 %prepare.1 = (f32[256,512]{1,0:T(8,128)S(1)}, f32[256,128]{1,0:T(8,128)S(1)}) custom-call(s32[1]{0:T(128)} %bitcast.1.refs_1_.refs_0_, bf16[4,64,512]{2,1,0:T(8,128)(2,1)S(1)} %copy-done, s32[4,64]{1,0:T(4,128)S(1)} %copy-done.2, bf16[4,64]{1,0:T(4,128)(2,1)S(1)} %copy-done.3, s16[80,512]{1,0:T(8,128)(2,1)S(1)} %pack_sums.3.refs_3_.refs_4_, ...), custom_call_target="tpu_custom_call" | custom-call | flops 1000000000 | tf_op jit(solution)/shard_map/prepare/pallas_call | solution.py:36
  51.0 1.8 %collective-permute-done.15.refs_3_ = s16[80,512]{1,0:T(8,128)(2,1)S(1)} collective-permute-done((s16[80,512]{1,0:T(8,128)(2,1)S(1)}, s16[80,512]{1,0:T(8,128)(2,1)S(1)}, u32[]{:S(2)}, u32[]{:S(2)}) %collective-permute-start.15) | collective-permute-done | bytes 81952 | tf_op jit(solution)/shard_map/ppermute | solution.py:174
  52.7 2.6 %collective-permute-done.14.refs_2_ = s16[80,512]{1,0:T(8,128)(2,1)S(1)} collective-permute-done((s16[80,512]{1,0:T(8,128)(2,1)S(1)}, s16[80,512]{1,0:T(8,128)(2,1)S(1)}, u32[]{:S(2)}, u32[]{:S(2)}) %collective-permute-start.14) | collective-permute-done | bytes 81952 | tf_op jit(solution)/shard_map/ppermute | solution.py:174
  55.3 0.4 mean_protos.1.refs_4_
  55.7 0.1 collective-permute-start.16
  55.8 1.3 %collective-permute-done.16.refs_5_ = f32[64,512]{1,0:T(8,128)S(1)} collective-permute-done((f32[64,512]{1,0:T(8,128)S(1)}, f32[64,512]{1,0:T(8,128)S(1)}, u32[]{:S(2)}, u32[]{:S(2)}) %collective-permute-start.16) | collective-permute-done | bytes 131104 | tf_op jit(solution)/shard_map/ppermute | solution.py:174
  57.1 1.7 %finish.1 = (f32[4,64,512]{2,1,0:T(8,128)}, f32[4,64]{1,0:T(4,128)}) custom-call(s32[1]{0:T(128)} %bitcast.refs_0_, bf16[4,64,512]{2,1,0:T(8,128)(2,1)S(1)} %copy-done, f32[256,512]{1,0:T(8,128)S(1)} %get-tuple-element.42.refs_4_.refs_2_, f32[256,128]{1,0:T(8,128)S(1)} %get-tuple-element.43.refs_3_, f32[64,512]{1,0:T(8,128)S(1)} %mean_protos.1.refs_4_, ...), custom_call_target="tpu_custom_call" | custom-call | flops 1000000000 | tf_op jit(solution)/shard_map/finish/pallas_call | solution.py:36
  (21 shorter events, 0.3 us)
Async XLA Ops:
  0.6 13.9 %collective-permute-start.4 = (bf16[512,2048]{1,0:T(8,128)(2,1)}, bf16[512,2048]{1,0:T(8,128)(2,1)S(1)}, u32[]{:S(2)}, u32[]{:S(2)}) collective-permute-start(bf16[512,2048]{1,0:T(8,128)(2,1)} %refs_3_.2), channel_id=1, source_target_pairs={{0,4},{4,0},{1,5},{5,1},{2,6},{6,2},{3,7},{7,3},{8,12},{12,8},{9,1... | collective-permute-start | bytes 6291464 | tf_op jit(solution)/shard_map/ppermute | solution.py:174
  1.1 9.3 %collective-permute-start.1 = (bf16[64,2,512]{2,1,0:T(2,128)(2,1)}, bf16[64,2,512]{2,1,0:T(2,128)(2,1)S(1)}, u32[]{:S(2)}, u32[]{:S(2)}) collective-permute-start(bf16[64,2,512]{2,1,0:T(2,128)(2,1)} %refs_0_.1), channel_id=1, source_target_pairs={{0,16},{8,24},{16,0},{24,8},{1,17},{9,25},{17,1},{25,9},{2,18},{10... | collective-permute-start | bytes 393224 | tf_op jit(solution)/shard_map/ppermute | solution.py:174
  3.7 6.8 %collective-permute-start = (bf16[64,2,512]{2,1,0:T(2,128)(2,1)}, bf16[64,2,512]{2,1,0:T(2,128)(2,1)S(1)}, u32[]{:S(2)}, u32[]{:S(2)}) collective-permute-start(bf16[64,2,512]{2,1,0:T(2,128)(2,1)} %refs_0_.1), channel_id=1, source_target_pairs={{0,8},{8,0},{16,24},{24,16},{1,9},{9,1},{17,25},{25,17},{2,10},{10... | collective-permute-start | bytes 393224 | tf_op jit(solution)/shard_map/ppermute | solution.py:174
  5.2 6.8 %collective-permute-start.2 = (bf16[64,2,512]{2,1,0:T(2,128)(2,1)}, bf16[64,2,512]{2,1,0:T(2,128)(2,1)S(1)}, u32[]{:S(2)}, u32[]{:S(2)}) collective-permute-start(bf16[64,2,512]{2,1,0:T(2,128)(2,1)} %refs_0_.1), channel_id=1, source_target_pairs={{0,24},{8,16},{16,8},{24,0},{1,25},{9,17},{17,9},{25,1},{2,26},{10... | collective-permute-start | bytes 393224 | tf_op jit(solution)/shard_map/ppermute | solution.py:174
  5.3 0.9 %copy-start = (bf16[4,64,512]{2,1,0:T(8,128)(2,1)S(1)}, bf16[4,64,512]{2,1,0:T(8,128)(2,1)}, u32[]{:S(2)}) copy-start(bf16[4,64,512]{2,1,0:T(8,128)(2,1)} %refs_1_.3) | copy-start | bytes 786436
  6.2 5.8 %copy-start.1 = (bf16[64,2,512]{2,1,0:T(2,128)(2,1)S(1)}, bf16[64,2,512]{2,1,0:T(2,128)(2,1)}, u32[]{:S(2)}) copy-start(bf16[64,2,512]{2,1,0:T(2,128)(2,1)} %refs_0_.1) | copy-start | bytes 393220
  14.5 3.0 %collective-permute-start.3 = (f32[1,1,512]{2,1,0:T(1,128)S(1)}, f32[1,1,512]{2,1,0:T(1,128)S(1)}, u32[]{:S(2)}, u32[]{:S(2)}) collective-permute-start(f32[1,1,512]{2,1,0:T(1,128)S(1)} %get-tuple-element.25.refs_0_), channel_id=1, source_target_pairs={{0,4},{4,0},{1,5},{5,1},{2,6},{6,2},{3,7},{7,3},{8,12},{12,8},{9,1... | collective-permute-start | bytes 6152 | tf_op jit(solution)/shard_map/ppermute | solution.py:174
  17.5 4.9 %collective-permute-start.5 = (s16[80,512]{1,0:T(8,128)(2,1)S(1)}, s16[80,512]{1,0:T(8,128)(2,1)S(1)}, u32[]{:S(2)}, u32[]{:S(2)}) collective-permute-start(s16[80,512]{1,0:T(8,128)(2,1)S(1)} %get-tuple-element.33), channel_id=1, source_target_pairs={{0,1},{1,0},{2,3},{3,2},{4,5},{5,4},{6,7},{7,6},{8,9},{9,8},{10,11... | collective-permute-start | bytes 245768 | tf_op jit(solution)/shard_map/ppermute | solution.py:174
  19.4 9.5 %collective-permute-start.6 = (s16[80,512]{1,0:T(8,128)(2,1)S(1)}, s16[80,512]{1,0:T(8,128)(2,1)S(1)}, u32[]{:S(2)}, u32[]{:S(2)}) collective-permute-start(s16[80,512]{1,0:T(8,128)(2,1)S(1)} %get-tuple-element.34), channel_id=1, source_target_pairs={{0,2},{1,3},{2,0},{3,1},{4,6},{5,7},{6,4},{7,5},{8,10},{9,11},{10,... | collective-permute-start | bytes 245768 | tf_op jit(solution)/shard_map/ppermute | solution.py:174
  22.0 7.0 %collective-permute-start.7 = (s16[80,512]{1,0:T(8,128)(2,1)S(1)}, s16[80,512]{1,0:T(8,128)(2,1)S(1)}, u32[]{:S(2)}, u32[]{:S(2)}) collective-permute-start(s16[80,512]{1,0:T(8,128)(2,1)S(1)} %get-tuple-element.35), channel_id=1, source_target_pairs={{0,3},{1,2},{2,1},{3,0},{4,7},{5,6},{6,5},{7,4},{8,11},{9,10},{10,... | collective-permute-start | bytes 245768 | tf_op jit(solution)/shard_map/ppermute | solution.py:174
  30.2 1.2 %collective-permute-start.8 = (f32[1,1,512]{2,1,0:T(1,128)S(1)}, f32[1,1,512]{2,1,0:T(1,128)S(1)}, u32[]{:S(2)}, u32[]{:S(2)}) collective-permute-start(f32[1,1,512]{2,1,0:T(1,128)S(1)} %get-tuple-element.36.refs_0_), channel_id=1, source_target_pairs={{0,4},{4,0},{1,5},{5,1},{2,6},{6,2},{3,7},{7,3},{8,12},{12,8},{9,1... | collective-permute-start | bytes 6152 | tf_op jit(solution)/shard_map/ppermute | solution.py:174
  31.4 6.7 %collective-permute-start.11 = (s16[80,512]{1,0:T(8,128)(2,1)S(1)}, s16[80,512]{1,0:T(8,128)(2,1)S(1)}, u32[]{:S(2)}, u32[]{:S(2)}) collective-permute-start(s16[80,512]{1,0:T(8,128)(2,1)S(1)} %pack_sums.3.refs_3_.refs_4_), channel_id=1, source_target_pairs={{0,3},{1,2},{2,1},{3,0},{4,7},{5,6},{6,5},{7,4},{8,11},{9,10},{10,... | collective-permute-start | bytes 245768 | tf_op jit(solution)/shard_map/ppermute | solution.py:174
  34.2 8.3 %collective-permute-start.10 = (s16[80,512]{1,0:T(8,128)(2,1)S(1)}, s16[80,512]{1,0:T(8,128)(2,1)S(1)}, u32[]{:S(2)}, u32[]{:S(2)}) collective-permute-start(s16[80,512]{1,0:T(8,128)(2,1)S(1)} %pack_sums.3.refs_3_.refs_4_), channel_id=1, source_target_pairs={{0,2},{1,3},{2,0},{3,1},{4,6},{5,7},{6,4},{7,5},{8,10},{9,11},{10,... | collective-permute-start | bytes 245768 | tf_op jit(solution)/shard_map/ppermute | solution.py:174
  34.7 7.8 %collective-permute-start.9 = (s16[80,512]{1,0:T(8,128)(2,1)S(1)}, s16[80,512]{1,0:T(8,128)(2,1)S(1)}, u32[]{:S(2)}, u32[]{:S(2)}) collective-permute-start(s16[80,512]{1,0:T(8,128)(2,1)S(1)} %pack_sums.3.refs_3_.refs_4_), channel_id=1, source_target_pairs={{0,1},{1,0},{2,3},{3,2},{4,5},{5,4},{6,7},{7,6},{8,9},{9,8},{10,11... | collective-permute-start | bytes 245768 | tf_op jit(solution)/shard_map/ppermute | solution.py:174
  43.8 6.1 %copy-start.2 = (s32[4,64]{1,0:T(4,128)S(1)}, s32[4,64]{1,0:T(4,128)}, u32[]{:S(2)}) copy-start(s32[4,64]{1,0:T(4,128)} %refs_2_.1) | copy-start | bytes 3076
  43.8 6.1 %copy-start.3 = (bf16[4,64]{1,0:T(4,128)(2,1)S(1)}, bf16[4,64]{1,0:T(4,128)(2,1)}, u32[]{:S(2)}) copy-start(bf16[4,64]{1,0:T(4,128)(2,1)} %refs_3_.3) | copy-start | bytes 1540
  43.8 1.5 %collective-permute-start.12 = (f32[64,640]{1,0:T(8,128)S(1)}, f32[64,640]{1,0:T(8,128)S(1)}, u32[]{:S(2)}, u32[]{:S(2)}) collective-permute-start(f32[64,640]{1,0:T(8,128)S(1)} %get-tuple-element.41), channel_id=1, source_target_pairs={{0,4},{4,0},{1,5},{5,1},{2,6},{6,2},{3,7},{7,3},{8,12},{12,8},{9,1... | collective-permute-start | bytes 491528 | tf_op jit(solution)/shard_map/ppermute | solution.py:174
  45.5 7.2 %collective-permute-start.15 = (s16[80,512]{1,0:T(8,128)(2,1)S(1)}, s16[80,512]{1,0:T(8,128)(2,1)S(1)}, u32[]{:S(2)}, u32[]{:S(2)}) collective-permute-start(s16[80,512]{1,0:T(8,128)(2,1)S(1)} %code_mixed.1.refs_8_.refs_0_), channel_id=1, source_target_pairs={{0,3},{1,2},{2,1},{3,0},{4,7},{5,6},{6,5},{7,4},{8,11},{9,10},{10,... | collective-permute-start | bytes 245768 | tf_op jit(solution)/shard_map/ppermute | solution.py:174
  48.0 7.3 %collective-permute-start.14 = (s16[80,512]{1,0:T(8,128)(2,1)S(1)}, s16[80,512]{1,0:T(8,128)(2,1)S(1)}, u32[]{:S(2)}, u32[]{:S(2)}) collective-permute-start(s16[80,512]{1,0:T(8,128)(2,1)S(1)} %code_mixed.1.refs_8_.refs_0_), channel_id=1, source_target_pairs={{0,2},{1,3},{2,0},{3,1},{4,6},{5,7},{6,4},{7,5},{8,10},{9,11},{10,... | collective-permute-start | bytes 245768 | tf_op jit(solution)/shard_map/ppermute | solution.py:174
  48.0 7.3 %collective-permute-start.13 = (s16[80,512]{1,0:T(8,128)(2,1)S(1)}, s16[80,512]{1,0:T(8,128)(2,1)S(1)}, u32[]{:S(2)}, u32[]{:S(2)}) collective-permute-start(s16[80,512]{1,0:T(8,128)(2,1)S(1)} %code_mixed.1.refs_8_.refs_0_), channel_id=1, source_target_pairs={{0,1},{1,0},{2,3},{3,2},{4,5},{5,4},{6,7},{7,6},{8,9},{9,8},{10,11... | collective-permute-start | bytes 245768 | tf_op jit(solution)/shard_map/ppermute | solution.py:174
  55.7 1.4 %collective-permute-start.16 = (f32[64,512]{1,0:T(8,128)S(1)}, f32[64,512]{1,0:T(8,128)S(1)}, u32[]{:S(2)}, u32[]{:S(2)}) collective-permute-start(f32[64,512]{1,0:T(8,128)S(1)} %mean_protos.1.refs_4_), channel_id=1, source_target_pairs={{0,4},{4,0},{1,5},{5,1},{2,6},{6,2},{3,7},{7,3},{8,12},{12,8},{9,1... | collective-permute-start | bytes 393224 | tf_op jit(solution)/shard_map/ppermute | solution.py:174

commit v5 on v4

--- a/solution.py
+++ b/solution.py
@@ -7,7 +7,6 @@
 from jax.experimental.pallas import tpu as pltpu
 from jax.sharding import PartitionSpec as P
 
-SWEEPS = 3
 LANES = 128
 ROW_TILE = 16
 LEVELS = 32767.0
@@ -131,42 +130,39 @@
     return tree_sum([p[0] for p in pairs]), tree_sum([p[1] for p in pairs])
 
 
-SUMS_AT = 4
-
-
-def pack_kernel(count, *refs):
-    parts, refs = refs[:count], refs[count:]
-    shares, outs = refs[: len(refs) // 2], refs[len(refs) // 2 :]
-    power, high, low = split_positive(tree_sum([part[0] for part in parts]))
-    for share, out in zip(shares, outs):
-        rows = share.shape[0] - ROW_TILE
-        out[:rows, :] = share[:rows, :]
-        at = lax.broadcasted_iota(jnp.int32, (ROW_TILE, share.shape[1]), 0)
-        under = to_f32(share[rows:, :])
-        for k, row in enumerate((power, high, low)):
-            under = jnp.where(at == SUMS_AT + k, row, under)
-        out[rows:, :] = to_i16(under)
-
-
-def pack_call(parts, shares):
-    return call(
-        functools.partial(pack_kernel, len(parts)),
-        "pack_sums",
-        [shape(share.shape, I16) for share in shares],
+def join_kernel(count, at, *refs):
+    refs[at][...] = tree_sum([part[...] for part in refs[:count]])
+
+
+def join_call(parts, shares):
+    count = len(parts)
+    out = call(
+        functools.partial(join_kernel, count, count + len(shares)),
+        "join_sums",
+        [shape(parts[0].shape)] + [shape(share.shape, I16) for share in shares],
+        aliases={count + i: 1 + i for i in range(len(shares))},
     )(*parts, *shares)
+    return out[0], out[1:]
+
+
+def join_kernel(count, at, *refs):
+    refs[at][...] = tree_sum([part[...] for part in refs[:count]])
+
+
+def join_call(parts, shares):
+    count = len(parts)
+    out = call(
+        functools.partial(join_kernel, count, count + len(shares)),
+        "join_sums",
+        [shape(parts[0].shape)] + [shape(share.shape, I16) for share in shares],
+        aliases={count + i: 1 + i for i in range(len(shares))},
+    )(*parts, *shares)
+    return out[0], out[1:]
 
 
 def read_sums(refs):
-    if refs[0].dtype == I16:
-        terms = []
-        for ref in refs:
-            under = to_f32(ref[ref.shape[0] - ROW_TILE :, :])
-            terms.append(join_positive(*(under[SUMS_AT + k : SUMS_AT + k + 1, :] for k in range(3))))
-        return tree_sum(terms)
-    total = refs[0][0]
-    for k in range(1, refs[0].shape[0]):
-        total = total + refs[0][k]
-    return total
+    terms = [ref[k] for ref in refs for k in range(ref.shape[0])]
+    return tree_sum(terms)
 
 
 def swap(values, axis, distance):
@@ -334,9 +330,8 @@
     return 1.0 / jnp.sum(weighted, axis=0, keepdims=True)
 
 
-def sweep_kernel(count, plan, *refs):
-    shares, refs = refs[:count], refs[count:]
-    sum_refs, (sums, share, _, row_scale, partial) = refs[:-5] or shares, refs[-5:]
+def sweep_kernel(plan, *refs):
+    sum_refs, (sums, _, row_scale, partial) = refs[:-4], refs[-4:]
     scale_rows(sum_refs, row_scale)
     for start in range(0, plan.shape[1], LANES):
         terms = plan[:, start : start + LANES] * column_scale(plan, row_scale, start)
@@ -345,19 +340,28 @@
         else:
             partial[...] += terms
     store_sums(sums, partial)
+
+
+def sweep_call(plan, copies, row_sums):
+    rows = plan.shape[0]
+    return call(
+        sweep_kernel,
+        "sweep",
+        [shape((copies, 1, rows)), shape(plan.shape)],
+        [pltpu.VMEM((rows, LANES), F32)] * 2,
+        aliases={0: 1},
+        flops=10**10,
+    )(plan, *row_sums)
+
+
+def total_kernel(*refs):
+    shares, share = refs[:-1], refs[-1]
     back, totals = decode_sum(shares)
     store_code(share, back / totals, totals)
 
 
-def sweep_call(plan, copies, shares, row_sums):
-    rows = plan.shape[0]
-    return call(
-        functools.partial(sweep_kernel, len(shares)),
-        "sweep",
-        [shape((copies, 1, rows)), shape(shares[0].shape, I16), shape(plan.shape)],
-        [pltpu.VMEM((rows, LANES), F32)] * 2,
-        aliases={0: 2},
-    )(plan, *shares, *row_sums)
+def total_call(shares, after=()):
+    return call(total_kernel, "student_totals", shape(shares[0].shape, I16), after=after, flops=10**6)(*shares)
 
 
 def last_kernel(share, count, block, place, plan, unit_protos, *refs):
@@ -400,6 +404,7 @@
         ],
         scalars=1,
         after=after,
+        flops=10**10,
     )(place, plan, unit_protos, *sums)
 
 
@@ -422,6 +427,17 @@
     rows, columns = parts[0].shape
     out = shape((rows + ROW_TILE, columns - LANES), I16)
     return call(code_kernel, "code_mixed", out, after=after)(*parts)
+
+
+def gate_call(arrays, after):
+    out = call(
+        lambda *refs: None,
+        "gate",
+        [shape(array.shape, array.dtype) for array in arrays],
+        after=after,
+        aliases={i: i for i in range(len(arrays))},
+    )(*arrays)
+    return list(out)
 
 
 def mean_kernel(*refs):
@@ -524,37 +540,41 @@
     feats = student_feats.reshape(crops * images, width)
     protos = [student_protos] + [swap(student_protos, "crop", k) for k in range(1, crop_devices)]
 
-    teacher_rows = image_devices * images * views
-    joint = crops * images % (proto_devices * ROW_TILE) == 0 and teacher_rows == width
-    pieces, copies = (proto_devices, 1) if joint else (1, crop_devices * proto_devices)
-    if not joint:
-        proto_place = jnp.zeros((1,), jnp.int32)
+    pieces = proto_devices
+    if crops * images % (proto_devices * ROW_TILE):
+        pieces, proto_place = 1, jnp.zeros((1,), jnp.int32)
+    few = crop_devices * proto_devices <= 8
+    copies = 1 if few else crop_devices * proto_devices
 
     def from_all(shares):
         return [shares[0]] + [swap(shares[k % len(shares)], "proto", k) for k in range(1, proto_devices)]
 
     def exchange(sums, shares):
-        if joint:
-            parts = [sums] + [swap(sums, "crop", k) for k in range(1, crop_devices)]
-            return from_all(pack_call(parts, shares)), []
-        return from_all(shares), [lax.all_to_all(sums, ("crop", "proto"), 0, 0)]
+        if not few:
+            return [lax.all_to_all(sums, ("crop", "proto"), 0, 0)], shares
+        total, shares = join_call([sums] + [swap(sums, "crop", k) for k in range(1, crop_devices)], shares)
+        return from_all([total]), shares
 
     unit_protos, unit_teacher, unit_feats, back = own_call(
         crop_place, proto_place, feats, student_protos, teacher_protos, block
     )
     shares = other_call(proto_place, unit_feats, back, protos[1:], pieces, block)
     plan, sums = first_call(teacher_parts, unit_teacher, copies, block)
-    for _ in range(SWEEPS - 2):
-        shares, row_sums = exchange(sums, shares)
-        sums, share, plan = sweep_call(plan, copies, shares, row_sums)
-        shares = [share]
-    if joint:
-        shares, row_sums = exchange(sums, shares)
-    else:
-        row_sums = [lax.all_to_all(sums, ("crop", "proto"), 0, 0)]
+    row_sums, shares = exchange(sums, shares)
+    shares = from_all(shares)
+    sums, plan = sweep_call(plan, copies, row_sums)
+    row_sums, shares = exchange(sums, [total_call(shares, after=[sums])])
+    shares = [shares[0]] + [swap(shares[0], "proto", k) for k in range(1, pieces)]
     mixed = last_call(
-        crop_place, plan, unit_protos, row_sums or shares, views * images, crop_devices, block
+        crop_place,
+        plan,
+        unit_protos,
+        row_sums,
+        views * images,
+        crop_devices,
+        block,
     )
+    mixed = [mixed[0]] + gate_call(mixed[1:], shares[1:])
 
     coded = code_call([mixed[0]] + [swap(mixed[k], "crop", k) for k in range(1, crop_devices)])
     base, fields = prepare_call(proto_place, student_feats, pairing, row_weight, shares, after=[coded])

time: 59 us -> 61 us (1.034)
  starting transfers between devices: 18.2 us -> 27.6 us
  waiting for transfers between devices: 23.3 us -> 15.8 us
    ppermute x17 -> x23, starting transfers between devices: 18.2 us -> 27.6 us  [swap(): return lax.ppermute(values, axis, [(i, i ^ distance) for i in range(count)])]
    ppermute x17 -> x23, waiting for transfers between devices: 23.3 us -> 15.8 us  [swap(): return lax.ppermute(values, axis, [(i, i ^ distance) for i in range(count)])]
    pallas_call x11 -> x13, Pallas kernels: 15.6 us -> 15.7 us  [run(): pl.pallas_call(body, in_specs=[IN_SMEM] * scalars + [IN_HBM if i in far e...]
  transfers between devices with their start and end apart: 17 -> 23, of which waited for: 10 -> 8; matrix products, arithmetic and copies ran while one was open for 0% -> 0% of each run, Pallas kernels for 18% -> 22%
where the time goes in v5:
time: 61 us; the launch traced here: 60.8 us
  starting transfers between devices  27.6 us (45%)
  waiting for transfers between devices  15.8 us (26%)
  Pallas kernels  15.7 us (26%)
  local copies, waits for them, and re-layouts  0.96 us (2%)
  between operations  0.78 us (1%)
    ppermute x23, starting transfers between devices, swap(): return lax.ppermute(values, axis, [(i, i ^ distance) for i in range(count)])  27.6 us
    ppermute x23, waiting for transfers between devices, swap(): return lax.ppermute(values, axis, [(i, i ^ distance) for i in range(count)])  15.8 us
    pallas_call x13, Pallas kernels, run(): pl.pallas_call(body, in_specs=[IN_SMEM] * scalars + [IN_HBM if i in far e...  15.7 us
  transfers between devices with their start and end apart: 23, of which 8 were waited for; matrix products, arithmetic and copies ran while one was open for 0% of the time, Pallas kernels for 22%

profile of v5, /device:TPU:0, one launch (start us, length us, event | category | flops | bytes accessed | tf_op | source)
XLA Modules:
  0.0 60.8 jit_solution(6368901368937548549)
XLA Ops:
  0.6 0.5 collective-permute-start.4
  1.1 2.6 %collective-permute-start.1 = (bf16[64,2,512]{2,1,0:T(2,128)(2,1)}, bf16[64,2,512]{2,1,0:T(2,128)(2,1)S(1)}, u32[]{:S(2)}, u32[]{:S(2)}) collective-permute-start(bf16[64,2,512]{2,1,0:T(2,128)(2,1)} %refs_0_.1), channel_id=1, source_target_pairs={{0,16},{8,24},{16,0},{24,8},{1,17},{9,25},{17,1},{25,9},{2,18},{10... | collective-permute-start | bytes 393224 | tf_op jit(solution)/shard_map/ppermute | solution.py:170
  3.7 1.5 %collective-permute-start = (bf16[64,2,512]{2,1,0:T(2,128)(2,1)}, bf16[64,2,512]{2,1,0:T(2,128)(2,1)S(1)}, u32[]{:S(2)}, u32[]{:S(2)}) collective-permute-start(bf16[64,2,512]{2,1,0:T(2,128)(2,1)} %refs_0_.1), channel_id=1, source_target_pairs={{0,8},{8,0},{16,24},{24,16},{1,9},{9,1},{17,25},{25,17},{2,10},{10... | collective-permute-start | bytes 393224 | tf_op jit(solution)/shard_map/ppermute | solution.py:170
  5.3 0.9 %copy-done = bf16[4,64,512]{2,1,0:T(8,128)(2,1)S(1)} copy-done((bf16[4,64,512]{2,1,0:T(8,128)(2,1)S(1)}, bf16[4,64,512]{2,1,0:T(8,128)(2,1)}, u32[]{:S(2)}) %copy-start) | copy-done | bytes 262168
  6.2 4.2 %student_own.1 = (bf16[512,2048]{1,0:T(8,128)(2,1)S(1)}, bf16[512,2048]{1,0:T(8,128)(2,1)S(1)}, bf16[256,512]{1,0:T(8,128)(2,1)S(1)}, f32[256,640]{1,0:T(8,128)S(1)}) custom-call(s32[1]{0:T(128)} %bitcast.refs_0_, s32[1]{0:T(128)} %bitcast.1.refs_1_.refs_0_, bf16[256,512]{1,0:T(8,128)(2,1)S(1)} %bitcast.3, bf16[512,2048]{1,0:T(8,128)(2,1)} %refs_3_.2, ...), custom_call_target="tpu_custom_call" | custom-call | flops 1073741824 | tf_op jit(solution)/shard_map/student_own/pallas_call | solution.py:35
  10.5 1.5 %collective-permute-done.2.refs_3_ = bf16[64,2,512]{2,1,0:T(2,128)(2,1)S(1)} collective-permute-done((bf16[64,2,512]{2,1,0:T(2,128)(2,1)}, bf16[64,2,512]{2,1,0:T(2,128)(2,1)S(1)}, u32[]{:S(2)}, u32[]{:S(2)}) %collective-permute-start.2) | collective-permute-done | bytes 131104 | tf_op jit(solution)/shard_map/ppermute | solution.py:170
  12.1 2.4 %first_sweep.1 = (f32[512,2048]{1,0:T(8,128)S(1)}, f32[1,1,512]{2,1,0:T(1,128)S(1)}) custom-call(bf16[64,2,512]{2,1,0:T(2,128)(2,1)S(1)} %copy-done.1, bf16[64,2,512]{2,1,0:T(2,128)(2,1)S(1)} %collective-permute-done.refs_1_, bf16[64,2,512]{2,1,0:T(2,128)(2,1)S(1)} %collective-permute-done.1.refs_2_, bf16[64,2,512]{2,1,0:T(2,128)(2,1)S(1)} %collective-permute-done.2.refs_3_, ...), custom_call_target="tpu_custom_call" | custom-call | flops 4294967296 | tf_op jit(solution)/shard_map/first_sweep/pallas_call | solution.py:35
  14.5 2.9 %student_other.1 = (s16[80,512]{1,0:T(8,128)(2,1)S(1)}, s16[80,512]{1,0:T(8,128)(2,1)S(1)}, s16[80,512]{1,0:T(8,128)(2,1)S(1)}, s16[80,512]{1,0:T(8,128)(2,1)S(1)}) custom-call(s32[1]{0:T(128)} %bitcast.1.refs_1_.refs_0_, bf16[256,512]{1,0:T(8,128)(2,1)S(1)} %get-tuple-element.28.refs_1_, f32[256,640]{1,0:T(8,128)S(1)} %get-tuple-element.29.refs_2_, ...), custom_call_target="tpu_custom_call" | custom-call | flops 1073741824 | tf_op jit(solution)/shard_map/student_other/pallas_call | solution.py:35
  17.4 3.9 %collective-permute-start.7 = (f32[1,1,512]{2,1,0:T(1,128)S(1)}, f32[1,1,512]{2,1,0:T(1,128)S(1)}, u32[]{:S(2)}, u32[]{:S(2)}) collective-permute-start(f32[1,1,512]{2,1,0:T(1,128)S(1)} %get-tuple-element.34.refs_1_), channel_id=1, source_target_pairs={{0,3},{1,2},{2,1},{3,0},{4,7},{5,6},{6,5},{7,4},{8,11},{9,10},{10,... | collective-permute-start | bytes 6152 | tf_op jit(solution)/shard_map/ppermute | solution.py:170
  21.3 0.6 %collective-permute-start.5 = (f32[1,1,512]{2,1,0:T(1,128)S(1)}, f32[1,1,512]{2,1,0:T(1,128)S(1)}, u32[]{:S(2)}, u32[]{:S(2)}) collective-permute-start(f32[1,1,512]{2,1,0:T(1,128)S(1)} %get-tuple-element.34.refs_1_), channel_id=1, source_target_pairs={{0,1},{1,0},{2,3},{3,2},{4,5},{5,4},{6,7},{7,6},{8,9},{9,8},{10,11... | collective-permute-start | bytes 6152 | tf_op jit(solution)/shard_map/ppermute | solution.py:170
  22.0 1.4 %collective-permute-start.9 = (s16[80,512]{1,0:T(8,128)(2,1)S(1)}, s16[80,512]{1,0:T(8,128)(2,1)S(1)}, u32[]{:S(2)}, u32[]{:S(2)}) collective-permute-start(s16[80,512]{1,0:T(8,128)(2,1)S(1)} %get-tuple-element.37), channel_id=1, source_target_pairs={{0,1},{1,0},{2,3},{3,2},{4,5},{5,4},{6,7},{7,6},{8,9},{9,8},{10,11... | collective-permute-start | bytes 245768 | tf_op jit(solution)/shard_map/ppermute | solution.py:170
  23.4 2.9 %collective-permute-start.10 = (s16[80,512]{1,0:T(8,128)(2,1)S(1)}, s16[80,512]{1,0:T(8,128)(2,1)S(1)}, u32[]{:S(2)}, u32[]{:S(2)}) collective-permute-start(s16[80,512]{1,0:T(8,128)(2,1)S(1)} %get-tuple-element.38), channel_id=1, source_target_pairs={{0,2},{1,3},{2,0},{3,1},{4,6},{5,7},{6,4},{7,5},{8,10},{9,11},{10,... | collective-permute-start | bytes 245768 | tf_op jit(solution)/shard_map/ppermute | solution.py:170
  26.3 0.4 collective-permute-start.11
  26.7 1.0 %sweep.1 = (f32[1,1,512]{2,1,0:T(1,128)S(1)}, f32[512,2048]{1,0:T(8,128)S(1)}) custom-call(f32[512,2048]{1,0:T(8,128)S(1)} %get-tuple-element.26.refs_0_, f32[1,1,512]{2,1,0:T(1,128)S(1)} %get-tuple-element.34.refs_1_, f32[1,1,512]{2,1,0:T(1,128)S(1)} %collective-permute-done.5.refs_2_, ...), custom_call_target="tpu_custom_call", output_to_operand_aliasing={{1}: (0, {})} | custom-call | flops 10000000000 | tf_op jit(solution)/shard_map/sweep/pallas_call | solution.py:35
  27.8 4.8 %collective-permute-done.10.refs_2_ = s16[80,512]{1,0:T(8,128)(2,1)S(1)} collective-permute-done((s16[80,512]{1,0:T(8,128)(2,1)S(1)}, s16[80,512]{1,0:T(8,128)(2,1)S(1)}, u32[]{:S(2)}, u32[]{:S(2)}) %collective-permute-start.10) | collective-permute-done | bytes 81952 | tf_op jit(solution)/shard_map/ppermute | solution.py:170
  32.6 0.5 student_totals.1.refs_2_
  33.2 2.5 %collective-permute-start.17 = (f32[1,1,512]{2,1,0:T(1,128)S(1)}, f32[1,1,512]{2,1,0:T(1,128)S(1)}, u32[]{:S(2)}, u32[]{:S(2)}) collective-permute-start(f32[1,1,512]{2,1,0:T(1,128)S(1)} %get-tuple-element.43.refs_3_), channel_id=1, source_target_pairs={{0,3},{1,2},{2,1},{3,0},{4,7},{5,6},{6,5},{7,4},{8,11},{9,10},{10,... | collective-permute-start | bytes 6152 | tf_op jit(solution)/shard_map/ppermute | solution.py:170
  35.7 0.5 collective-permute-start.16
  36.2 1.5 %collective-permute-start.15 = (f32[1,1,512]{2,1,0:T(1,128)S(1)}, f32[1,1,512]{2,1,0:T(1,128)S(1)}, u32[]{:S(2)}, u32[]{:S(2)}) collective-permute-start(f32[1,1,512]{2,1,0:T(1,128)S(1)} %get-tuple-element.43.refs_3_), channel_id=1, source_target_pairs={{0,1},{1,0},{2,3},{3,2},{4,5},{5,4},{6,7},{7,6},{8,9},{9,8},{10,11... | collective-permute-start | bytes 6152 | tf_op jit(solution)/shard_map/ppermute | solution.py:170
  37.6 2.4 %collective-permute-start.14 = (s16[80,512]{1,0:T(8,128)(2,1)S(1)}, s16[80,512]{1,0:T(8,128)(2,1)S(1)}, u32[]{:S(2)}, u32[]{:S(2)}) collective-permute-start(s16[80,512]{1,0:T(8,128)(2,1)S(1)} %get-tuple-element.40.refs_4_), channel_id=1, source_target_pairs={{0,3},{1,2},{2,1},{3,0},{4,7},{5,6},{6,5},{7,4},{8,11},{9,10},{10,... | collective-permute-start | bytes 245768 | tf_op jit(solution)/shard_map/ppermute | solution.py:170
  40.0 2.0 %collective-permute-start.12 = (s16[80,512]{1,0:T(8,128)(2,1)S(1)}, s16[80,512]{1,0:T(8,128)(2,1)S(1)}, u32[]{:S(2)}, u32[]{:S(2)}) collective-permute-start(s16[80,512]{1,0:T(8,128)(2,1)S(1)} %get-tuple-element.40.refs_4_), channel_id=1, source_target_pairs={{0,1},{1,0},{2,3},{3,2},{4,5},{5,4},{6,7},{7,6},{8,9},{9,8},{10,11... | collective-permute-start | bytes 245768 | tf_op jit(solution)/shard_map/ppermute | solution.py:170
  42.0 1.3 %last_sweep.1 = (f32[64,640]{1,0:T(8,128)S(1)}, f32[64,640]{1,0:T(8,128)S(1)}) custom-call(s32[1]{0:T(128)} %bitcast.refs_0_, f32[512,2048]{1,0:T(8,128)S(1)} %get-tuple-element.41.refs_1_, bf16[512,2048]{1,0:T(8,128)(2,1)S(1)} %get-tuple-element.42.refs_2_, f32[1,1,512]{2,1,0:T(1,128)S(1)} %get-tuple-element.43.refs_3_, ...), custom_call_target="tpu_custom_call" | custom-call | flops 10000000000 | tf_op jit(solution)/shard_map/last_sweep/pallas_call | solution.py:35
  43.4 0.6 collective-permute-done.14.refs_3_.refs_7_
  43.9 1.7 %collective-permute-done.13.refs_2_.refs_6_ = s16[80,512]{1,0:T(8,128)(2,1)S(1)} collective-permute-done((s16[80,512]{1,0:T(8,128)(2,1)S(1)}, s16[80,512]{1,0:T(8,128)(2,1)S(1)}, u32[]{:S(2)}, u32[]{:S(2)}) %collective-permute-start.13) | collective-permute-done | bytes 81952 | tf_op jit(solution)/shard_map/ppermute | solution.py:170
  45.7 1.4 %collective-permute-done.18.refs_1_ = f32[64,640]{1,0:T(8,128)S(1)} collective-permute-done((f32[64,640]{1,0:T(8,128)S(1)}, f32[64,640]{1,0:T(8,128)S(1)}, u32[]{:S(2)}, u32[]{:S(2)}) %collective-permute-start.18) | collective-permute-done | bytes 163872 | tf_op jit(solution)/shard_map/ppermute | solution.py:170
  47.3 2.4 %collective-permute-start.21 = (s16[80,512]{1,0:T(8,128)(2,1)S(1)}, s16[80,512]{1,0:T(8,128)(2,1)S(1)}, u32[]{:S(2)}, u32[]{:S(2)}) collective-permute-start(s16[80,512]{1,0:T(8,128)(2,1)S(1)} %code_mixed.1.refs_8_.refs_0_), channel_id=1, source_target_pairs={{0,3},{1,2},{2,1},{3,0},{4,7},{5,6},{6,5},{7,4},{8,11},{9,10},{10,... | collective-permute-start | bytes 245768 | tf_op jit(solution)/shard_map/ppermute | solution.py:170
  49.7 2.0 %collective-permute-start.19 = (s16[80,512]{1,0:T(8,128)(2,1)S(1)}, s16[80,512]{1,0:T(8,128)(2,1)S(1)}, u32[]{:S(2)}, u32[]{:S(2)}) collective-permute-start(s16[80,512]{1,0:T(8,128)(2,1)S(1)} %code_mixed.1.refs_8_.refs_0_), channel_id=1, source_target_pairs={{0,1},{1,0},{2,3},{3,2},{4,5},{5,4},{6,7},{7,6},{8,9},{9,8},{10,11... | collective-permute-start | bytes 245768 | tf_op jit(solution)/shard_map/ppermute | solution.py:170
  51.7 1.0 %prepare.1 = (f32[256,512]{1,0:T(8,128)S(1)}, f32[256,128]{1,0:T(8,128)S(1)}) custom-call(s32[1]{0:T(128)} %bitcast.1.refs_1_.refs_0_, bf16[4,64,512]{2,1,0:T(8,128)(2,1)S(1)} %copy-done, s32[4,64]{1,0:T(4,128)S(1)} %copy-done.2, bf16[4,64]{1,0:T(4,128)(2,1)S(1)} %copy-done.3, s16[80,512]{1,0:T(8,128)(2,1)S(1)} %get-tuple-element.40.refs_4_, ...), custom_call_target="tpu_custom_call" | custom-call | flops 1000000000 | tf_op jit(solution)/shard_map/prepare/pallas_call | solution.py:35
  52.8 1.8 %collective-permute-done.21.refs_3_ = s16[80,512]{1,0:T(8,128)(2,1)S(1)} collective-permute-done((s16[80,512]{1,0:T(8,128)(2,1)S(1)}, s16[80,512]{1,0:T(8,128)(2,1)S(1)}, u32[]{:S(2)}, u32[]{:S(2)}) %collective-permute-start.21) | collective-permute-done | bytes 81952 | tf_op jit(solution)/shard_map/ppermute | solution.py:170
  54.5 2.8 %collective-permute-done.20.refs_2_ = s16[80,512]{1,0:T(8,128)(2,1)S(1)} collective-permute-done((s16[80,512]{1,0:T(8,128)(2,1)S(1)}, s16[80,512]{1,0:T(8,128)(2,1)S(1)}, u32[]{:S(2)}, u32[]{:S(2)}) %collective-permute-start.20) | collective-permute-done | bytes 81952 | tf_op jit(solution)/shard_map/ppermute | solution.py:170
  57.8 1.2 %collective-permute-done.22.refs_5_ = f32[64,512]{1,0:T(8,128)S(1)} collective-permute-done((f32[64,512]{1,0:T(8,128)S(1)}, f32[64,512]{1,0:T(8,128)S(1)}, u32[]{:S(2)}, u32[]{:S(2)}) %collective-permute-start.22) | collective-permute-done | bytes 131104 | tf_op jit(solution)/shard_map/ppermute | solution.py:170
  59.1 1.7 %finish.1 = (f32[4,64,512]{2,1,0:T(8,128)}, f32[4,64]{1,0:T(4,128)}) custom-call(s32[1]{0:T(128)} %bitcast.refs_0_, bf16[4,64,512]{2,1,0:T(8,128)(2,1)S(1)} %copy-done, f32[256,512]{1,0:T(8,128)S(1)} %get-tuple-element.46.refs_4_.refs_2_, f32[256,128]{1,0:T(8,128)S(1)} %get-tuple-element.47.refs_3_, f32[64,512]{1,0:T(8,128)S(1)} %mean_protos.1.refs_4_, ...), custom_call_target="tpu_custom_call" | custom-call | flops 1000000000 | tf_op jit(solution)/shard_map/finish/pallas_call | solution.py:35
  (35 shorter events, 1.1 us)
Async XLA Ops:
  0.6 13.9 %collective-permute-start.4 = (bf16[512,2048]{1,0:T(8,128)(2,1)}, bf16[512,2048]{1,0:T(8,128)(2,1)S(1)}, u32[]{:S(2)}, u32[]{:S(2)}) collective-permute-start(bf16[512,2048]{1,0:T(8,128)(2,1)} %refs_3_.2), channel_id=1, source_target_pairs={{0,4},{4,0},{1,5},{5,1},{2,6},{6,2},{3,7},{7,3},{8,12},{12,8},{9,1... | collective-permute-start | bytes 6291464 | tf_op jit(solution)/shard_map/ppermute | solution.py:170
  1.1 9.3 %collective-permute-start.1 = (bf16[64,2,512]{2,1,0:T(2,128)(2,1)}, bf16[64,2,512]{2,1,0:T(2,128)(2,1)S(1)}, u32[]{:S(2)}, u32[]{:S(2)}) collective-permute-start(bf16[64,2,512]{2,1,0:T(2,128)(2,1)} %refs_0_.1), channel_id=1, source_target_pairs={{0,16},{8,24},{16,0},{24,8},{1,17},{9,25},{17,1},{25,9},{2,18},{10... | collective-permute-start | bytes 393224 | tf_op jit(solution)/shard_map/ppermute | solution.py:170
  3.7 6.8 %collective-permute-start = (bf16[64,2,512]{2,1,0:T(2,128)(2,1)}, bf16[64,2,512]{2,1,0:T(2,128)(2,1)S(1)}, u32[]{:S(2)}, u32[]{:S(2)}) collective-permute-start(bf16[64,2,512]{2,1,0:T(2,128)(2,1)} %refs_0_.1), channel_id=1, source_target_pairs={{0,8},{8,0},{16,24},{24,16},{1,9},{9,1},{17,25},{25,17},{2,10},{10... | collective-permute-start | bytes 393224 | tf_op jit(solution)/shard_map/ppermute | solution.py:170
  5.2 6.8 %collective-permute-start.2 = (bf16[64,2,512]{2,1,0:T(2,128)(2,1)}, bf16[64,2,512]{2,1,0:T(2,128)(2,1)S(1)}, u32[]{:S(2)}, u32[]{:S(2)}) collective-permute-start(bf16[64,2,512]{2,1,0:T(2,128)(2,1)} %refs_0_.1), channel_id=1, source_target_pairs={{0,24},{8,16},{16,8},{24,0},{1,25},{9,17},{17,9},{25,1},{2,26},{10... | collective-permute-start | bytes 393224 | tf_op jit(solution)/shard_map/ppermute | solution.py:170
  5.3 0.9 %copy-start = (bf16[4,64,512]{2,1,0:T(8,128)(2,1)S(1)}, bf16[4,64,512]{2,1,0:T(8,128)(2,1)}, u32[]{:S(2)}) copy-start(bf16[4,64,512]{2,1,0:T(8,128)(2,1)} %refs_1_.3) | copy-start | bytes 786436
  6.2 5.8 %copy-start.1 = (bf16[64,2,512]{2,1,0:T(2,128)(2,1)S(1)}, bf16[64,2,512]{2,1,0:T(2,128)(2,1)}, u32[]{:S(2)}) copy-start(bf16[64,2,512]{2,1,0:T(2,128)(2,1)} %refs_0_.1) | copy-start | bytes 393220
  14.4 3.0 %collective-permute-start.3 = (f32[1,1,512]{2,1,0:T(1,128)S(1)}, f32[1,1,512]{2,1,0:T(1,128)S(1)}, u32[]{:S(2)}, u32[]{:S(2)}) collective-permute-start(f32[1,1,512]{2,1,0:T(1,128)S(1)} %get-tuple-element.27.refs_0_), channel_id=1, source_target_pairs={{0,4},{4,0},{1,5},{5,1},{2,6},{6,2},{3,7},{7,3},{8,12},{12,8},{9,1... | collective-permute-start | bytes 6152 | tf_op jit(solution)/shard_map/ppermute | solution.py:170
  17.4 8.8 %collective-permute-start.7 = (f32[1,1,512]{2,1,0:T(1,128)S(1)}, f32[1,1,512]{2,1,0:T(1,128)S(1)}, u32[]{:S(2)}, u32[]{:S(2)}) collective-permute-start(f32[1,1,512]{2,1,0:T(1,128)S(1)} %get-tuple-element.34.refs_1_), channel_id=1, source_target_pairs={{0,3},{1,2},{2,1},{3,0},{4,7},{5,6},{6,5},{7,4},{8,11},{9,10},{10,... | collective-permute-start | bytes 6152 | tf_op jit(solution)/shard_map/ppermute | solution.py:170
  21.3 5.4 %collective-permute-start.6 = (f32[1,1,512]{2,1,0:T(1,128)S(1)}, f32[1,1,512]{2,1,0:T(1,128)S(1)}, u32[]{:S(2)}, u32[]{:S(2)}) collective-permute-start(f32[1,1,512]{2,1,0:T(1,128)S(1)} %get-tuple-element.34.refs_1_), channel_id=1, source_target_pairs={{0,2},{1,3},{2,0},{3,1},{4,6},{5,7},{6,4},{7,5},{8,10},{9,11},{10,... | collective-permute-start | bytes 6152 | tf_op jit(solution)/shard_map/ppermute | solution.py:170
  21.3 5.4 %collective-permute-start.5 = (f32[1,1,512]{2,1,0:T(1,128)S(1)}, f32[1,1,512]{2,1,0:T(1,128)S(1)}, u32[]{:S(2)}, u32[]{:S(2)}) collective-permute-start(f32[1,1,512]{2,1,0:T(1,128)S(1)} %get-tuple-element.34.refs_1_), channel_id=1, source_target_pairs={{0,1},{1,0},{2,3},{3,2},{4,5},{5,4},{6,7},{7,6},{8,9},{9,8},{10,11... | collective-permute-start | bytes 6152 | tf_op jit(solution)/shard_map/ppermute | solution.py:170
  22.0 5.8 %collective-permute-start.9 = (s16[80,512]{1,0:T(8,128)(2,1)S(1)}, s16[80,512]{1,0:T(8,128)(2,1)S(1)}, u32[]{:S(2)}, u32[]{:S(2)}) collective-permute-start(s16[80,512]{1,0:T(8,128)(2,1)S(1)} %get-tuple-element.37), channel_id=1, source_target_pairs={{0,1},{1,0},{2,3},{3,2},{4,5},{5,4},{6,7},{7,6},{8,9},{9,8},{10,11... | collective-permute-start | bytes 245768 | tf_op jit(solution)/shard_map/ppermute | solution.py:170
  23.4 9.3 %collective-permute-start.10 = (s16[80,512]{1,0:T(8,128)(2,1)S(1)}, s16[80,512]{1,0:T(8,128)(2,1)S(1)}, u32[]{:S(2)}, u32[]{:S(2)}) collective-permute-start(s16[80,512]{1,0:T(8,128)(2,1)S(1)} %get-tuple-element.38), channel_id=1, source_target_pairs={{0,2},{1,3},{2,0},{3,1},{4,6},{5,7},{6,4},{7,5},{8,10},{9,11},{10,... | collective-permute-start | bytes 245768 | tf_op jit(solution)/shard_map/ppermute | solution.py:170
  26.3 6.4 %collective-permute-start.11 = (s16[80,512]{1,0:T(8,128)(2,1)S(1)}, s16[80,512]{1,0:T(8,128)(2,1)S(1)}, u32[]{:S(2)}, u32[]{:S(2)}) collective-permute-start(s16[80,512]{1,0:T(8,128)(2,1)S(1)} %get-tuple-element.39), channel_id=1, source_target_pairs={{0,3},{1,2},{2,1},{3,0},{4,7},{5,6},{6,5},{7,4},{8,11},{9,10},{10,... | collective-permute-start | bytes 245768 | tf_op jit(solution)/shard_map/ppermute | solution.py:170
  27.7 5.5 %collective-permute-start.8 = (f32[1,1,512]{2,1,0:T(1,128)S(1)}, f32[1,1,512]{2,1,0:T(1,128)S(1)}, u32[]{:S(2)}, u32[]{:S(2)}) collective-permute-start(f32[1,1,512]{2,1,0:T(1,128)S(1)} %get-tuple-element.35.refs_4_.refs_0_), channel_id=1, source_target_pairs={{0,4},{4,0},{1,5},{5,1},{2,6},{6,2},{3,7},{7,3},{8,12},{12,8},{9,1... | collective-permute-start | bytes 6152 | tf_op jit(solution)/shard_map/ppermute | solution.py:170
  33.2 6.9 %collective-permute-start.17 = (f32[1,1,512]{2,1,0:T(1,128)S(1)}, f32[1,1,512]{2,1,0:T(1,128)S(1)}, u32[]{:S(2)}, u32[]{:S(2)}) collective-permute-start(f32[1,1,512]{2,1,0:T(1,128)S(1)} %get-tuple-element.43.refs_3_), channel_id=1, source_target_pairs={{0,3},{1,2},{2,1},{3,0},{4,7},{5,6},{6,5},{7,4},{8,11},{9,10},{10,... | collective-permute-start | bytes 6152 | tf_op jit(solution)/shard_map/ppermute | solution.py:170
  35.7 6.4 %collective-permute-start.16 = (f32[1,1,512]{2,1,0:T(1,128)S(1)}, f32[1,1,512]{2,1,0:T(1,128)S(1)}, u32[]{:S(2)}, u32[]{:S(2)}) collective-permute-start(f32[1,1,512]{2,1,0:T(1,128)S(1)} %get-tuple-element.43.refs_3_), channel_id=1, source_target_pairs={{0,2},{1,3},{2,0},{3,1},{4,6},{5,7},{6,4},{7,5},{8,10},{9,11},{10,... | collective-permute-start | bytes 6152 | tf_op jit(solution)/shard_map/ppermute | solution.py:170
  36.2 5.9 %collective-permute-start.15 = (f32[1,1,512]{2,1,0:T(1,128)S(1)}, f32[1,1,512]{2,1,0:T(1,128)S(1)}, u32[]{:S(2)}, u32[]{:S(2)}) collective-permute-start(f32[1,1,512]{2,1,0:T(1,128)S(1)} %get-tuple-element.43.refs_3_), channel_id=1, source_target_pairs={{0,1},{1,0},{2,3},{3,2},{4,5},{5,4},{6,7},{7,6},{8,9},{9,8},{10,11... | collective-permute-start | bytes 6152 | tf_op jit(solution)/shard_map/ppermute | solution.py:170
  37.6 6.3 %collective-permute-start.14 = (s16[80,512]{1,0:T(8,128)(2,1)S(1)}, s16[80,512]{1,0:T(8,128)(2,1)S(1)}, u32[]{:S(2)}, u32[]{:S(2)}) collective-permute-start(s16[80,512]{1,0:T(8,128)(2,1)S(1)} %get-tuple-element.40.refs_4_), channel_id=1, source_target_pairs={{0,3},{1,2},{2,1},{3,0},{4,7},{5,6},{6,5},{7,4},{8,11},{9,10},{10,... | collective-permute-start | bytes 245768 | tf_op jit(solution)/shard_map/ppermute | solution.py:170
  40.0 5.6 %collective-permute-start.13 = (s16[80,512]{1,0:T(8,128)(2,1)S(1)}, s16[80,512]{1,0:T(8,128)(2,1)S(1)}, u32[]{:S(2)}, u32[]{:S(2)}) collective-permute-start(s16[80,512]{1,0:T(8,128)(2,1)S(1)} %get-tuple-element.40.refs_4_), channel_id=1, source_target_pairs={{0,2},{1,3},{2,0},{3,1},{4,6},{5,7},{6,4},{7,5},{8,10},{9,11},{10,... | collective-permute-start | bytes 245768 | tf_op jit(solution)/shard_map/ppermute | solution.py:170
  40.0 5.6 %collective-permute-start.12 = (s16[80,512]{1,0:T(8,128)(2,1)S(1)}, s16[80,512]{1,0:T(8,128)(2,1)S(1)}, u32[]{:S(2)}, u32[]{:S(2)}) collective-permute-start(s16[80,512]{1,0:T(8,128)(2,1)S(1)} %get-tuple-element.40.refs_4_), channel_id=1, source_target_pairs={{0,1},{1,0},{2,3},{3,2},{4,5},{5,4},{6,7},{7,6},{8,9},{9,8},{10,11... | collective-permute-start | bytes 245768 | tf_op jit(solution)/shard_map/ppermute | solution.py:170
  45.6 6.1 %copy-start.2 = (s32[4,64]{1,0:T(4,128)S(1)}, s32[4,64]{1,0:T(4,128)}, u32[]{:S(2)}) copy-start(s32[4,64]{1,0:T(4,128)} %refs_2_.1) | copy-start | bytes 3076
  45.6 6.1 %copy-start.3 = (bf16[4,64]{1,0:T(4,128)(2,1)S(1)}, bf16[4,64]{1,0:T(4,128)(2,1)}, u32[]{:S(2)}) copy-start(bf16[4,64]{1,0:T(4,128)(2,1)} %refs_3_.3) | copy-start | bytes 1540
  45.7 1.5 %collective-permute-start.18 = (f32[64,640]{1,0:T(8,128)S(1)}, f32[64,640]{1,0:T(8,128)S(1)}, u32[]{:S(2)}, u32[]{:S(2)}) collective-permute-start(f32[64,640]{1,0:T(8,128)S(1)} %gate.1), channel_id=1, source_target_pairs={{0,4},{4,0},{1,5},{5,1},{2,6},{6,2},{3,7},{7,3},{8,12},{12,8},{9,1... | collective-permute-start | bytes 491528 | tf_op jit(solution)/shard_map/ppermute | solution.py:170
  47.3 7.2 %collective-permute-start.21 = (s16[80,512]{1,0:T(8,128)(2,1)S(1)}, s16[80,512]{1,0:T(8,128)(2,1)S(1)}, u32[]{:S(2)}, u32[]{:S(2)}) collective-permute-start(s16[80,512]{1,0:T(8,128)(2,1)S(1)} %code_mixed.1.refs_8_.refs_0_), channel_id=1, source_target_pairs={{0,3},{1,2},{2,1},{3,0},{4,7},{5,6},{6,5},{7,4},{8,11},{9,10},{10,... | collective-permute-start | bytes 245768 | tf_op jit(solution)/shard_map/ppermute | solution.py:170
  49.7 7.6 %collective-permute-start.20 = (s16[80,512]{1,0:T(8,128)(2,1)S(1)}, s16[80,512]{1,0:T(8,128)(2,1)S(1)}, u32[]{:S(2)}, u32[]{:S(2)}) collective-permute-start(s16[80,512]{1,0:T(8,128)(2,1)S(1)} %code_mixed.1.refs_8_.refs_0_), channel_id=1, source_target_pairs={{0,2},{1,3},{2,0},{3,1},{4,6},{5,7},{6,4},{7,5},{8,10},{9,11},{10,... | collective-permute-start | bytes 245768 | tf_op jit(solution)/shard_map/ppermute | solution.py:170
  49.7 7.6 %collective-permute-start.19 = (s16[80,512]{1,0:T(8,128)(2,1)S(1)}, s16[80,512]{1,0:T(8,128)(2,1)S(1)}, u32[]{:S(2)}, u32[]{:S(2)}) collective-permute-start(s16[80,512]{1,0:T(8,128)(2,1)S(1)} %code_mixed.1.refs_8_.refs_0_), channel_id=1, source_target_pairs={{0,1},{1,0},{2,3},{3,2},{4,5},{5,4},{6,7},{7,6},{8,9},{9,8},{10,11... | collective-permute-start | bytes 245768 | tf_op jit(solution)/shard_map/ppermute | solution.py:170
  57.7 1.4 %collective-permute-start.22 = (f32[64,512]{1,0:T(8,128)S(1)}, f32[64,512]{1,0:T(8,128)S(1)}, u32[]{:S(2)}, u32[]{:S(2)}) collective-permute-start(f32[64,512]{1,0:T(8,128)S(1)} %mean_protos.1.refs_4_), channel_id=1, source_target_pairs={{0,4},{4,0},{1,5},{5,1},{2,6},{6,2},{3,7},{7,3},{8,12},{12,8},{9,1... | collective-permute-start | bytes 393224 | tf_op jit(solution)/shard_map/ppermute | solution.py:170

commit v6 on v4

--- a/solution.py
+++ b/solution.py
@@ -103,31 +103,37 @@
     return values.astype(jnp.int32).astype(F32)
 
 
+def coded(rows, width):
+    return jax.ShapeDtypeStruct((rows * width // LANES + ROW_TILE, LANES), I16)
+
+
 def store_code(out, values, extra):
     rows, width = values.shape
     largest = jnp.maximum(jnp.max(jnp.abs(values), axis=1, keepdims=True), 1e-30)
     power = jnp.floor(jnp.log2(largest)) + 1.0
     whole = jnp.floor(values * (jnp.exp2(-power) * LEVELS) + 0.5)
-    out[:rows, :] = to_i16(jnp.clip(whole, -LEVELS, LEVELS))
+    whole = to_i16(jnp.clip(whole, -LEVELS, LEVELS))
+    for k in range(width // LANES):
+        out[k * rows : (k + 1) * rows, :] = whole[:, k * LANES : (k + 1) * LANES]
     extra_power, high, low = split_positive(extra)
     lane = lax.broadcasted_iota(jnp.int32, (rows, LANES), 1)
     tail = jnp.where(lane == 0, power, jnp.where(lane == 1, extra_power, jnp.where(lane == 2, high, low)))
     if rows < LANES:
         tail = jnp.concatenate([tail, jnp.zeros((LANES - rows, LANES), F32)], axis=0)
-    block = tail.T[:ROW_TILE, :]
-    out[rows:, :] = to_i16(jnp.concatenate([block, jnp.zeros((ROW_TILE, width - LANES), F32)], axis=1))
-
-
-def decode(ref):
-    rows = ref.shape[0] - ROW_TILE
-    block = to_f32(ref[rows:, :LANES])
+    out[out.shape[0] - ROW_TILE :, :] = to_i16(tail.T[:ROW_TILE, :])
+
+
+def decode(ref, rows):
+    count = (ref.shape[0] - ROW_TILE) // rows
+    block = to_f32(ref[count * rows :, :])
     tail = jnp.concatenate([block, jnp.zeros((LANES - ROW_TILE, LANES), F32)], axis=0).T[:rows, :]
-    values = to_f32(ref[:rows, :]) * (jnp.exp2(tail[:, 0:1]) * (1.0 / LEVELS))
+    values = jnp.concatenate([to_f32(ref[k * rows : (k + 1) * rows, :]) for k in range(count)], axis=1)
+    values = values * (jnp.exp2(tail[:, 0:1]) * (1.0 / LEVELS))
     return values, join_positive(tail[:, 1:2], tail[:, 2:3], tail[:, 3:4])
 
 
-def decode_sum(refs):
-    pairs = [decode(ref) for ref in refs]
+def decode_sum(refs, rows):
+    pairs = [decode(ref, rows) for ref in refs]
     return tree_sum([p[0] for p in pairs]), tree_sum([p[1] for p in pairs])
 
 
@@ -137,15 +143,18 @@
 def pack_kernel(count, *refs):
     parts, refs = refs[:count], refs[count:]
     shares, outs = refs[: len(refs) // 2], refs[len(refs) // 2 :]
-    power, high, low = split_positive(tree_sum([part[0] for part in parts]))
+    terms = split_positive(tree_sum([part[0] for part in parts]))
+    groups = terms[0].shape[1] // LANES
     for share, out in zip(shares, outs):
-        rows = share.shape[0] - ROW_TILE
-        out[:rows, :] = share[:rows, :]
-        at = lax.broadcasted_iota(jnp.int32, (ROW_TILE, share.shape[1]), 0)
-        under = to_f32(share[rows:, :])
-        for k, row in enumerate((power, high, low)):
-            under = jnp.where(at == SUMS_AT + k, row, under)
-        out[rows:, :] = to_i16(under)
+        last = share.shape[0] - ROW_TILE
+        out[:last, :] = share[:last, :]
+        at = lax.broadcasted_iota(jnp.int32, (ROW_TILE, LANES), 0)
+        under = to_f32(share[last:, :])
+        for k, row in enumerate(terms):
+            for j in range(groups):
+                piece = row[:, j * LANES : (j + 1) * LANES]
+                under = jnp.where(at == SUMS_AT + k * groups + j, piece, under)
+        out[last:, :] = to_i16(under)
 
 
 def pack_call(parts, shares):
@@ -159,9 +168,14 @@
 def read_sums(refs):
     if refs[0].dtype == I16:
         terms = []
+        groups = (ROW_TILE - SUMS_AT) // 3
         for ref in refs:
             under = to_f32(ref[ref.shape[0] - ROW_TILE :, :])
-            terms.append(join_positive(*(under[SUMS_AT + k : SUMS_AT + k + 1, :] for k in range(3))))
+            rows = [
+                jnp.concatenate([under[at + j : at + j + 1, :] for j in range(groups)], axis=1)
+                for at in range(SUMS_AT, SUMS_AT + 3 * groups, groups)
+            ]
+            terms.append(join_positive(*rows))
         return tree_sum(terms)
     total = refs[0][0]
     for k in range(1, refs[0].shape[0]):
@@ -252,7 +266,7 @@
             copy.wait()
             weights = unit_columns(buffer[:, here].astype(F32)).astype(BF16)
             add_side(back, unit_feats, weights, False)
-    share = outs[0].shape[0] - ROW_TILE
+    share = back.shape[0] // len(outs)
     for k, out in enumerate(outs):
         first = pl.multiple_of(jnp.bitwise_xor(place[0], k) * share, share)
         total = back[pl.ds(first, share), :]
@@ -266,7 +280,7 @@
     return call(
         functools.partial(other_kernel, count, block),
         "student_other",
-        [shape((rows // pieces + ROW_TILE, width), I16)] * pieces,
+        [coded(rows // pieces, width)] * pieces,
         [pltpu.VMEM((rows, width + LANES), F32)]
         + [pltpu.VMEM((width, columns), BF16)] * count
         + [pltpu.SemaphoreType.DMA((count, columns // block))],
@@ -334,7 +348,7 @@
     return 1.0 / jnp.sum(weighted, axis=0, keepdims=True)
 
 
-def sweep_kernel(count, plan, *refs):
+def sweep_kernel(count, share_rows, plan, *refs):
     shares, refs = refs[:count], refs[count:]
     sum_refs, (sums, share, _, row_scale, partial) = refs[:-5] or shares, refs[-5:]
     scale_rows(sum_refs, row_scale)
@@ -345,14 +359,14 @@
         else:
             partial[...] += terms
     store_sums(sums, partial)
-    back, totals = decode_sum(shares)
+    back, totals = decode_sum(shares, share_rows)
     store_code(share, back / totals, totals)
 
 
-def sweep_call(plan, copies, shares, row_sums):
+def sweep_call(plan, copies, share_rows, shares, row_sums):
     rows = plan.shape[0]
     return call(
-        functools.partial(sweep_kernel, len(shares)),
+        functools.partial(sweep_kernel, len(shares), share_rows),
         "sweep",
         [shape((copies, 1, rows)), shape(shares[0].shape, I16), shape(plan.shape)],
         [pltpu.VMEM((rows, LANES), F32)] * 2,
@@ -413,26 +427,26 @@
 
 def code_kernel(*refs):
     parts, out = refs[:-1], refs[-1]
-    width = out.shape[1]
+    width = parts[0].shape[1] - LANES
     total = tree_sum([part[...] for part in parts])
     store_code(out, total[:, :width], lane_sums(total[:, width:]))
 
 
 def code_call(parts, after=()):
     rows, columns = parts[0].shape
-    out = shape((rows + ROW_TILE, columns - LANES), I16)
+    out = coded(rows, columns - LANES)
     return call(code_kernel, "code_mixed", out, after=after)(*parts)
 
 
 def mean_kernel(*refs):
     parts, out = refs[:-1], refs[-1]
-    mixed, totals = decode_sum(parts)
+    mixed, totals = decode_sum(parts, out.shape[0])
     out[...] = mixed / totals
 
 
-def mean_call(parts, after=()):
-    rows, width = parts[0].shape
-    return call(mean_kernel, "mean_protos", shape((rows - ROW_TILE, width)), after=after)(*parts)
+def mean_call(parts, width, after=()):
+    rows = (parts[0].shape[0] - ROW_TILE) * LANES // width
+    return call(mean_kernel, "mean_protos", shape((rows, width)), after=after)(*parts)
 
 
 FIELDS = 4
@@ -440,10 +454,10 @@
 
 def prepare_kernel(place, feats, picked, weights, *refs):
     shares, (base, fields, expected, totals) = refs[:-4], refs[-4:]
-    rows = shares[0].shape[0] - ROW_TILE
+    rows = expected.shape[0] // len(shares)
     for k, part in enumerate(shares):
         first = pl.multiple_of(jnp.bitwise_xor(place[0], k) * rows, rows)
-        values, extra = decode(part)
+        values, extra = decode(part, rows)
         expected[pl.ds(first, rows), :] = values
         totals[pl.ds(first, rows), :] = jnp.broadcast_to(extra, (rows, LANES))
     images = feats.shape[1]
@@ -525,7 +539,7 @@
     protos = [student_protos] + [swap(student_protos, "crop", k) for k in range(1, crop_devices)]
 
     teacher_rows = image_devices * images * views
-    joint = crops * images % (proto_devices * ROW_TILE) == 0 and teacher_rows == width
+    joint = crops * images % (proto_devices * ROW_TILE) == 0 and 3 * teacher_rows == (ROW_TILE - SUMS_AT) * LANES
     pieces, copies = (proto_devices, 1) if joint else (1, crop_devices * proto_devices)
     if not joint:
         proto_place = jnp.zeros((1,), jnp.int32)
@@ -546,7 +560,7 @@
     plan, sums = first_call(teacher_parts, unit_teacher, copies, block)
     for _ in range(SWEEPS - 2):
         shares, row_sums = exchange(sums, shares)
-        sums, share, plan = sweep_call(plan, copies, shares, row_sums)
+        sums, share, plan = sweep_call(plan, copies, crops * images // pieces, shares, row_sums)
         shares = [share]
     if joint:
         shares, row_sums = exchange(sums, shares)
@@ -556,9 +570,9 @@
         crop_place, plan, unit_protos, row_sums or shares, views * images, crop_devices, block
     )
 
-    coded = code_call([mixed[0]] + [swap(mixed[k], "crop", k) for k in range(1, crop_devices)])
-    base, fields = prepare_call(proto_place, student_feats, pairing, row_weight, shares, after=[coded])
-    means = mean_call(from_all([coded]), after=[base])
+    sent = code_call([mixed[0]] + [swap(mixed[k], "crop", k) for k in range(1, crop_devices)])
+    base, fields = prepare_call(proto_place, student_feats, pairing, row_weight, shares, after=[sent])
+    means = mean_call(from_all([sent]), width, after=[base])
     means = [means] + [swap(means, "crop", k) for k in range(1, crop_devices)]
     return finish_call(views, crop_place, student_feats, base, fields, means)
 

time: 59 us -> 56.2 us (0.953)
  waiting for transfers between devices: 23.3 us -> 20.5 us
    ppermute x17, waiting for transfers between devices: 23.3 us -> 20.5 us  [swap(): return lax.ppermute(values, axis, [(i, i ^ distance) for i in range(count)])]
  transfers between devices with their start and end apart: 17 -> 17, of which waited for: 10 -> 11; matrix products, arithmetic and copies ran while one was open for 0% -> 0% of each run, Pallas kernels for 18% -> 19%
where the time goes in v6:
time: 56.2 us; the launch traced here: 56 us
  waiting for transfers between devices  20.5 us (36%)
  starting transfers between devices  18.2 us (32%)
  Pallas kernels  15.6 us (28%)
  local copies, waits for them, and re-layouts  0.97 us (2%)
  between operations  0.77 us (1%)
    ppermute x17, waiting for transfers between devices, swap(): return lax.ppermute(values, axis, [(i, i ^ distance) for i in range(count)])  20.5 us
    ppermute x17, starting transfers between devices, swap(): return lax.ppermute(values, axis, [(i, i ^ distance) for i in range(count)])  18.2 us
    pallas_call x11, Pallas kernels, run(): pl.pallas_call(body, in_specs=[IN_SMEM] * scalars + [IN_HBM if i in far e...  15.6 us
  transfers between devices with their start and end apart: 17, of which 11 were waited for; matrix products, arithmetic and copies ran while one was open for 0% of the time, Pallas kernels for 19%

profile of v6, /device:TPU:0, one launch (start us, length us, event | category | flops | bytes accessed | tf_op | source)
XLA Modules:
  0.0 56.0 jit_solution(2484737826872912996)
XLA Ops:
  0.6 0.5 collective-permute-start.4
  1.1 2.6 %collective-permute-start.1 = (bf16[64,2,512]{2,1,0:T(2,128)(2,1)}, bf16[64,2,512]{2,1,0:T(2,128)(2,1)S(1)}, u32[]{:S(2)}, u32[]{:S(2)}) collective-permute-start(bf16[64,2,512]{2,1,0:T(2,128)(2,1)} %refs_0_.1), channel_id=1, source_target_pairs={{0,16},{8,24},{16,0},{24,8},{1,17},{9,25},{17,1},{25,9},{2,18},{10... | collective-permute-start | bytes 393224 | tf_op jit(solution)/shard_map/ppermute | solution.py:188
  3.7 1.5 %collective-permute-start = (bf16[64,2,512]{2,1,0:T(2,128)(2,1)}, bf16[64,2,512]{2,1,0:T(2,128)(2,1)S(1)}, u32[]{:S(2)}, u32[]{:S(2)}) collective-permute-start(bf16[64,2,512]{2,1,0:T(2,128)(2,1)} %refs_0_.1), channel_id=1, source_target_pairs={{0,8},{8,0},{16,24},{24,16},{1,9},{9,1},{17,25},{25,17},{2,10},{10... | collective-permute-start | bytes 393224 | tf_op jit(solution)/shard_map/ppermute | solution.py:188
  5.3 0.9 %copy-done = bf16[4,64,512]{2,1,0:T(8,128)(2,1)S(1)} copy-done((bf16[4,64,512]{2,1,0:T(8,128)(2,1)S(1)}, bf16[4,64,512]{2,1,0:T(8,128)(2,1)}, u32[]{:S(2)}) %copy-start) | copy-done | bytes 262168
  6.2 4.2 %student_own.1 = (bf16[512,2048]{1,0:T(8,128)(2,1)S(1)}, bf16[512,2048]{1,0:T(8,128)(2,1)S(1)}, bf16[256,512]{1,0:T(8,128)(2,1)S(1)}, f32[256,640]{1,0:T(8,128)S(1)}) custom-call(s32[1]{0:T(128)} %bitcast.refs_0_, s32[1]{0:T(128)} %bitcast.1.refs_1_.refs_0_, bf16[256,512]{1,0:T(8,128)(2,1)S(1)} %bitcast.3, bf16[512,2048]{1,0:T(8,128)(2,1)} %refs_3_.2, ...), custom_call_target="tpu_custom_call" | custom-call | flops 1073741824 | tf_op jit(solution)/shard_map/student_own/pallas_call | solution.py:36
  10.5 1.5 %collective-permute-done.2.refs_3_ = bf16[64,2,512]{2,1,0:T(2,128)(2,1)S(1)} collective-permute-done((bf16[64,2,512]{2,1,0:T(2,128)(2,1)}, bf16[64,2,512]{2,1,0:T(2,128)(2,1)S(1)}, u32[]{:S(2)}, u32[]{:S(2)}) %collective-permute-start.2) | collective-permute-done | bytes 131104 | tf_op jit(solution)/shard_map/ppermute | solution.py:188
  12.1 2.4 %first_sweep.1 = (f32[512,2048]{1,0:T(8,128)S(1)}, f32[1,1,512]{2,1,0:T(1,128)S(1)}) custom-call(bf16[64,2,512]{2,1,0:T(2,128)(2,1)S(1)} %copy-done.1, bf16[64,2,512]{2,1,0:T(2,128)(2,1)S(1)} %collective-permute-done.refs_1_, bf16[64,2,512]{2,1,0:T(2,128)(2,1)S(1)} %collective-permute-done.1.refs_2_, bf16[64,2,512]{2,1,0:T(2,128)(2,1)S(1)} %collective-permute-done.2.refs_3_, ...), custom_call_target="tpu_custom_call" | custom-call | flops 4294967296 | tf_op jit(solution)/shard_map/first_sweep/pallas_call | solution.py:36
  14.6 2.9 %student_other.1 = (s16[272,128]{1,0:T(8,128)(2,1)S(1)}, s16[272,128]{1,0:T(8,128)(2,1)S(1)}, s16[272,128]{1,0:T(8,128)(2,1)S(1)}, s16[272,128]{1,0:T(8,128)(2,1)S(1)}) custom-call(s32[1]{0:T(128)} %bitcast.1.refs_1_.refs_0_, bf16[256,512]{1,0:T(8,128)(2,1)S(1)} %get-tuple-element.26.refs_1_, f32[256,640]{1,0:T(8,128)S(1)} %get-tuple-element.27.refs_2_, ...), custom_call_target="tpu_custom_call" | custom-call | flops 1073741824 | tf_op jit(solution)/shard_map/student_other/pallas_call | solution.py:36
  17.5 1.9 %collective-permute-start.5 = (s16[272,128]{1,0:T(8,128)(2,1)S(1)}, s16[272,128]{1,0:T(8,128)(2,1)S(1)}, u32[]{:S(2)}, u32[]{:S(2)}) collective-permute-start(s16[272,128]{1,0:T(8,128)(2,1)S(1)} %get-tuple-element.33), channel_id=1, source_target_pairs={{0,1},{1,0},{2,3},{3,2},{4,5},{5,4},{6,7},{7,6},{8,9},{9,8},{10,11... | collective-permute-start | bytes 208904 | tf_op jit(solution)/shard_map/ppermute | solution.py:188
  19.4 2.6 %collective-permute-start.6 = (s16[272,128]{1,0:T(8,128)(2,1)S(1)}, s16[272,128]{1,0:T(8,128)(2,1)S(1)}, u32[]{:S(2)}, u32[]{:S(2)}) collective-permute-start(s16[272,128]{1,0:T(8,128)(2,1)S(1)} %get-tuple-element.34), channel_id=1, source_target_pairs={{0,2},{1,3},{2,0},{3,1},{4,6},{5,7},{6,4},{7,5},{8,10},{9,11},{10,... | collective-permute-start | bytes 208904 | tf_op jit(solution)/shard_map/ppermute | solution.py:188
  22.0 0.2 collective-permute-done.5.refs_2_
  22.2 5.0 %collective-permute-done.6.refs_3_ = s16[272,128]{1,0:T(8,128)(2,1)S(1)} collective-permute-done((s16[272,128]{1,0:T(8,128)(2,1)S(1)}, s16[272,128]{1,0:T(8,128)(2,1)S(1)}, u32[]{:S(2)}, u32[]{:S(2)}) %collective-permute-start.6) | collective-permute-done | bytes 69664 | tf_op jit(solution)/shard_map/ppermute | solution.py:188
  27.2 0.9 %collective-permute-done.7.refs_4_ = s16[272,128]{1,0:T(8,128)(2,1)S(1)} collective-permute-done((s16[272,128]{1,0:T(8,128)(2,1)S(1)}, s16[272,128]{1,0:T(8,128)(2,1)S(1)}, u32[]{:S(2)}, u32[]{:S(2)}) %collective-permute-start.7) | collective-permute-done | bytes 69664 | tf_op jit(solution)/shard_map/ppermute | solution.py:188
  28.1 1.3 %sweep.1 = (f32[1,1,512]{2,1,0:T(1,128)S(1)}, s16[272,128]{1,0:T(8,128)(2,1)S(1)}, f32[512,2048]{1,0:T(8,128)S(1)}) custom-call(f32[512,2048]{1,0:T(8,128)S(1)} %get-tuple-element.24.refs_0_, s16[272,128]{1,0:T(8,128)(2,1)S(1)} %get-tuple-element.32.refs_1_, s16[272,128]{1,0:T(8,128)(2,1)S(1)} %collective-permute-done.5.refs_2_, ...), custom_call_target="tpu_custom_call", output_to_operand_aliasing={{2}: (0, {})} | custom-call | flops 1000000000 | tf_op jit(solution)/shard_map/sweep/pallas_call | solution.py:36
  29.5 1.1 %collective-permute-done.8.refs_1_ = f32[1,1,512]{2,1,0:T(1,128)S(1)} collective-permute-done((f32[1,1,512]{2,1,0:T(1,128)S(1)}, f32[1,1,512]{2,1,0:T(1,128)S(1)}, u32[]{:S(2)}, u32[]{:S(2)}) %collective-permute-start.8) | collective-permute-done | bytes 2080 | tf_op jit(solution)/shard_map/ppermute | solution.py:188
  30.6 2.7 %collective-permute-start.11 = (s16[272,128]{1,0:T(8,128)(2,1)S(1)}, s16[272,128]{1,0:T(8,128)(2,1)S(1)}, u32[]{:S(2)}, u32[]{:S(2)}) collective-permute-start(s16[272,128]{1,0:T(8,128)(2,1)S(1)} %pack_sums.3.refs_3_.refs_4_), channel_id=1, source_target_pairs={{0,3},{1,2},{2,1},{3,0},{4,7},{5,6},{6,5},{7,4},{8,11},{9,10},{10,... | collective-permute-start | bytes 208904 | tf_op jit(solution)/shard_map/ppermute | solution.py:188
  33.3 0.3 collective-permute-start.10
  33.7 1.4 %collective-permute-start.9 = (s16[272,128]{1,0:T(8,128)(2,1)S(1)}, s16[272,128]{1,0:T(8,128)(2,1)S(1)}, u32[]{:S(2)}, u32[]{:S(2)}) collective-permute-start(s16[272,128]{1,0:T(8,128)(2,1)S(1)} %pack_sums.3.refs_3_.refs_4_), channel_id=1, source_target_pairs={{0,1},{1,0},{2,3},{3,2},{4,5},{5,4},{6,7},{7,6},{8,9},{9,8},{10,11... | collective-permute-start | bytes 208904 | tf_op jit(solution)/shard_map/ppermute | solution.py:188
  35.1 2.1 %collective-permute-done.11.refs_6_.refs_7_ = s16[272,128]{1,0:T(8,128)(2,1)S(1)} collective-permute-done((s16[272,128]{1,0:T(8,128)(2,1)S(1)}, s16[272,128]{1,0:T(8,128)(2,1)S(1)}, u32[]{:S(2)}, u32[]{:S(2)}) %collective-permute-start.11) | collective-permute-done | bytes 69664 | tf_op jit(solution)/shard_map/ppermute | solution.py:188
  37.2 3.3 %collective-permute-done.10.refs_5_.refs_6_ = s16[272,128]{1,0:T(8,128)(2,1)S(1)} collective-permute-done((s16[272,128]{1,0:T(8,128)(2,1)S(1)}, s16[272,128]{1,0:T(8,128)(2,1)S(1)}, u32[]{:S(2)}, u32[]{:S(2)}) %collective-permute-start.10) | collective-permute-done | bytes 69664 | tf_op jit(solution)/shard_map/ppermute | solution.py:188
  40.4 1.3 %last_sweep.1 = (f32[64,640]{1,0:T(8,128)S(1)}, f32[64,640]{1,0:T(8,128)S(1)}) custom-call(s32[1]{0:T(128)} %bitcast.refs_0_, f32[512,2048]{1,0:T(8,128)S(1)} %get-tuple-element.38.refs_1_, bf16[512,2048]{1,0:T(8,128)(2,1)S(1)} %get-tuple-element.39.refs_2_, s16[272,128]{1,0:T(8,128)(2,1)S(1)} %pack_sums.3.refs_3_.refs_4_, ...), custom_call_target="tpu_custom_call" | custom-call | flops 1000000000 | tf_op jit(solution)/shard_map/last_sweep/pallas_call | solution.py:36
  41.9 1.4 %collective-permute-done.12.refs_1_ = f32[64,640]{1,0:T(8,128)S(1)} collective-permute-done((f32[64,640]{1,0:T(8,128)S(1)}, f32[64,640]{1,0:T(8,128)S(1)}, u32[]{:S(2)}, u32[]{:S(2)}) %collective-permute-start.12) | collective-permute-done | bytes 163872 | tf_op jit(solution)/shard_map/ppermute | solution.py:188
  43.3 0.2 code_mixed.1.refs_8_.refs_0_
  43.5 2.5 %collective-permute-start.15 = (s16[272,128]{1,0:T(8,128)(2,1)S(1)}, s16[272,128]{1,0:T(8,128)(2,1)S(1)}, u32[]{:S(2)}, u32[]{:S(2)}) collective-permute-start(s16[272,128]{1,0:T(8,128)(2,1)S(1)} %code_mixed.1.refs_8_.refs_0_), channel_id=1, source_target_pairs={{0,3},{1,2},{2,1},{3,0},{4,7},{5,6},{6,5},{7,4},{8,11},{9,10},{10,... | collective-permute-start | bytes 208904 | tf_op jit(solution)/shard_map/ppermute | solution.py:188
  46.0 1.9 %collective-permute-start.13 = (s16[272,128]{1,0:T(8,128)(2,1)S(1)}, s16[272,128]{1,0:T(8,128)(2,1)S(1)}, u32[]{:S(2)}, u32[]{:S(2)}) collective-permute-start(s16[272,128]{1,0:T(8,128)(2,1)S(1)} %code_mixed.1.refs_8_.refs_0_), channel_id=1, source_target_pairs={{0,1},{1,0},{2,3},{3,2},{4,5},{5,4},{6,7},{7,6},{8,9},{9,8},{10,11... | collective-permute-start | bytes 208904 | tf_op jit(solution)/shard_map/ppermute | solution.py:188
  47.9 1.0 %prepare.1 = (f32[256,512]{1,0:T(8,128)S(1)}, f32[256,128]{1,0:T(8,128)S(1)}) custom-call(s32[1]{0:T(128)} %bitcast.1.refs_1_.refs_0_, bf16[4,64,512]{2,1,0:T(8,128)(2,1)S(1)} %copy-done, s32[4,64]{1,0:T(4,128)S(1)} %copy-done.2, bf16[4,64]{1,0:T(4,128)(2,1)S(1)} %copy-done.3, s16[272,128]{1,0:T(8,128)(2,1)S(1)} %pack_sums.3.refs_3_.refs_4_, ...), custom_call_target="tpu_custom_call" | custom-call | flops 1000000000 | tf_op jit(solution)/shard_map/prepare/pallas_call | solution.py:36
  48.9 1.4 %collective-permute-done.15.refs_3_ = s16[272,128]{1,0:T(8,128)(2,1)S(1)} collective-permute-done((s16[272,128]{1,0:T(8,128)(2,1)S(1)}, s16[272,128]{1,0:T(8,128)(2,1)S(1)}, u32[]{:S(2)}, u32[]{:S(2)}) %collective-permute-start.15) | collective-permute-done | bytes 69664 | tf_op jit(solution)/shard_map/ppermute | solution.py:188
  50.4 2.1 %collective-permute-done.14.refs_2_ = s16[272,128]{1,0:T(8,128)(2,1)S(1)} collective-permute-done((s16[272,128]{1,0:T(8,128)(2,1)S(1)}, s16[272,128]{1,0:T(8,128)(2,1)S(1)}, u32[]{:S(2)}, u32[]{:S(2)}) %collective-permute-start.14) | collective-permute-done | bytes 69664 | tf_op jit(solution)/shard_map/ppermute | solution.py:188
  52.5 0.4 mean_protos.1.refs_4_
  52.9 0.1 collective-permute-start.16
  53.0 1.3 %collective-permute-done.16.refs_5_ = f32[64,512]{1,0:T(8,128)S(1)} collective-permute-done((f32[64,512]{1,0:T(8,128)S(1)}, f32[64,512]{1,0:T(8,128)S(1)}, u32[]{:S(2)}, u32[]{:S(2)}) %collective-permute-start.16) | collective-permute-done | bytes 131104 | tf_op jit(solution)/shard_map/ppermute | solution.py:188
  54.3 1.7 %finish.1 = (f32[4,64,512]{2,1,0:T(8,128)}, f32[4,64]{1,0:T(4,128)}) custom-call(s32[1]{0:T(128)} %bitcast.refs_0_, bf16[4,64,512]{2,1,0:T(8,128)(2,1)S(1)} %copy-done, f32[256,512]{1,0:T(8,128)S(1)} %get-tuple-element.42.refs_4_.refs_2_, f32[256,128]{1,0:T(8,128)S(1)} %get-tuple-element.43.refs_3_, f32[64,512]{1,0:T(8,128)S(1)} %mean_protos.1.refs_4_, ...), custom_call_target="tpu_custom_call" | custom-call | flops 1000000000 | tf_op jit(solution)/shard_map/finish/pallas_call | solution.py:36
  (21 shorter events, 0.4 us)
Async XLA Ops:
  0.6 13.9 %collective-permute-start.4 = (bf16[512,2048]{1,0:T(8,128)(2,1)}, bf16[512,2048]{1,0:T(8,128)(2,1)S(1)}, u32[]{:S(2)}, u32[]{:S(2)}) collective-permute-start(bf16[512,2048]{1,0:T(8,128)(2,1)} %refs_3_.2), channel_id=1, source_target_pairs={{0,4},{4,0},{1,5},{5,1},{2,6},{6,2},{3,7},{7,3},{8,12},{12,8},{9,1... | collective-permute-start | bytes 6291464 | tf_op jit(solution)/shard_map/ppermute | solution.py:188
  1.1 9.3 %collective-permute-start.1 = (bf16[64,2,512]{2,1,0:T(2,128)(2,1)}, bf16[64,2,512]{2,1,0:T(2,128)(2,1)S(1)}, u32[]{:S(2)}, u32[]{:S(2)}) collective-permute-start(bf16[64,2,512]{2,1,0:T(2,128)(2,1)} %refs_0_.1), channel_id=1, source_target_pairs={{0,16},{8,24},{16,0},{24,8},{1,17},{9,25},{17,1},{25,9},{2,18},{10... | collective-permute-start | bytes 393224 | tf_op jit(solution)/shard_map/ppermute | solution.py:188
  3.7 6.8 %collective-permute-start = (bf16[64,2,512]{2,1,0:T(2,128)(2,1)}, bf16[64,2,512]{2,1,0:T(2,128)(2,1)S(1)}, u32[]{:S(2)}, u32[]{:S(2)}) collective-permute-start(bf16[64,2,512]{2,1,0:T(2,128)(2,1)} %refs_0_.1), channel_id=1, source_target_pairs={{0,8},{8,0},{16,24},{24,16},{1,9},{9,1},{17,25},{25,17},{2,10},{10... | collective-permute-start | bytes 393224 | tf_op jit(solution)/shard_map/ppermute | solution.py:188
  5.2 6.8 %collective-permute-start.2 = (bf16[64,2,512]{2,1,0:T(2,128)(2,1)}, bf16[64,2,512]{2,1,0:T(2,128)(2,1)S(1)}, u32[]{:S(2)}, u32[]{:S(2)}) collective-permute-start(bf16[64,2,512]{2,1,0:T(2,128)(2,1)} %refs_0_.1), channel_id=1, source_target_pairs={{0,24},{8,16},{16,8},{24,0},{1,25},{9,17},{17,9},{25,1},{2,26},{10... | collective-permute-start | bytes 393224 | tf_op jit(solution)/shard_map/ppermute | solution.py:188
  5.3 0.9 %copy-start = (bf16[4,64,512]{2,1,0:T(8,128)(2,1)S(1)}, bf16[4,64,512]{2,1,0:T(8,128)(2,1)}, u32[]{:S(2)}) copy-start(bf16[4,64,512]{2,1,0:T(8,128)(2,1)} %refs_1_.3) | copy-start | bytes 786436
  6.2 5.8 %copy-start.1 = (bf16[64,2,512]{2,1,0:T(2,128)(2,1)S(1)}, bf16[64,2,512]{2,1,0:T(2,128)(2,1)}, u32[]{:S(2)}) copy-start(bf16[64,2,512]{2,1,0:T(2,128)(2,1)} %refs_0_.1) | copy-start | bytes 393220
  14.5 3.0 %collective-permute-start.3 = (f32[1,1,512]{2,1,0:T(1,128)S(1)}, f32[1,1,512]{2,1,0:T(1,128)S(1)}, u32[]{:S(2)}, u32[]{:S(2)}) collective-permute-start(f32[1,1,512]{2,1,0:T(1,128)S(1)} %get-tuple-element.25.refs_0_), channel_id=1, source_target_pairs={{0,4},{4,0},{1,5},{5,1},{2,6},{6,2},{3,7},{7,3},{8,12},{12,8},{9,1... | collective-permute-start | bytes 6152 | tf_op jit(solution)/shard_map/ppermute | solution.py:188
  17.5 4.7 %collective-permute-start.5 = (s16[272,128]{1,0:T(8,128)(2,1)S(1)}, s16[272,128]{1,0:T(8,128)(2,1)S(1)}, u32[]{:S(2)}, u32[]{:S(2)}) collective-permute-start(s16[272,128]{1,0:T(8,128)(2,1)S(1)} %get-tuple-element.33), channel_id=1, source_target_pairs={{0,1},{1,0},{2,3},{3,2},{4,5},{5,4},{6,7},{7,6},{8,9},{9,8},{10,11... | collective-permute-start | bytes 208904 | tf_op jit(solution)/shard_map/ppermute | solution.py:188
  19.4 7.8 %collective-permute-start.6 = (s16[272,128]{1,0:T(8,128)(2,1)S(1)}, s16[272,128]{1,0:T(8,128)(2,1)S(1)}, u32[]{:S(2)}, u32[]{:S(2)}) collective-permute-start(s16[272,128]{1,0:T(8,128)(2,1)S(1)} %get-tuple-element.34), channel_id=1, source_target_pairs={{0,2},{1,3},{2,0},{3,1},{4,6},{5,7},{6,4},{7,5},{8,10},{9,11},{10,... | collective-permute-start | bytes 208904 | tf_op jit(solution)/shard_map/ppermute | solution.py:188
  22.0 6.2 %collective-permute-start.7 = (s16[272,128]{1,0:T(8,128)(2,1)S(1)}, s16[272,128]{1,0:T(8,128)(2,1)S(1)}, u32[]{:S(2)}, u32[]{:S(2)}) collective-permute-start(s16[272,128]{1,0:T(8,128)(2,1)S(1)} %get-tuple-element.35), channel_id=1, source_target_pairs={{0,3},{1,2},{2,1},{3,0},{4,7},{5,6},{6,5},{7,4},{8,11},{9,10},{10,... | collective-permute-start | bytes 208904 | tf_op jit(solution)/shard_map/ppermute | solution.py:188
  29.4 1.2 %collective-permute-start.8 = (f32[1,1,512]{2,1,0:T(1,128)S(1)}, f32[1,1,512]{2,1,0:T(1,128)S(1)}, u32[]{:S(2)}, u32[]{:S(2)}) collective-permute-start(f32[1,1,512]{2,1,0:T(1,128)S(1)} %get-tuple-element.36.refs_0_), channel_id=1, source_target_pairs={{0,4},{4,0},{1,5},{5,1},{2,6},{6,2},{3,7},{7,3},{8,12},{12,8},{9,1... | collective-permute-start | bytes 6152 | tf_op jit(solution)/shard_map/ppermute | solution.py:188
  30.6 6.5 %collective-permute-start.11 = (s16[272,128]{1,0:T(8,128)(2,1)S(1)}, s16[272,128]{1,0:T(8,128)(2,1)S(1)}, u32[]{:S(2)}, u32[]{:S(2)}) collective-permute-start(s16[272,128]{1,0:T(8,128)(2,1)S(1)} %pack_sums.3.refs_3_.refs_4_), channel_id=1, source_target_pairs={{0,3},{1,2},{2,1},{3,0},{4,7},{5,6},{6,5},{7,4},{8,11},{9,10},{10,... | collective-permute-start | bytes 208904 | tf_op jit(solution)/shard_map/ppermute | solution.py:188
  33.3 7.1 %collective-permute-start.10 = (s16[272,128]{1,0:T(8,128)(2,1)S(1)}, s16[272,128]{1,0:T(8,128)(2,1)S(1)}, u32[]{:S(2)}, u32[]{:S(2)}) collective-permute-start(s16[272,128]{1,0:T(8,128)(2,1)S(1)} %pack_sums.3.refs_3_.refs_4_), channel_id=1, source_target_pairs={{0,2},{1,3},{2,0},{3,1},{4,6},{5,7},{6,4},{7,5},{8,10},{9,11},{10,... | collective-permute-start | bytes 208904 | tf_op jit(solution)/shard_map/ppermute | solution.py:188
  33.7 6.8 %collective-permute-start.9 = (s16[272,128]{1,0:T(8,128)(2,1)S(1)}, s16[272,128]{1,0:T(8,128)(2,1)S(1)}, u32[]{:S(2)}, u32[]{:S(2)}) collective-permute-start(s16[272,128]{1,0:T(8,128)(2,1)S(1)} %pack_sums.3.refs_3_.refs_4_), channel_id=1, source_target_pairs={{0,1},{1,0},{2,3},{3,2},{4,5},{5,4},{6,7},{7,6},{8,9},{9,8},{10,11... | collective-permute-start | bytes 208904 | tf_op jit(solution)/shard_map/ppermute | solution.py:188
  41.8 6.1 %copy-start.2 = (s32[4,64]{1,0:T(4,128)S(1)}, s32[4,64]{1,0:T(4,128)}, u32[]{:S(2)}) copy-start(s32[4,64]{1,0:T(4,128)} %refs_2_.1) | copy-start | bytes 3076
  41.8 6.1 %copy-start.3 = (bf16[4,64]{1,0:T(4,128)(2,1)S(1)}, bf16[4,64]{1,0:T(4,128)(2,1)}, u32[]{:S(2)}) copy-start(bf16[4,64]{1,0:T(4,128)(2,1)} %refs_3_.3) | copy-start | bytes 1540
  41.8 1.5 %collective-permute-start.12 = (f32[64,640]{1,0:T(8,128)S(1)}, f32[64,640]{1,0:T(8,128)S(1)}, u32[]{:S(2)}, u32[]{:S(2)}) collective-permute-start(f32[64,640]{1,0:T(8,128)S(1)} %get-tuple-element.41), channel_id=1, source_target_pairs={{0,4},{4,0},{1,5},{5,1},{2,6},{6,2},{3,7},{7,3},{8,12},{12,8},{9,1... | collective-permute-start | bytes 491528 | tf_op jit(solution)/shard_map/ppermute | solution.py:188
  43.5 6.9 %collective-permute-start.15 = (s16[272,128]{1,0:T(8,128)(2,1)S(1)}, s16[272,128]{1,0:T(8,128)(2,1)S(1)}, u32[]{:S(2)}, u32[]{:S(2)}) collective-permute-start(s16[272,128]{1,0:T(8,128)(2,1)S(1)} %code_mixed.1.refs_8_.refs_0_), channel_id=1, source_target_pairs={{0,3},{1,2},{2,1},{3,0},{4,7},{5,6},{6,5},{7,4},{8,11},{9,10},{10,... | collective-permute-start | bytes 208904 | tf_op jit(solution)/shard_map/ppermute | solution.py:188
  46.0 6.6 %collective-permute-start.14 = (s16[272,128]{1,0:T(8,128)(2,1)S(1)}, s16[272,128]{1,0:T(8,128)(2,1)S(1)}, u32[]{:S(2)}, u32[]{:S(2)}) collective-permute-start(s16[272,128]{1,0:T(8,128)(2,1)S(1)} %code_mixed.1.refs_8_.refs_0_), channel_id=1, source_target_pairs={{0,2},{1,3},{2,0},{3,1},{4,6},{5,7},{6,4},{7,5},{8,10},{9,11},{10,... | collective-permute-start | bytes 208904 | tf_op jit(solution)/shard_map/ppermute | solution.py:188
  46.0 6.6 %collective-permute-start.13 = (s16[272,128]{1,0:T(8,128)(2,1)S(1)}, s16[272,128]{1,0:T(8,128)(2,1)S(1)}, u32[]{:S(2)}, u32[]{:S(2)}) collective-permute-start(s16[272,128]{1,0:T(8,128)(2,1)S(1)} %code_mixed.1.refs_8_.refs_0_), channel_id=1, source_target_pairs={{0,1},{1,0},{2,3},{3,2},{4,5},{5,4},{6,7},{7,6},{8,9},{9,8},{10,11... | collective-permute-start | bytes 208904 | tf_op jit(solution)/shard_map/ppermute | solution.py:188
  52.9 1.4 %collective-permute-start.16 = (f32[64,512]{1,0:T(8,128)S(1)}, f32[64,512]{1,0:T(8,128)S(1)}, u32[]{:S(2)}, u32[]{:S(2)}) collective-permute-start(f32[64,512]{1,0:T(8,128)S(1)} %mean_protos.1.refs_4_), channel_id=1, source_target_pairs={{0,4},{4,0},{1,5},{5,1},{2,6},{6,2},{3,7},{7,3},{8,12},{12,8},{9,1... | collective-permute-start | bytes 393224 | tf_op jit(solution)/shard_map/ppermute | solution.py:188

commit v7 on v6

--- a/solution.py
+++ b/solution.py
@@ -26,7 +26,7 @@
 IN_SMEM = pl.BlockSpec(memory_space=pltpu.SMEM)
 
 
-def call(kernel, name, out_shape, scratch=(), scalars=0, vmem=16, after=(), flops=10**9, aliases=None, far=()):
+def call(kernel, name, out_shape, scratch=(), scalars=0, vmem=16, after=(), flops=10**9, aliases=None, far=(), far_out=()):
     def run(*operands):
         count = len(operands)
 
@@ -38,7 +38,9 @@
             in_specs=[IN_SMEM] * scalars
             + [IN_HBM if i in far else IN_VMEM for i in range(scalars, count)]
             + [pl.BlockSpec(memory_space=pl.ANY)] * len(after),
-            out_specs=jax.tree.map(lambda _: IN_VMEM, out_shape),
+            out_specs=[IN_HBM if i in far_out else IN_VMEM for i in range(len(out_shape))]
+            if isinstance(out_shape, list)
+            else IN_VMEM,
             out_shape=out_shape,
             scratch_shapes=list(scratch),
             compiler_params=pltpu.CompilerParams(vmem_limit_bytes=vmem * 1024 * 1024),
@@ -188,10 +190,10 @@
     return lax.ppermute(values, axis, [(i, i ^ distance) for i in range(count)])
 
 
-def fetch(sources, buffers, sems, block):
-    columns = buffers[0].shape[1]
+def fetch(sources, buffers, sems, block, first=0, last=None):
+    last = buffers[0].shape[1] if last is None else last
     copies = []
-    for j, start in enumerate(range(0, columns, block)):
+    for j, start in enumerate(range(first, last, block)):
         here = pl.ds(start, block)
         copies.append(
             [
@@ -253,19 +255,44 @@
     )(crop_place, proto_place, feats, protos, teacher_protos)
 
 
-def other_kernel(count, block, place, unit_feats, partial, *refs):
+def begin_kernel(count, block, last, unit_feats, partial, *refs):
+    sources, (back, *buffers, sems) = refs[:count], refs[count:]
+    copies = fetch(sources, buffers, sems, block, 0, last)
+    back[...] = partial[...]
+    add_blocks(copies, buffers, back, unit_feats, block, 0)
+
+
+def add_blocks(copies, buffers, back, unit_feats, block, first):
+    for j, group in enumerate(copies):
+        here = slice(first + j * block, first + (j + 1) * block)
+        for copy, buffer in zip(group, buffers):
+            copy.wait()
+            weights = unit_columns(buffer[:, here].astype(F32)).astype(BF16)
+            add_side(back, unit_feats, weights, False)
+
+
+def begin_call(unit_feats, back, protos, last, block):
+    width, columns = protos[0].shape
+    count = len(protos)
+    return call(
+        functools.partial(begin_kernel, count, block, last),
+        "student_begin",
+        shape(back.shape),
+        [pltpu.VMEM((width, columns), BF16)] * count + [pltpu.SemaphoreType.DMA((count, last // block))],
+        vmem=48 if count > 1 else 16,
+        far=range(2, 2 + count),
+        flops=4 * unit_feats.shape[0] * count * last * width,
+    )(unit_feats, back, *protos)
+
+
+def other_kernel(count, block, from_column, place, unit_feats, partial, *refs):
     sources, refs = refs[:count], refs[count:]
     outs, refs = refs[: -count - 2], refs[-count - 2 :]
     back, buffers, sems = refs[0], refs[1:-1], refs[-1]
     width = unit_feats.shape[1]
-    copies = fetch(sources, buffers, sems, block)
+    copies = fetch(sources, buffers, sems, block, from_column)
     back[...] = partial[...]
-    for j, group in enumerate(copies):
-        here = slice(j * block, (j + 1) * block)
-        for copy, buffer in zip(group, buffers):
-            copy.wait()
-            weights = unit_columns(buffer[:, here].astype(F32)).astype(BF16)
-            add_side(back, unit_feats, weights, False)
+    add_blocks(copies, buffers, back, unit_feats, block, from_column)
     share = back.shape[0] // len(outs)
     for k, out in enumerate(outs):
         first = pl.multiple_of(jnp.bitwise_xor(place[0], k) * share, share)
@@ -273,17 +300,17 @@
         store_code(out, total[:, :width], lane_sums(total[:, width:]))
 
 
-def other_call(place, unit_feats, back, protos, pieces, block):
+def other_call(place, unit_feats, back, protos, pieces, from_column, block):
     width, columns = protos[0].shape
     rows = unit_feats.shape[0]
     count = len(protos)
     return call(
-        functools.partial(other_kernel, count, block),
+        functools.partial(other_kernel, count, block, from_column),
         "student_other",
         [coded(rows // pieces, width)] * pieces,
         [pltpu.VMEM((rows, width + LANES), F32)]
         + [pltpu.VMEM((width, columns), BF16)] * count
-        + [pltpu.SemaphoreType.DMA((count, columns // block))],
+        + [pltpu.SemaphoreType.DMA((count, (columns - from_column) // block))],
         scalars=1,
         vmem=48 if count > 1 else 16,
         far=range(3, 3 + count),
@@ -492,7 +519,8 @@
 
 
 def finish_kernel(views, place, feats, base, fields, *refs):
-    parts, (gradient, loss, means) = refs[:-3], refs[-3:]
+    parts, (gradient, loss, means, ready, sems) = refs[:-5], refs[-5:]
+    copies = []
     rows = parts[0].shape[0]
     for k, part in enumerate(parts):
         first = pl.multiple_of(jnp.bitwise_xor(place[0], k) * rows, rows)
@@ -507,10 +535,14 @@
         for view in range(1, views):
             chosen = jnp.where(view_column == view, means[view * images : (view + 1) * images, :], chosen)
         along = cubic * lane_sums(raw * chosen)
-        gradient[crop] = base[here, :] - factor * chosen + along * raw
+        ready[crop] = base[here, :] - factor * chosen + along * raw
+        copies.append(pltpu.make_async_copy(ready.at[crop], gradient.at[crop], sems.at[crop]))
+        copies[-1].start()
         unit = (raw * scales).astype(BF16).astype(F32)
         column = fields[here, FIELDS - 1 : FIELDS] - lane_sums(unit * chosen) * (1.0 / student_softness)
         loss[crop : crop + 1, :] = jnp.broadcast_to(column, (images, LANES)).T[:1, :]
+    for copy in copies:
+        copy.wait()
 
 
 def finish_call(views, place, feats, base, fields, means):
@@ -519,8 +551,13 @@
         functools.partial(finish_kernel, views),
         "finish",
         [shape((crops, images, width)), shape((crops, images))],
-        [pltpu.VMEM((views * images, width), F32)],
+        [
+            pltpu.VMEM((views * images, width), F32),
+            pltpu.VMEM((crops, images, width), F32),
+            pltpu.SemaphoreType.DMA((crops,)),
+        ],
         scalars=1,
+        far_out=[0],
     )(place, feats, base, fields, *means)
 
 
@@ -556,8 +593,10 @@
     unit_protos, unit_teacher, unit_feats, back = own_call(
         crop_place, proto_place, feats, student_protos, teacher_protos, block
     )
-    shares = other_call(proto_place, unit_feats, back, protos[1:], pieces, block)
-    plan, sums = first_call(teacher_parts, unit_teacher, copies, block)
+    half = student_protos.shape[1] // (2 * block) * block
+    back = begin_call(unit_feats, back, protos[1:], half, block)
+    plan, sums = first_call(teacher_parts, unit_teacher, copies, block, after=[back])
+    shares = other_call(proto_place, unit_feats, back, protos[1:], pieces, half, block)
     for _ in range(SWEEPS - 2):
         shares, row_sums = exchange(sums, shares)
         sums, share, plan = sweep_call(plan, copies, crops * images // pieces, shares, row_sums)

time: 56.2 us -> 55.7 us (level)
  waiting for transfers between devices: 20.5 us -> 19.1 us
  Pallas kernels: 15.6 us -> 16.4 us
    ppermute x17, waiting for transfers between devices: 20.5 us -> 19.1 us  [swap(): return lax.ppermute(values, axis, [(i, i ^ distance) for i in range(count)])]
    pallas_call x11 -> x12, Pallas kernels: 15.6 us -> 16.4 us  [run(): pl.pallas_call(body, in_specs=[IN_SMEM] * scalars + [IN_HBM if i in far e...]
  transfers between devices with their start and end apart: 17 -> 17, of which waited for: 11 -> 11; matrix products, arithmetic and copies ran while one was open for 0% -> 0% of each run, Pallas kernels for 19% -> 15%
where the time goes in v7:
time: 55.7 us; the launch traced here: 55.5 us
  waiting for transfers between devices  19.1 us (34%)
  starting transfers between devices  18.2 us (33%)
  Pallas kernels  16.4 us (29%)
  local copies, waits for them, and re-layouts  0.97 us (2%)
  between operations  0.78 us (1%)
    ppermute x17, waiting for transfers between devices, swap(): return lax.ppermute(values, axis, [(i, i ^ distance) for i in range(count)])  19.1 us
    ppermute x17, starting transfers between devices, swap(): return lax.ppermute(values, axis, [(i, i ^ distance) for i in range(count)])  18.2 us
    pallas_call x12, Pallas kernels, run(): pl.pallas_call(body, in_specs=[IN_SMEM] * scalars + [IN_HBM if i in far e...  16.4 us
  transfers between devices with their start and end apart: 17, of which 11 were waited for; matrix products, arithmetic and copies ran while one was open for 0% of the time, Pallas kernels for 15%

profile of v7, /device:TPU:0, one launch (start us, length us, event | category | flops | bytes accessed | tf_op | source)
XLA Modules:
  0.0 55.5 jit_solution(12277381362459845883)
XLA Ops:
  0.6 0.5 collective-permute-start.3
  1.1 2.6 %collective-permute-start.1 = (bf16[64,2,512]{2,1,0:T(2,128)(2,1)}, bf16[64,2,512]{2,1,0:T(2,128)(2,1)S(1)}, u32[]{:S(2)}, u32[]{:S(2)}) collective-permute-start(bf16[64,2,512]{2,1,0:T(2,128)(2,1)} %refs_0_.1), channel_id=1, source_target_pairs={{0,16},{8,24},{16,0},{24,8},{1,17},{9,25},{17,1},{25,9},{2,18},{10... | collective-permute-start | bytes 393224 | tf_op jit(solution)/shard_map/ppermute | solution.py:190
  3.7 1.5 %collective-permute-start = (bf16[64,2,512]{2,1,0:T(2,128)(2,1)}, bf16[64,2,512]{2,1,0:T(2,128)(2,1)S(1)}, u32[]{:S(2)}, u32[]{:S(2)}) collective-permute-start(bf16[64,2,512]{2,1,0:T(2,128)(2,1)} %refs_0_.1), channel_id=1, source_target_pairs={{0,8},{8,0},{16,24},{24,16},{1,9},{9,1},{17,25},{25,17},{2,10},{10... | collective-permute-start | bytes 393224 | tf_op jit(solution)/shard_map/ppermute | solution.py:190
  5.3 0.9 %copy-done = bf16[4,64,512]{2,1,0:T(8,128)(2,1)S(1)} copy-done((bf16[4,64,512]{2,1,0:T(8,128)(2,1)S(1)}, bf16[4,64,512]{2,1,0:T(8,128)(2,1)}, u32[]{:S(2)}) %copy-start) | copy-done | bytes 262168
  6.2 4.2 %student_own.1 = (bf16[512,2048]{1,0:T(8,128)(2,1)S(1)}, bf16[512,2048]{1,0:T(8,128)(2,1)S(1)}, bf16[256,512]{1,0:T(8,128)(2,1)S(1)}, f32[256,640]{1,0:T(8,128)S(1)}) custom-call(s32[1]{0:T(128)} %bitcast.refs_0_, s32[1]{0:T(128)} %bitcast.1.refs_1_.refs_0_, bf16[256,512]{1,0:T(8,128)(2,1)S(1)} %bitcast.3, bf16[512,2048]{1,0:T(8,128)(2,1)} %refs_3_.2, ...), custom_call_target="tpu_custom_call" | custom-call | flops 1073741824 | tf_op jit(solution)/shard_map/student_own/pallas_call | solution.py:36
  10.5 1.3 %student_begin.1.refs_5_.refs_2_ = f32[256,640]{1,0:T(8,128)S(1)} custom-call(bf16[256,512]{1,0:T(8,128)(2,1)S(1)} %get-tuple-element.24.refs_0_.refs_1_, f32[256,640]{1,0:T(8,128)S(1)} %get-tuple-element.25.refs_1_, bf16[512,2048]{1,0:T(8,128)(2,1)S(1)} %collective-permute-done.3.refs_2_.refs_3_), custom_call_target="tpu_custom_call" | custom-call | flops 536870912 | tf_op jit(solution)/shard_map/student_begin/pallas_call | solution.py:36
  11.8 0.2 collective-permute-done.2.refs_3_
  12.1 2.4 %first_sweep.1 = (f32[512,2048]{1,0:T(8,128)S(1)}, f32[1,1,512]{2,1,0:T(1,128)S(1)}) custom-call(bf16[64,2,512]{2,1,0:T(2,128)(2,1)S(1)} %copy-done.1, bf16[64,2,512]{2,1,0:T(2,128)(2,1)S(1)} %collective-permute-done.refs_1_, bf16[64,2,512]{2,1,0:T(2,128)(2,1)S(1)} %collective-permute-done.1.refs_2_, bf16[64,2,512]{2,1,0:T(2,128)(2,1)S(1)} %collective-permute-done.2.refs_3_, ...), custom_call_target="tpu_custom_call" | custom-call | flops 4294967296 | tf_op jit(solution)/shard_map/first_sweep/pallas_call | solution.py:36
  14.5 1.7 %student_other.1 = (s16[272,128]{1,0:T(8,128)(2,1)S(1)}, s16[272,128]{1,0:T(8,128)(2,1)S(1)}, s16[272,128]{1,0:T(8,128)(2,1)S(1)}, s16[272,128]{1,0:T(8,128)(2,1)S(1)}) custom-call(s32[1]{0:T(128)} %bitcast.1.refs_1_.refs_0_, bf16[256,512]{1,0:T(8,128)(2,1)S(1)} %get-tuple-element.24.refs_0_.refs_1_, f32[256,640]{1,0:T(8,128)S(1)} %student_begin.1.refs_5_.refs_2_, ...), custom_call_target="tpu_custom_call" | custom-call | flops 1073741824 | tf_op jit(solution)/shard_map/student_other/pallas_call | solution.py:36
  16.3 1.9 %collective-permute-start.5 = (s16[272,128]{1,0:T(8,128)(2,1)S(1)}, s16[272,128]{1,0:T(8,128)(2,1)S(1)}, u32[]{:S(2)}, u32[]{:S(2)}) collective-permute-start(s16[272,128]{1,0:T(8,128)(2,1)S(1)} %get-tuple-element.33), channel_id=1, source_target_pairs={{0,1},{1,0},{2,3},{3,2},{4,5},{5,4},{6,7},{7,6},{8,9},{9,8},{10,11... | collective-permute-start | bytes 208904 | tf_op jit(solution)/shard_map/ppermute | solution.py:190
  18.2 2.6 %collective-permute-start.6 = (s16[272,128]{1,0:T(8,128)(2,1)S(1)}, s16[272,128]{1,0:T(8,128)(2,1)S(1)}, u32[]{:S(2)}, u32[]{:S(2)}) collective-permute-start(s16[272,128]{1,0:T(8,128)(2,1)S(1)} %get-tuple-element.34), channel_id=1, source_target_pairs={{0,2},{1,3},{2,0},{3,1},{4,6},{5,7},{6,4},{7,5},{8,10},{9,11},{10,... | collective-permute-start | bytes 208904 | tf_op jit(solution)/shard_map/ppermute | solution.py:190
  20.8 0.2 collective-permute-done.5.refs_2_
  21.0 5.0 %collective-permute-done.6.refs_3_ = s16[272,128]{1,0:T(8,128)(2,1)S(1)} collective-permute-done((s16[272,128]{1,0:T(8,128)(2,1)S(1)}, s16[272,128]{1,0:T(8,128)(2,1)S(1)}, u32[]{:S(2)}, u32[]{:S(2)}) %collective-permute-start.6) | collective-permute-done | bytes 69664 | tf_op jit(solution)/shard_map/ppermute | solution.py:190
  26.1 0.9 %collective-permute-done.7.refs_4_ = s16[272,128]{1,0:T(8,128)(2,1)S(1)} collective-permute-done((s16[272,128]{1,0:T(8,128)(2,1)S(1)}, s16[272,128]{1,0:T(8,128)(2,1)S(1)}, u32[]{:S(2)}, u32[]{:S(2)}) %collective-permute-start.7) | collective-permute-done | bytes 69664 | tf_op jit(solution)/shard_map/ppermute | solution.py:190
  27.0 1.3 %sweep.1 = (f32[1,1,512]{2,1,0:T(1,128)S(1)}, s16[272,128]{1,0:T(8,128)(2,1)S(1)}, f32[512,2048]{1,0:T(8,128)S(1)}) custom-call(f32[512,2048]{1,0:T(8,128)S(1)} %get-tuple-element.26.refs_0_, s16[272,128]{1,0:T(8,128)(2,1)S(1)} %get-tuple-element.32.refs_1_, s16[272,128]{1,0:T(8,128)(2,1)S(1)} %collective-permute-done.5.refs_2_, ...), custom_call_target="tpu_custom_call", output_to_operand_aliasing={{2}: (0, {})} | custom-call | flops 1000000000 | tf_op jit(solution)/shard_map/sweep/pallas_call | solution.py:36
  28.3 1.1 %collective-permute-done.8.refs_1_ = f32[1,1,512]{2,1,0:T(1,128)S(1)} collective-permute-done((f32[1,1,512]{2,1,0:T(1,128)S(1)}, f32[1,1,512]{2,1,0:T(1,128)S(1)}, u32[]{:S(2)}, u32[]{:S(2)}) %collective-permute-start.8) | collective-permute-done | bytes 2080 | tf_op jit(solution)/shard_map/ppermute | solution.py:190
  29.5 2.7 %collective-permute-start.11 = (s16[272,128]{1,0:T(8,128)(2,1)S(1)}, s16[272,128]{1,0:T(8,128)(2,1)S(1)}, u32[]{:S(2)}, u32[]{:S(2)}) collective-permute-start(s16[272,128]{1,0:T(8,128)(2,1)S(1)} %pack_sums.3.refs_3_.refs_4_), channel_id=1, source_target_pairs={{0,3},{1,2},{2,1},{3,0},{4,7},{5,6},{6,5},{7,4},{8,11},{9,10},{10,... | collective-permute-start | bytes 208904 | tf_op jit(solution)/shard_map/ppermute | solution.py:190
  32.2 0.3 collective-permute-start.10
  32.5 1.4 %collective-permute-start.9 = (s16[272,128]{1,0:T(8,128)(2,1)S(1)}, s16[272,128]{1,0:T(8,128)(2,1)S(1)}, u32[]{:S(2)}, u32[]{:S(2)}) collective-permute-start(s16[272,128]{1,0:T(8,128)(2,1)S(1)} %pack_sums.3.refs_3_.refs_4_), channel_id=1, source_target_pairs={{0,1},{1,0},{2,3},{3,2},{4,5},{5,4},{6,7},{7,6},{8,9},{9,8},{10,11... | collective-permute-start | bytes 208904 | tf_op jit(solution)/shard_map/ppermute | solution.py:190
  33.9 2.1 %collective-permute-done.11.refs_6_.refs_7_ = s16[272,128]{1,0:T(8,128)(2,1)S(1)} collective-permute-done((s16[272,128]{1,0:T(8,128)(2,1)S(1)}, s16[272,128]{1,0:T(8,128)(2,1)S(1)}, u32[]{:S(2)}, u32[]{:S(2)}) %collective-permute-start.11) | collective-permute-done | bytes 69664 | tf_op jit(solution)/shard_map/ppermute | solution.py:190
  36.0 3.2 %collective-permute-done.10.refs_5_.refs_6_ = s16[272,128]{1,0:T(8,128)(2,1)S(1)} collective-permute-done((s16[272,128]{1,0:T(8,128)(2,1)S(1)}, s16[272,128]{1,0:T(8,128)(2,1)S(1)}, u32[]{:S(2)}, u32[]{:S(2)}) %collective-permute-start.10) | collective-permute-done | bytes 69664 | tf_op jit(solution)/shard_map/ppermute | solution.py:190
  39.2 1.4 %last_sweep.1 = (f32[64,640]{1,0:T(8,128)S(1)}, f32[64,640]{1,0:T(8,128)S(1)}) custom-call(s32[1]{0:T(128)} %bitcast.refs_0_, f32[512,2048]{1,0:T(8,128)S(1)} %get-tuple-element.38.refs_1_, bf16[512,2048]{1,0:T(8,128)(2,1)S(1)} %get-tuple-element.39.refs_2_, s16[272,128]{1,0:T(8,128)(2,1)S(1)} %pack_sums.3.refs_3_.refs_4_, ...), custom_call_target="tpu_custom_call" | custom-call | flops 1000000000 | tf_op jit(solution)/shard_map/last_sweep/pallas_call | solution.py:36
  40.7 1.4 %collective-permute-done.12.refs_1_ = f32[64,640]{1,0:T(8,128)S(1)} collective-permute-done((f32[64,640]{1,0:T(8,128)S(1)}, f32[64,640]{1,0:T(8,128)S(1)}, u32[]{:S(2)}, u32[]{:S(2)}) %collective-permute-start.12) | collective-permute-done | bytes 163872 | tf_op jit(solution)/shard_map/ppermute | solution.py:190
  42.1 0.2 code_mixed.1.refs_8_.refs_0_
  42.3 2.5 %collective-permute-start.15 = (s16[272,128]{1,0:T(8,128)(2,1)S(1)}, s16[272,128]{1,0:T(8,128)(2,1)S(1)}, u32[]{:S(2)}, u32[]{:S(2)}) collective-permute-start(s16[272,128]{1,0:T(8,128)(2,1)S(1)} %code_mixed.1.refs_8_.refs_0_), channel_id=1, source_target_pairs={{0,3},{1,2},{2,1},{3,0},{4,7},{5,6},{6,5},{7,4},{8,11},{9,10},{10,... | collective-permute-start | bytes 208904 | tf_op jit(solution)/shard_map/ppermute | solution.py:190
  44.8 1.9 %collective-permute-start.13 = (s16[272,128]{1,0:T(8,128)(2,1)S(1)}, s16[272,128]{1,0:T(8,128)(2,1)S(1)}, u32[]{:S(2)}, u32[]{:S(2)}) collective-permute-start(s16[272,128]{1,0:T(8,128)(2,1)S(1)} %code_mixed.1.refs_8_.refs_0_), channel_id=1, source_target_pairs={{0,1},{1,0},{2,3},{3,2},{4,5},{5,4},{6,7},{7,6},{8,9},{9,8},{10,11... | collective-permute-start | bytes 208904 | tf_op jit(solution)/shard_map/ppermute | solution.py:190
  46.7 1.0 %prepare.1 = (f32[256,512]{1,0:T(8,128)S(1)}, f32[256,128]{1,0:T(8,128)S(1)}) custom-call(s32[1]{0:T(128)} %bitcast.1.refs_1_.refs_0_, bf16[4,64,512]{2,1,0:T(8,128)(2,1)S(1)} %copy-done, s32[4,64]{1,0:T(4,128)S(1)} %copy-done.2, bf16[4,64]{1,0:T(4,128)(2,1)S(1)} %copy-done.3, s16[272,128]{1,0:T(8,128)(2,1)S(1)} %pack_sums.3.refs_3_.refs_4_, ...), custom_call_target="tpu_custom_call" | custom-call | flops 1000000000 | tf_op jit(solution)/shard_map/prepare/pallas_call | solution.py:36
  47.7 1.4 %collective-permute-done.15.refs_3_ = s16[272,128]{1,0:T(8,128)(2,1)S(1)} collective-permute-done((s16[272,128]{1,0:T(8,128)(2,1)S(1)}, s16[272,128]{1,0:T(8,128)(2,1)S(1)}, u32[]{:S(2)}, u32[]{:S(2)}) %collective-permute-start.15) | collective-permute-done | bytes 69664 | tf_op jit(solution)/shard_map/ppermute | solution.py:190
  49.2 2.1 %collective-permute-done.14.refs_2_ = s16[272,128]{1,0:T(8,128)(2,1)S(1)} collective-permute-done((s16[272,128]{1,0:T(8,128)(2,1)S(1)}, s16[272,128]{1,0:T(8,128)(2,1)S(1)}, u32[]{:S(2)}, u32[]{:S(2)}) %collective-permute-start.14) | collective-permute-done | bytes 69664 | tf_op jit(solution)/shard_map/ppermute | solution.py:190
  51.3 0.4 mean_protos.1.refs_4_
  51.8 1.3 %collective-permute-done.16.refs_5_ = f32[64,512]{1,0:T(8,128)S(1)} collective-permute-done((f32[64,512]{1,0:T(8,128)S(1)}, f32[64,512]{1,0:T(8,128)S(1)}, u32[]{:S(2)}, u32[]{:S(2)}) %collective-permute-start.16) | collective-permute-done | bytes 131104 | tf_op jit(solution)/shard_map/ppermute | solution.py:190
  53.1 2.4 %finish.1 = (f32[4,64,512]{2,1,0:T(8,128)}, f32[4,64]{1,0:T(4,128)}) custom-call(s32[1]{0:T(128)} %bitcast.refs_0_, bf16[4,64,512]{2,1,0:T(8,128)(2,1)S(1)} %copy-done, f32[256,512]{1,0:T(8,128)S(1)} %get-tuple-element.42.refs_4_.refs_2_, f32[256,128]{1,0:T(8,128)S(1)} %get-tuple-element.43.refs_3_, f32[64,512]{1,0:T(8,128)S(1)} %mean_protos.1.refs_4_, ...), custom_call_target="tpu_custom_call" | custom-call | flops 1000000000 | tf_op jit(solution)/shard_map/finish/pallas_call | solution.py:36
  (22 shorter events, 0.4 us)
Async XLA Ops:
  0.6 9.8 %collective-permute-start.3 = (bf16[512,2048]{1,0:T(8,128)(2,1)}, bf16[512,2048]{1,0:T(8,128)(2,1)S(1)}, u32[]{:S(2)}, u32[]{:S(2)}) collective-permute-start(bf16[512,2048]{1,0:T(8,128)(2,1)} %refs_3_.2), channel_id=1, source_target_pairs={{0,4},{4,0},{1,5},{5,1},{2,6},{6,2},{3,7},{7,3},{8,12},{12,8},{9,1... | collective-permute-start | bytes 6291464 | tf_op jit(solution)/shard_map/ppermute | solution.py:190
  1.1 10.7 %collective-permute-start.1 = (bf16[64,2,512]{2,1,0:T(2,128)(2,1)}, bf16[64,2,512]{2,1,0:T(2,128)(2,1)S(1)}, u32[]{:S(2)}, u32[]{:S(2)}) collective-permute-start(bf16[64,2,512]{2,1,0:T(2,128)(2,1)} %refs_0_.1), channel_id=1, source_target_pairs={{0,16},{8,24},{16,0},{24,8},{1,17},{9,25},{17,1},{25,9},{2,18},{10... | collective-permute-start | bytes 393224 | tf_op jit(solution)/shard_map/ppermute | solution.py:190
  3.7 8.1 %collective-permute-start = (bf16[64,2,512]{2,1,0:T(2,128)(2,1)}, bf16[64,2,512]{2,1,0:T(2,128)(2,1)S(1)}, u32[]{:S(2)}, u32[]{:S(2)}) collective-permute-start(bf16[64,2,512]{2,1,0:T(2,128)(2,1)} %refs_0_.1), channel_id=1, source_target_pairs={{0,8},{8,0},{16,24},{24,16},{1,9},{9,1},{17,25},{25,17},{2,10},{10... | collective-permute-start | bytes 393224 | tf_op jit(solution)/shard_map/ppermute | solution.py:190
  5.2 6.8 %collective-permute-start.2 = (bf16[64,2,512]{2,1,0:T(2,128)(2,1)}, bf16[64,2,512]{2,1,0:T(2,128)(2,1)S(1)}, u32[]{:S(2)}, u32[]{:S(2)}) collective-permute-start(bf16[64,2,512]{2,1,0:T(2,128)(2,1)} %refs_0_.1), channel_id=1, source_target_pairs={{0,24},{8,16},{16,8},{24,0},{1,25},{9,17},{17,9},{25,1},{2,26},{10... | collective-permute-start | bytes 393224 | tf_op jit(solution)/shard_map/ppermute | solution.py:190
  5.3 0.9 %copy-start = (bf16[4,64,512]{2,1,0:T(8,128)(2,1)S(1)}, bf16[4,64,512]{2,1,0:T(8,128)(2,1)}, u32[]{:S(2)}) copy-start(bf16[4,64,512]{2,1,0:T(8,128)(2,1)} %refs_1_.3) | copy-start | bytes 786436
  10.4 1.6 %copy-start.1 = (bf16[64,2,512]{2,1,0:T(2,128)(2,1)S(1)}, bf16[64,2,512]{2,1,0:T(2,128)(2,1)}, u32[]{:S(2)}) copy-start(bf16[64,2,512]{2,1,0:T(2,128)(2,1)} %refs_0_.1) | copy-start | bytes 393220
  14.5 1.8 %collective-permute-start.4 = (f32[1,1,512]{2,1,0:T(1,128)S(1)}, f32[1,1,512]{2,1,0:T(1,128)S(1)}, u32[]{:S(2)}, u32[]{:S(2)}) collective-permute-start(f32[1,1,512]{2,1,0:T(1,128)S(1)} %get-tuple-element.27.refs_0_), channel_id=1, source_target_pairs={{0,4},{4,0},{1,5},{5,1},{2,6},{6,2},{3,7},{7,3},{8,12},{12,8},{9,1... | collective-permute-start | bytes 6152 | tf_op jit(solution)/shard_map/ppermute | solution.py:190
  16.3 4.7 %collective-permute-start.5 = (s16[272,128]{1,0:T(8,128)(2,1)S(1)}, s16[272,128]{1,0:T(8,128)(2,1)S(1)}, u32[]{:S(2)}, u32[]{:S(2)}) collective-permute-start(s16[272,128]{1,0:T(8,128)(2,1)S(1)} %get-tuple-element.33), channel_id=1, source_target_pairs={{0,1},{1,0},{2,3},{3,2},{4,5},{5,4},{6,7},{7,6},{8,9},{9,8},{10,11... | collective-permute-start | bytes 208904 | tf_op jit(solution)/shard_map/ppermute | solution.py:190
  18.2 7.9 %collective-permute-start.6 = (s16[272,128]{1,0:T(8,128)(2,1)S(1)}, s16[272,128]{1,0:T(8,128)(2,1)S(1)}, u32[]{:S(2)}, u32[]{:S(2)}) collective-permute-start(s16[272,128]{1,0:T(8,128)(2,1)S(1)} %get-tuple-element.34), channel_id=1, source_target_pairs={{0,2},{1,3},{2,0},{3,1},{4,6},{5,7},{6,4},{7,5},{8,10},{9,11},{10,... | collective-permute-start | bytes 208904 | tf_op jit(solution)/shard_map/ppermute | solution.py:190
  20.8 6.2 %collective-permute-start.7 = (s16[272,128]{1,0:T(8,128)(2,1)S(1)}, s16[272,128]{1,0:T(8,128)(2,1)S(1)}, u32[]{:S(2)}, u32[]{:S(2)}) collective-permute-start(s16[272,128]{1,0:T(8,128)(2,1)S(1)} %get-tuple-element.35), channel_id=1, source_target_pairs={{0,3},{1,2},{2,1},{3,0},{4,7},{5,6},{6,5},{7,4},{8,11},{9,10},{10,... | collective-permute-start | bytes 208904 | tf_op jit(solution)/shard_map/ppermute | solution.py:190
  28.3 1.2 %collective-permute-start.8 = (f32[1,1,512]{2,1,0:T(1,128)S(1)}, f32[1,1,512]{2,1,0:T(1,128)S(1)}, u32[]{:S(2)}, u32[]{:S(2)}) collective-permute-start(f32[1,1,512]{2,1,0:T(1,128)S(1)} %get-tuple-element.36.refs_0_), channel_id=1, source_target_pairs={{0,4},{4,0},{1,5},{5,1},{2,6},{6,2},{3,7},{7,3},{8,12},{12,8},{9,1... | collective-permute-start | bytes 6152 | tf_op jit(solution)/shard_map/ppermute | solution.py:190
  29.5 6.5 %collective-permute-start.11 = (s16[272,128]{1,0:T(8,128)(2,1)S(1)}, s16[272,128]{1,0:T(8,128)(2,1)S(1)}, u32[]{:S(2)}, u32[]{:S(2)}) collective-permute-start(s16[272,128]{1,0:T(8,128)(2,1)S(1)} %pack_sums.3.refs_3_.refs_4_), channel_id=1, source_target_pairs={{0,3},{1,2},{2,1},{3,0},{4,7},{5,6},{6,5},{7,4},{8,11},{9,10},{10,... | collective-permute-start | bytes 208904 | tf_op jit(solution)/shard_map/ppermute | solution.py:190
  32.2 7.1 %collective-permute-start.10 = (s16[272,128]{1,0:T(8,128)(2,1)S(1)}, s16[272,128]{1,0:T(8,128)(2,1)S(1)}, u32[]{:S(2)}, u32[]{:S(2)}) collective-permute-start(s16[272,128]{1,0:T(8,128)(2,1)S(1)} %pack_sums.3.refs_3_.refs_4_), channel_id=1, source_target_pairs={{0,2},{1,3},{2,0},{3,1},{4,6},{5,7},{6,4},{7,5},{8,10},{9,11},{10,... | collective-permute-start | bytes 208904 | tf_op jit(solution)/shard_map/ppermute | solution.py:190
  32.5 6.8 %collective-permute-start.9 = (s16[272,128]{1,0:T(8,128)(2,1)S(1)}, s16[272,128]{1,0:T(8,128)(2,1)S(1)}, u32[]{:S(2)}, u32[]{:S(2)}) collective-permute-start(s16[272,128]{1,0:T(8,128)(2,1)S(1)} %pack_sums.3.refs_3_.refs_4_), channel_id=1, source_target_pairs={{0,1},{1,0},{2,3},{3,2},{4,5},{5,4},{6,7},{7,6},{8,9},{9,8},{10,11... | collective-permute-start | bytes 208904 | tf_op jit(solution)/shard_map/ppermute | solution.py:190
  40.6 6.1 %copy-start.2 = (s32[4,64]{1,0:T(4,128)S(1)}, s32[4,64]{1,0:T(4,128)}, u32[]{:S(2)}) copy-start(s32[4,64]{1,0:T(4,128)} %refs_2_.1) | copy-start | bytes 3076
  40.6 6.1 %copy-start.3 = (bf16[4,64]{1,0:T(4,128)(2,1)S(1)}, bf16[4,64]{1,0:T(4,128)(2,1)}, u32[]{:S(2)}) copy-start(bf16[4,64]{1,0:T(4,128)(2,1)} %refs_3_.3) | copy-start | bytes 1540
  40.6 1.5 %collective-permute-start.12 = (f32[64,640]{1,0:T(8,128)S(1)}, f32[64,640]{1,0:T(8,128)S(1)}, u32[]{:S(2)}, u32[]{:S(2)}) collective-permute-start(f32[64,640]{1,0:T(8,128)S(1)} %get-tuple-element.41), channel_id=1, source_target_pairs={{0,4},{4,0},{1,5},{5,1},{2,6},{6,2},{3,7},{7,3},{8,12},{12,8},{9,1... | collective-permute-start | bytes 491528 | tf_op jit(solution)/shard_map/ppermute | solution.py:190
  42.3 6.9 %collective-permute-start.15 = (s16[272,128]{1,0:T(8,128)(2,1)S(1)}, s16[272,128]{1,0:T(8,128)(2,1)S(1)}, u32[]{:S(2)}, u32[]{:S(2)}) collective-permute-start(s16[272,128]{1,0:T(8,128)(2,1)S(1)} %code_mixed.1.refs_8_.refs_0_), channel_id=1, source_target_pairs={{0,3},{1,2},{2,1},{3,0},{4,7},{5,6},{6,5},{7,4},{8,11},{9,10},{10,... | collective-permute-start | bytes 208904 | tf_op jit(solution)/shard_map/ppermute | solution.py:190
  44.8 6.6 %collective-permute-start.14 = (s16[272,128]{1,0:T(8,128)(2,1)S(1)}, s16[272,128]{1,0:T(8,128)(2,1)S(1)}, u32[]{:S(2)}, u32[]{:S(2)}) collective-permute-start(s16[272,128]{1,0:T(8,128)(2,1)S(1)} %code_mixed.1.refs_8_.refs_0_), channel_id=1, source_target_pairs={{0,2},{1,3},{2,0},{3,1},{4,6},{5,7},{6,4},{7,5},{8,10},{9,11},{10,... | collective-permute-start | bytes 208904 | tf_op jit(solution)/shard_map/ppermute | solution.py:190
  44.8 6.6 %collective-permute-start.13 = (s16[272,128]{1,0:T(8,128)(2,1)S(1)}, s16[272,128]{1,0:T(8,128)(2,1)S(1)}, u32[]{:S(2)}, u32[]{:S(2)}) collective-permute-start(s16[272,128]{1,0:T(8,128)(2,1)S(1)} %code_mixed.1.refs_8_.refs_0_), channel_id=1, source_target_pairs={{0,1},{1,0},{2,3},{3,2},{4,5},{5,4},{6,7},{7,6},{8,9},{9,8},{10,11... | collective-permute-start | bytes 208904 | tf_op jit(solution)/shard_map/ppermute | solution.py:190
  51.7 1.4 %collective-permute-start.16 = (f32[64,512]{1,0:T(8,128)S(1)}, f32[64,512]{1,0:T(8,128)S(1)}, u32[]{:S(2)}, u32[]{:S(2)}) collective-permute-start(f32[64,512]{1,0:T(8,128)S(1)} %mean_protos.1.refs_4_), channel_id=1, source_target_pairs={{0,4},{4,0},{1,5},{5,1},{2,6},{6,2},{3,7},{7,3},{8,12},{12,8},{9,1... | collective-permute-start | bytes 393224 | tf_op jit(solution)/shard_map/ppermute | solution.py:190

commit v8 on v7

--- a/solution.py
+++ b/solution.py
@@ -26,7 +26,7 @@
 IN_SMEM = pl.BlockSpec(memory_space=pltpu.SMEM)
 
 
-def call(kernel, name, out_shape, scratch=(), scalars=0, vmem=16, after=(), flops=10**9, aliases=None, far=(), far_out=()):
+def call(kernel, name, out_shape, scratch=(), scalars=0, vmem=16, after=(), flops=10**9, aliases=None, far=()):
     def run(*operands):
         count = len(operands)
 
@@ -38,9 +38,7 @@
             in_specs=[IN_SMEM] * scalars
             + [IN_HBM if i in far else IN_VMEM for i in range(scalars, count)]
             + [pl.BlockSpec(memory_space=pl.ANY)] * len(after),
-            out_specs=[IN_HBM if i in far_out else IN_VMEM for i in range(len(out_shape))]
-            if isinstance(out_shape, list)
-            else IN_VMEM,
+            out_specs=jax.tree.map(lambda _: IN_VMEM, out_shape),
             out_shape=out_shape,
             scratch_shapes=list(scratch),
             compiler_params=pltpu.CompilerParams(vmem_limit_bytes=vmem * 1024 * 1024),
@@ -375,9 +373,8 @@
     return 1.0 / jnp.sum(weighted, axis=0, keepdims=True)
 
 
-def sweep_kernel(count, share_rows, plan, *refs):
-    shares, refs = refs[:count], refs[count:]
-    sum_refs, (sums, share, _, row_scale, partial) = refs[:-5] or shares, refs[-5:]
+def sweep_kernel(plan, *refs):
+    sum_refs, (sums, _, row_scale, partial) = refs[:-4], refs[-4:]
     scale_rows(sum_refs, row_scale)
     for start in range(0, plan.shape[1], LANES):
         terms = plan[:, start : start + LANES] * column_scale(plan, row_scale, start)
@@ -386,19 +383,28 @@
         else:
             partial[...] += terms
     store_sums(sums, partial)
-    back, totals = decode_sum(shares, share_rows)
+
+
+def sweep_call(plan, copies, row_sums):
+    rows = plan.shape[0]
+    return call(
+        sweep_kernel,
+        "sweep",
+        [shape((copies, 1, rows)), shape(plan.shape)],
+        [pltpu.VMEM((rows, LANES), F32)] * 2,
+        aliases={0: 1},
+    )(plan, *row_sums)
+
+
+def total_kernel(rows, *refs):
+    shares, share = refs[:-1], refs[-1]
+    back, totals = decode_sum(shares, rows)
     store_code(share, back / totals, totals)
 
 
-def sweep_call(plan, copies, share_rows, shares, row_sums):
-    rows = plan.shape[0]
-    return call(
-        functools.partial(sweep_kernel, len(shares), share_rows),
-        "sweep",
-        [shape((copies, 1, rows)), shape(shares[0].shape, I16), shape(plan.shape)],
-        [pltpu.VMEM((rows, LANES), F32)] * 2,
-        aliases={0: 2},
-    )(plan, *shares, *row_sums)
+def total_call(shares, rows, after):
+    out = shape(shares[0].shape, I16)
+    return call(functools.partial(total_kernel, rows), "student_totals", out, after=after)(*shares)
 
 
 def last_kernel(share, count, block, place, plan, unit_protos, *refs):
@@ -519,8 +525,7 @@
 
 
 def finish_kernel(views, place, feats, base, fields, *refs):
-    parts, (gradient, loss, means, ready, sems) = refs[:-5], refs[-5:]
-    copies = []
+    parts, (gradient, loss, means) = refs[:-3], refs[-3:]
     rows = parts[0].shape[0]
     for k, part in enumerate(parts):
         first = pl.multiple_of(jnp.bitwise_xor(place[0], k) * rows, rows)
@@ -535,14 +540,10 @@
         for view in range(1, views):
             chosen = jnp.where(view_column == view, means[view * images : (view + 1) * images, :], chosen)
         along = cubic * lane_sums(raw * chosen)
-        ready[crop] = base[here, :] - factor * chosen + along * raw
-        copies.append(pltpu.make_async_copy(ready.at[crop], gradient.at[crop], sems.at[crop]))
-        copies[-1].start()
+        gradient[crop] = base[here, :] - factor * chosen + along * raw
         unit = (raw * scales).astype(BF16).astype(F32)
         column = fields[here, FIELDS - 1 : FIELDS] - lane_sums(unit * chosen) * (1.0 / student_softness)
         loss[crop : crop + 1, :] = jnp.broadcast_to(column, (images, LANES)).T[:1, :]
-    for copy in copies:
-        copy.wait()
 
 
 def finish_call(views, place, feats, base, fields, means):
@@ -551,13 +552,8 @@
         functools.partial(finish_kernel, views),
         "finish",
         [shape((crops, images, width)), shape((crops, images))],
-        [
-            pltpu.VMEM((views * images, width), F32),
-            pltpu.VMEM((crops, images, width), F32),
-            pltpu.SemaphoreType.DMA((crops,)),
-        ],
+        [pltpu.VMEM((views * images, width), F32)],
         scalars=1,
-        far_out=[0],
     )(place, feats, base, fields, *means)
 
 
@@ -599,8 +595,8 @@
     shares = other_call(proto_place, unit_feats, back, protos[1:], pieces, half, block)
     for _ in range(SWEEPS - 2):
         shares, row_sums = exchange(sums, shares)
-        sums, share, plan = sweep_call(plan, copies, crops * images // pieces, shares, row_sums)
-        shares = [share]
+        sums, plan = sweep_call(plan, copies, row_sums or shares)
+        shares = [total_call(shares, crops * images // pieces, [sums])]
     if joint:
         shares, row_sums = exchange(sums, shares)
     else:

time: 55.7 us -> 54.7 us (0.982)
    pallas_call x12 -> x13, Pallas kernels: 16.4 us -> 16 us  [run(): pl.pallas_call(body, in_specs=[IN_SMEM] * scalars + [IN_HBM if i in far e...]
  transfers between devices with their start and end apart: 17 -> 17, of which waited for: 11 -> 11; matrix products, arithmetic and copies ran while one was open for 0% -> 0% of each run, Pallas kernels for 15% -> 16%
where the time goes in v8:
time: 54.7 us; the launch traced here: 54.6 us
  waiting for transfers between devices  18.6 us (34%)
  starting transfers between devices  18.3 us (33%)
  Pallas kernels  16 us (29%)
  local copies, waits for them, and re-layouts  0.97 us (2%)
  between operations  0.79 us (1%)
    ppermute x17, waiting for transfers between devices, swap(): return lax.ppermute(values, axis, [(i, i ^ distance) for i in range(count)])  18.6 us
    ppermute x17, starting transfers between devices, swap(): return lax.ppermute(values, axis, [(i, i ^ distance) for i in range(count)])  18.3 us
    pallas_call x13, Pallas kernels, run(): pl.pallas_call(body, in_specs=[IN_SMEM] * scalars + [IN_HBM if i in far e...  16 us
  transfers between devices with their start and end apart: 17, of which 11 were waited for; matrix products, arithmetic and copies ran while one was open for 0% of the time, Pallas kernels for 16%

profile of v8, /device:TPU:0, one launch (start us, length us, event | category | flops | bytes accessed | tf_op | source)
XLA Modules:
  0.0 54.6 jit_solution(4357936633580968264)
XLA Ops:
  0.6 0.5 collective-permute-start.3
  1.1 2.6 %collective-permute-start.1 = (bf16[64,2,512]{2,1,0:T(2,128)(2,1)}, bf16[64,2,512]{2,1,0:T(2,128)(2,1)S(1)}, u32[]{:S(2)}, u32[]{:S(2)}) collective-permute-start(bf16[64,2,512]{2,1,0:T(2,128)(2,1)} %refs_0_.1), channel_id=1, source_target_pairs={{0,16},{8,24},{16,0},{24,8},{1,17},{9,25},{17,1},{25,9},{2,18},{10... | collective-permute-start | bytes 393224 | tf_op jit(solution)/shard_map/ppermute | solution.py:188
  3.7 1.5 %collective-permute-start = (bf16[64,2,512]{2,1,0:T(2,128)(2,1)}, bf16[64,2,512]{2,1,0:T(2,128)(2,1)S(1)}, u32[]{:S(2)}, u32[]{:S(2)}) collective-permute-start(bf16[64,2,512]{2,1,0:T(2,128)(2,1)} %refs_0_.1), channel_id=1, source_target_pairs={{0,8},{8,0},{16,24},{24,16},{1,9},{9,1},{17,25},{25,17},{2,10},{10... | collective-permute-start | bytes 393224 | tf_op jit(solution)/shard_map/ppermute | solution.py:188
  5.3 0.9 %copy-done = bf16[4,64,512]{2,1,0:T(8,128)(2,1)S(1)} copy-done((bf16[4,64,512]{2,1,0:T(8,128)(2,1)S(1)}, bf16[4,64,512]{2,1,0:T(8,128)(2,1)}, u32[]{:S(2)}) %copy-start) | copy-done | bytes 262168
  6.2 4.2 %student_own.1 = (bf16[512,2048]{1,0:T(8,128)(2,1)S(1)}, bf16[512,2048]{1,0:T(8,128)(2,1)S(1)}, bf16[256,512]{1,0:T(8,128)(2,1)S(1)}, f32[256,640]{1,0:T(8,128)S(1)}) custom-call(s32[1]{0:T(128)} %bitcast.refs_0_, s32[1]{0:T(128)} %bitcast.1.refs_1_.refs_0_, bf16[256,512]{1,0:T(8,128)(2,1)S(1)} %bitcast.3, bf16[512,2048]{1,0:T(8,128)(2,1)} %refs_3_.2, ...), custom_call_target="tpu_custom_call" | custom-call | flops 1073741824 | tf_op jit(solution)/shard_map/student_own/pallas_call | solution.py:36
  10.5 1.3 %student_begin.1.refs_5_.refs_2_ = f32[256,640]{1,0:T(8,128)S(1)} custom-call(bf16[256,512]{1,0:T(8,128)(2,1)S(1)} %get-tuple-element.23.refs_0_.refs_1_, f32[256,640]{1,0:T(8,128)S(1)} %get-tuple-element.24.refs_1_, bf16[512,2048]{1,0:T(8,128)(2,1)S(1)} %collective-permute-done.3.refs_2_.refs_3_), custom_call_target="tpu_custom_call" | custom-call | flops 536870912 | tf_op jit(solution)/shard_map/student_begin/pallas_call | solution.py:36
  11.8 0.2 collective-permute-done.2.refs_3_
  12.1 2.4 %first_sweep.1 = (f32[512,2048]{1,0:T(8,128)S(1)}, f32[1,1,512]{2,1,0:T(1,128)S(1)}) custom-call(bf16[64,2,512]{2,1,0:T(2,128)(2,1)S(1)} %copy-done.1, bf16[64,2,512]{2,1,0:T(2,128)(2,1)S(1)} %collective-permute-done.refs_1_, bf16[64,2,512]{2,1,0:T(2,128)(2,1)S(1)} %collective-permute-done.1.refs_2_, bf16[64,2,512]{2,1,0:T(2,128)(2,1)S(1)} %collective-permute-done.2.refs_3_, ...), custom_call_target="tpu_custom_call" | custom-call | flops 4294967296 | tf_op jit(solution)/shard_map/first_sweep/pallas_call | solution.py:36
  14.5 1.7 %student_other.1 = (s16[272,128]{1,0:T(8,128)(2,1)S(1)}, s16[272,128]{1,0:T(8,128)(2,1)S(1)}, s16[272,128]{1,0:T(8,128)(2,1)S(1)}, s16[272,128]{1,0:T(8,128)(2,1)S(1)}) custom-call(s32[1]{0:T(128)} %bitcast.1.refs_1_.refs_0_, bf16[256,512]{1,0:T(8,128)(2,1)S(1)} %get-tuple-element.23.refs_0_.refs_1_, f32[256,640]{1,0:T(8,128)S(1)} %student_begin.1.refs_5_.refs_2_, ...), custom_call_target="tpu_custom_call" | custom-call | flops 1073741824 | tf_op jit(solution)/shard_map/student_other/pallas_call | solution.py:36
  16.3 1.9 %collective-permute-start.5 = (s16[272,128]{1,0:T(8,128)(2,1)S(1)}, s16[272,128]{1,0:T(8,128)(2,1)S(1)}, u32[]{:S(2)}, u32[]{:S(2)}) collective-permute-start(s16[272,128]{1,0:T(8,128)(2,1)S(1)} %get-tuple-element.32), channel_id=1, source_target_pairs={{0,1},{1,0},{2,3},{3,2},{4,5},{5,4},{6,7},{7,6},{8,9},{9,8},{10,11... | collective-permute-start | bytes 208904 | tf_op jit(solution)/shard_map/ppermute | solution.py:188
  18.2 2.6 %collective-permute-start.6 = (s16[272,128]{1,0:T(8,128)(2,1)S(1)}, s16[272,128]{1,0:T(8,128)(2,1)S(1)}, u32[]{:S(2)}, u32[]{:S(2)}) collective-permute-start(s16[272,128]{1,0:T(8,128)(2,1)S(1)} %get-tuple-element.33), channel_id=1, source_target_pairs={{0,2},{1,3},{2,0},{3,1},{4,6},{5,7},{6,4},{7,5},{8,10},{9,11},{10,... | collective-permute-start | bytes 208904 | tf_op jit(solution)/shard_map/ppermute | solution.py:188
  20.8 0.2 collective-permute-done.5.refs_2_.refs_1_
  21.0 5.1 %collective-permute-done.6.refs_3_.refs_2_ = s16[272,128]{1,0:T(8,128)(2,1)S(1)} collective-permute-done((s16[272,128]{1,0:T(8,128)(2,1)S(1)}, s16[272,128]{1,0:T(8,128)(2,1)S(1)}, u32[]{:S(2)}, u32[]{:S(2)}) %collective-permute-start.6) | collective-permute-done | bytes 69664 | tf_op jit(solution)/shard_map/ppermute | solution.py:188
  26.1 0.9 %collective-permute-done.7.refs_4_.refs_3_ = s16[272,128]{1,0:T(8,128)(2,1)S(1)} collective-permute-done((s16[272,128]{1,0:T(8,128)(2,1)S(1)}, s16[272,128]{1,0:T(8,128)(2,1)S(1)}, u32[]{:S(2)}, u32[]{:S(2)}) %collective-permute-start.7) | collective-permute-done | bytes 69664 | tf_op jit(solution)/shard_map/ppermute | solution.py:188
  27.0 1.0 %sweep.1 = (f32[1,1,512]{2,1,0:T(1,128)S(1)}, f32[512,2048]{1,0:T(8,128)S(1)}) custom-call(f32[512,2048]{1,0:T(8,128)S(1)} %get-tuple-element.25.refs_0_, s16[272,128]{1,0:T(8,128)(2,1)S(1)} %get-tuple-element.31.refs_1_.refs_0_, s16[272,128]{1,0:T(8,128)(2,1)S(1)} %collective-permute-done.5.refs_2_.refs_1_, ...), custom_call_target="tpu_custom_call", output_to_operand_aliasing={{1}: (0, {})} | custom-call | flops 1000000000 | tf_op jit(solution)/shard_map/sweep/pallas_call | solution.py:36
  28.0 0.5 %student_totals.1.refs_2_ = s16[272,128]{1,0:T(8,128)(2,1)S(1)} custom-call(s16[272,128]{1,0:T(8,128)(2,1)S(1)} %get-tuple-element.31.refs_1_.refs_0_, s16[272,128]{1,0:T(8,128)(2,1)S(1)} %collective-permute-done.5.refs_2_.refs_1_, s16[272,128]{1,0:T(8,128)(2,1)S(1)} %collective-permute-done.6.refs_3_.refs_2_, ...), custom_call_target="tpu_custom_call" | custom-call | flops 1000000000 | tf_op jit(solution)/shard_map/student_totals/pallas_call | solution.py:36
  28.6 0.6 %collective-permute-done.8.refs_1_ = f32[1,1,512]{2,1,0:T(1,128)S(1)} collective-permute-done((f32[1,1,512]{2,1,0:T(1,128)S(1)}, f32[1,1,512]{2,1,0:T(1,128)S(1)}, u32[]{:S(2)}, u32[]{:S(2)}) %collective-permute-start.8) | collective-permute-done | bytes 2080 | tf_op jit(solution)/shard_map/ppermute | solution.py:188
  29.2 2.7 %collective-permute-start.11 = (s16[272,128]{1,0:T(8,128)(2,1)S(1)}, s16[272,128]{1,0:T(8,128)(2,1)S(1)}, u32[]{:S(2)}, u32[]{:S(2)}) collective-permute-start(s16[272,128]{1,0:T(8,128)(2,1)S(1)} %pack_sums.3.refs_3_.refs_4_), channel_id=1, source_target_pairs={{0,3},{1,2},{2,1},{3,0},{4,7},{5,6},{6,5},{7,4},{8,11},{9,10},{10,... | collective-permute-start | bytes 208904 | tf_op jit(solution)/shard_map/ppermute | solution.py:188
  31.9 0.3 collective-permute-start.10
  32.2 1.4 %collective-permute-start.9 = (s16[272,128]{1,0:T(8,128)(2,1)S(1)}, s16[272,128]{1,0:T(8,128)(2,1)S(1)}, u32[]{:S(2)}, u32[]{:S(2)}) collective-permute-start(s16[272,128]{1,0:T(8,128)(2,1)S(1)} %pack_sums.3.refs_3_.refs_4_), channel_id=1, source_target_pairs={{0,1},{1,0},{2,3},{3,2},{4,5},{5,4},{6,7},{7,6},{8,9},{9,8},{10,11... | collective-permute-start | bytes 208904 | tf_op jit(solution)/shard_map/ppermute | solution.py:188
  33.7 2.1 %collective-permute-done.11.refs_6_.refs_7_ = s16[272,128]{1,0:T(8,128)(2,1)S(1)} collective-permute-done((s16[272,128]{1,0:T(8,128)(2,1)S(1)}, s16[272,128]{1,0:T(8,128)(2,1)S(1)}, u32[]{:S(2)}, u32[]{:S(2)}) %collective-permute-start.11) | collective-permute-done | bytes 69664 | tf_op jit(solution)/shard_map/ppermute | solution.py:188
  35.7 3.2 %collective-permute-done.10.refs_5_.refs_6_ = s16[272,128]{1,0:T(8,128)(2,1)S(1)} collective-permute-done((s16[272,128]{1,0:T(8,128)(2,1)S(1)}, s16[272,128]{1,0:T(8,128)(2,1)S(1)}, u32[]{:S(2)}, u32[]{:S(2)}) %collective-permute-start.10) | collective-permute-done | bytes 69664 | tf_op jit(solution)/shard_map/ppermute | solution.py:188
  39.0 1.4 %last_sweep.1 = (f32[64,640]{1,0:T(8,128)S(1)}, f32[64,640]{1,0:T(8,128)S(1)}) custom-call(s32[1]{0:T(128)} %bitcast.refs_0_, f32[512,2048]{1,0:T(8,128)S(1)} %get-tuple-element.36.refs_1_, bf16[512,2048]{1,0:T(8,128)(2,1)S(1)} %get-tuple-element.37.refs_2_, s16[272,128]{1,0:T(8,128)(2,1)S(1)} %pack_sums.3.refs_3_.refs_4_, ...), custom_call_target="tpu_custom_call" | custom-call | flops 1000000000 | tf_op jit(solution)/shard_map/last_sweep/pallas_call | solution.py:36
  40.4 1.4 %collective-permute-done.12.refs_1_ = f32[64,640]{1,0:T(8,128)S(1)} collective-permute-done((f32[64,640]{1,0:T(8,128)S(1)}, f32[64,640]{1,0:T(8,128)S(1)}, u32[]{:S(2)}, u32[]{:S(2)}) %collective-permute-start.12) | collective-permute-done | bytes 163872 | tf_op jit(solution)/shard_map/ppermute | solution.py:188
  42.0 2.5 %collective-permute-start.15 = (s16[272,128]{1,0:T(8,128)(2,1)S(1)}, s16[272,128]{1,0:T(8,128)(2,1)S(1)}, u32[]{:S(2)}, u32[]{:S(2)}) collective-permute-start(s16[272,128]{1,0:T(8,128)(2,1)S(1)} %code_mixed.1.refs_8_.refs_0_), channel_id=1, source_target_pairs={{0,3},{1,2},{2,1},{3,0},{4,7},{5,6},{6,5},{7,4},{8,11},{9,10},{10,... | collective-permute-start | bytes 208904 | tf_op jit(solution)/shard_map/ppermute | solution.py:188
  44.5 1.9 %collective-permute-start.13 = (s16[272,128]{1,0:T(8,128)(2,1)S(1)}, s16[272,128]{1,0:T(8,128)(2,1)S(1)}, u32[]{:S(2)}, u32[]{:S(2)}) collective-permute-start(s16[272,128]{1,0:T(8,128)(2,1)S(1)} %code_mixed.1.refs_8_.refs_0_), channel_id=1, source_target_pairs={{0,1},{1,0},{2,3},{3,2},{4,5},{5,4},{6,7},{7,6},{8,9},{9,8},{10,11... | collective-permute-start | bytes 208904 | tf_op jit(solution)/shard_map/ppermute | solution.py:188
  46.4 1.0 %prepare.1 = (f32[256,512]{1,0:T(8,128)S(1)}, f32[256,128]{1,0:T(8,128)S(1)}) custom-call(s32[1]{0:T(128)} %bitcast.1.refs_1_.refs_0_, bf16[4,64,512]{2,1,0:T(8,128)(2,1)S(1)} %copy-done, s32[4,64]{1,0:T(4,128)S(1)} %copy-done.2, bf16[4,64]{1,0:T(4,128)(2,1)S(1)} %copy-done.3, s16[272,128]{1,0:T(8,128)(2,1)S(1)} %pack_sums.3.refs_3_.refs_4_, ...), custom_call_target="tpu_custom_call" | custom-call | flops 1000000000 | tf_op jit(solution)/shard_map/prepare/pallas_call | solution.py:36
  47.5 1.4 %collective-permute-done.15.refs_3_ = s16[272,128]{1,0:T(8,128)(2,1)S(1)} collective-permute-done((s16[272,128]{1,0:T(8,128)(2,1)S(1)}, s16[272,128]{1,0:T(8,128)(2,1)S(1)}, u32[]{:S(2)}, u32[]{:S(2)}) %collective-permute-start.15) | collective-permute-done | bytes 69664 | tf_op jit(solution)/shard_map/ppermute | solution.py:188
  48.9 2.1 %collective-permute-done.14.refs_2_ = s16[272,128]{1,0:T(8,128)(2,1)S(1)} collective-permute-done((s16[272,128]{1,0:T(8,128)(2,1)S(1)}, s16[272,128]{1,0:T(8,128)(2,1)S(1)}, u32[]{:S(2)}, u32[]{:S(2)}) %collective-permute-start.14) | collective-permute-done | bytes 69664 | tf_op jit(solution)/shard_map/ppermute | solution.py:188
  51.1 0.4 mean_protos.1.refs_4_
  51.5 1.3 %collective-permute-done.16.refs_5_ = f32[64,512]{1,0:T(8,128)S(1)} collective-permute-done((f32[64,512]{1,0:T(8,128)S(1)}, f32[64,512]{1,0:T(8,128)S(1)}, u32[]{:S(2)}, u32[]{:S(2)}) %collective-permute-start.16) | collective-permute-done | bytes 131104 | tf_op jit(solution)/shard_map/ppermute | solution.py:188
  52.9 1.7 %finish.1 = (f32[4,64,512]{2,1,0:T(8,128)}, f32[4,64]{1,0:T(4,128)}) custom-call(s32[1]{0:T(128)} %bitcast.refs_0_, bf16[4,64,512]{2,1,0:T(8,128)(2,1)S(1)} %copy-done, f32[256,512]{1,0:T(8,128)S(1)} %get-tuple-element.40.refs_4_.refs_2_, f32[256,128]{1,0:T(8,128)S(1)} %get-tuple-element.41.refs_3_, f32[64,512]{1,0:T(8,128)S(1)} %mean_protos.1.refs_4_, ...), custom_call_target="tpu_custom_call" | custom-call | flops 1000000000 | tf_op jit(solution)/shard_map/finish/pallas_call | solution.py:36
  (23 shorter events, 0.7 us)
Async XLA Ops:
  0.6 9.8 %collective-permute-start.3 = (bf16[512,2048]{1,0:T(8,128)(2,1)}, bf16[512,2048]{1,0:T(8,128)(2,1)S(1)}, u32[]{:S(2)}, u32[]{:S(2)}) collective-permute-start(bf16[512,2048]{1,0:T(8,128)(2,1)} %refs_3_.2), channel_id=1, source_target_pairs={{0,4},{4,0},{1,5},{5,1},{2,6},{6,2},{3,7},{7,3},{8,12},{12,8},{9,1... | collective-permute-start | bytes 6291464 | tf_op jit(solution)/shard_map/ppermute | solution.py:188
  1.1 10.7 %collective-permute-start.1 = (bf16[64,2,512]{2,1,0:T(2,128)(2,1)}, bf16[64,2,512]{2,1,0:T(2,128)(2,1)S(1)}, u32[]{:S(2)}, u32[]{:S(2)}) collective-permute-start(bf16[64,2,512]{2,1,0:T(2,128)(2,1)} %refs_0_.1), channel_id=1, source_target_pairs={{0,16},{8,24},{16,0},{24,8},{1,17},{9,25},{17,1},{25,9},{2,18},{10... | collective-permute-start | bytes 393224 | tf_op jit(solution)/shard_map/ppermute | solution.py:188
  3.7 8.1 %collective-permute-start = (bf16[64,2,512]{2,1,0:T(2,128)(2,1)}, bf16[64,2,512]{2,1,0:T(2,128)(2,1)S(1)}, u32[]{:S(2)}, u32[]{:S(2)}) collective-permute-start(bf16[64,2,512]{2,1,0:T(2,128)(2,1)} %refs_0_.1), channel_id=1, source_target_pairs={{0,8},{8,0},{16,24},{24,16},{1,9},{9,1},{17,25},{25,17},{2,10},{10... | collective-permute-start | bytes 393224 | tf_op jit(solution)/shard_map/ppermute | solution.py:188
  5.2 6.8 %collective-permute-start.2 = (bf16[64,2,512]{2,1,0:T(2,128)(2,1)}, bf16[64,2,512]{2,1,0:T(2,128)(2,1)S(1)}, u32[]{:S(2)}, u32[]{:S(2)}) collective-permute-start(bf16[64,2,512]{2,1,0:T(2,128)(2,1)} %refs_0_.1), channel_id=1, source_target_pairs={{0,24},{8,16},{16,8},{24,0},{1,25},{9,17},{17,9},{25,1},{2,26},{10... | collective-permute-start | bytes 393224 | tf_op jit(solution)/shard_map/ppermute | solution.py:188
  5.3 0.9 %copy-start = (bf16[4,64,512]{2,1,0:T(8,128)(2,1)S(1)}, bf16[4,64,512]{2,1,0:T(8,128)(2,1)}, u32[]{:S(2)}) copy-start(bf16[4,64,512]{2,1,0:T(8,128)(2,1)} %refs_1_.3) | copy-start | bytes 786436
  10.4 1.6 %copy-start.1 = (bf16[64,2,512]{2,1,0:T(2,128)(2,1)S(1)}, bf16[64,2,512]{2,1,0:T(2,128)(2,1)}, u32[]{:S(2)}) copy-start(bf16[64,2,512]{2,1,0:T(2,128)(2,1)} %refs_0_.1) | copy-start | bytes 393220
  14.5 1.8 %collective-permute-start.4 = (f32[1,1,512]{2,1,0:T(1,128)S(1)}, f32[1,1,512]{2,1,0:T(1,128)S(1)}, u32[]{:S(2)}, u32[]{:S(2)}) collective-permute-start(f32[1,1,512]{2,1,0:T(1,128)S(1)} %get-tuple-element.26.refs_0_), channel_id=1, source_target_pairs={{0,4},{4,0},{1,5},{5,1},{2,6},{6,2},{3,7},{7,3},{8,12},{12,8},{9,1... | collective-permute-start | bytes 6152 | tf_op jit(solution)/shard_map/ppermute | solution.py:188
  16.3 4.7 %collective-permute-start.5 = (s16[272,128]{1,0:T(8,128)(2,1)S(1)}, s16[272,128]{1,0:T(8,128)(2,1)S(1)}, u32[]{:S(2)}, u32[]{:S(2)}) collective-permute-start(s16[272,128]{1,0:T(8,128)(2,1)S(1)} %get-tuple-element.32), channel_id=1, source_target_pairs={{0,1},{1,0},{2,3},{3,2},{4,5},{5,4},{6,7},{7,6},{8,9},{9,8},{10,11... | collective-permute-start | bytes 208904 | tf_op jit(solution)/shard_map/ppermute | solution.py:188
  18.2 7.9 %collective-permute-start.6 = (s16[272,128]{1,0:T(8,128)(2,1)S(1)}, s16[272,128]{1,0:T(8,128)(2,1)S(1)}, u32[]{:S(2)}, u32[]{:S(2)}) collective-permute-start(s16[272,128]{1,0:T(8,128)(2,1)S(1)} %get-tuple-element.33), channel_id=1, source_target_pairs={{0,2},{1,3},{2,0},{3,1},{4,6},{5,7},{6,4},{7,5},{8,10},{9,11},{10,... | collective-permute-start | bytes 208904 | tf_op jit(solution)/shard_map/ppermute | solution.py:188
  20.8 6.2 %collective-permute-start.7 = (s16[272,128]{1,0:T(8,128)(2,1)S(1)}, s16[272,128]{1,0:T(8,128)(2,1)S(1)}, u32[]{:S(2)}, u32[]{:S(2)}) collective-permute-start(s16[272,128]{1,0:T(8,128)(2,1)S(1)} %get-tuple-element.34), channel_id=1, source_target_pairs={{0,3},{1,2},{2,1},{3,0},{4,7},{5,6},{6,5},{7,4},{8,11},{9,10},{10,... | collective-permute-start | bytes 208904 | tf_op jit(solution)/shard_map/ppermute | solution.py:188
  27.9 1.2 %collective-permute-start.8 = (f32[1,1,512]{2,1,0:T(1,128)S(1)}, f32[1,1,512]{2,1,0:T(1,128)S(1)}, u32[]{:S(2)}, u32[]{:S(2)}) collective-permute-start(f32[1,1,512]{2,1,0:T(1,128)S(1)} %get-tuple-element.35.refs_4_.refs_0_), channel_id=1, source_target_pairs={{0,4},{4,0},{1,5},{5,1},{2,6},{6,2},{3,7},{7,3},{8,12},{12,8},{9,1... | collective-permute-start | bytes 6152 | tf_op jit(solution)/shard_map/ppermute | solution.py:188
  29.2 6.5 %collective-permute-start.11 = (s16[272,128]{1,0:T(8,128)(2,1)S(1)}, s16[272,128]{1,0:T(8,128)(2,1)S(1)}, u32[]{:S(2)}, u32[]{:S(2)}) collective-permute-start(s16[272,128]{1,0:T(8,128)(2,1)S(1)} %pack_sums.3.refs_3_.refs_4_), channel_id=1, source_target_pairs={{0,3},{1,2},{2,1},{3,0},{4,7},{5,6},{6,5},{7,4},{8,11},{9,10},{10,... | collective-permute-start | bytes 208904 | tf_op jit(solution)/shard_map/ppermute | solution.py:188
  31.9 7.1 %collective-permute-start.10 = (s16[272,128]{1,0:T(8,128)(2,1)S(1)}, s16[272,128]{1,0:T(8,128)(2,1)S(1)}, u32[]{:S(2)}, u32[]{:S(2)}) collective-permute-start(s16[272,128]{1,0:T(8,128)(2,1)S(1)} %pack_sums.3.refs_3_.refs_4_), channel_id=1, source_target_pairs={{0,2},{1,3},{2,0},{3,1},{4,6},{5,7},{6,4},{7,5},{8,10},{9,11},{10,... | collective-permute-start | bytes 208904 | tf_op jit(solution)/shard_map/ppermute | solution.py:188
  32.2 6.8 %collective-permute-start.9 = (s16[272,128]{1,0:T(8,128)(2,1)S(1)}, s16[272,128]{1,0:T(8,128)(2,1)S(1)}, u32[]{:S(2)}, u32[]{:S(2)}) collective-permute-start(s16[272,128]{1,0:T(8,128)(2,1)S(1)} %pack_sums.3.refs_3_.refs_4_), channel_id=1, source_target_pairs={{0,1},{1,0},{2,3},{3,2},{4,5},{5,4},{6,7},{7,6},{8,9},{9,8},{10,11... | collective-permute-start | bytes 208904 | tf_op jit(solution)/shard_map/ppermute | solution.py:188
  40.3 6.1 %copy-start.2 = (s32[4,64]{1,0:T(4,128)S(1)}, s32[4,64]{1,0:T(4,128)}, u32[]{:S(2)}) copy-start(s32[4,64]{1,0:T(4,128)} %refs_2_.1) | copy-start | bytes 3076
  40.4 6.1 %copy-start.3 = (bf16[4,64]{1,0:T(4,128)(2,1)S(1)}, bf16[4,64]{1,0:T(4,128)(2,1)}, u32[]{:S(2)}) copy-start(bf16[4,64]{1,0:T(4,128)(2,1)} %refs_3_.3) | copy-start | bytes 1540
  40.4 1.5 %collective-permute-start.12 = (f32[64,640]{1,0:T(8,128)S(1)}, f32[64,640]{1,0:T(8,128)S(1)}, u32[]{:S(2)}, u32[]{:S(2)}) collective-permute-start(f32[64,640]{1,0:T(8,128)S(1)} %get-tuple-element.39), channel_id=1, source_target_pairs={{0,4},{4,0},{1,5},{5,1},{2,6},{6,2},{3,7},{7,3},{8,12},{12,8},{9,1... | collective-permute-start | bytes 491528 | tf_op jit(solution)/shard_map/ppermute | solution.py:188
  42.0 6.9 %collective-permute-start.15 = (s16[272,128]{1,0:T(8,128)(2,1)S(1)}, s16[272,128]{1,0:T(8,128)(2,1)S(1)}, u32[]{:S(2)}, u32[]{:S(2)}) collective-permute-start(s16[272,128]{1,0:T(8,128)(2,1)S(1)} %code_mixed.1.refs_8_.refs_0_), channel_id=1, source_target_pairs={{0,3},{1,2},{2,1},{3,0},{4,7},{5,6},{6,5},{7,4},{8,11},{9,10},{10,... | collective-permute-start | bytes 208904 | tf_op jit(solution)/shard_map/ppermute | solution.py:188
  44.5 6.5 %collective-permute-start.14 = (s16[272,128]{1,0:T(8,128)(2,1)S(1)}, s16[272,128]{1,0:T(8,128)(2,1)S(1)}, u32[]{:S(2)}, u32[]{:S(2)}) collective-permute-start(s16[272,128]{1,0:T(8,128)(2,1)S(1)} %code_mixed.1.refs_8_.refs_0_), channel_id=1, source_target_pairs={{0,2},{1,3},{2,0},{3,1},{4,6},{5,7},{6,4},{7,5},{8,10},{9,11},{10,... | collective-permute-start | bytes 208904 | tf_op jit(solution)/shard_map/ppermute | solution.py:188
  44.5 6.5 %collective-permute-start.13 = (s16[272,128]{1,0:T(8,128)(2,1)S(1)}, s16[272,128]{1,0:T(8,128)(2,1)S(1)}, u32[]{:S(2)}, u32[]{:S(2)}) collective-permute-start(s16[272,128]{1,0:T(8,128)(2,1)S(1)} %code_mixed.1.refs_8_.refs_0_), channel_id=1, source_target_pairs={{0,1},{1,0},{2,3},{3,2},{4,5},{5,4},{6,7},{7,6},{8,9},{9,8},{10,11... | collective-permute-start | bytes 208904 | tf_op jit(solution)/shard_map/ppermute | solution.py:188
  51.4 1.4 %collective-permute-start.16 = (f32[64,512]{1,0:T(8,128)S(1)}, f32[64,512]{1,0:T(8,128)S(1)}, u32[]{:S(2)}, u32[]{:S(2)}) collective-permute-start(f32[64,512]{1,0:T(8,128)S(1)} %mean_protos.1.refs_4_), channel_id=1, source_target_pairs={{0,4},{4,0},{1,5},{5,1},{2,6},{6,2},{3,7},{7,3},{8,12},{12,8},{9,1... | collective-permute-start | bytes 393224 | tf_op jit(solution)/shard_map/ppermute | solution.py:188

commit v9 on v8

--- a/solution.py
+++ b/solution.py
@@ -565,7 +565,7 @@
     proto_devices = lax.axis_size("proto")
     crop_place = lax.axis_index("crop").reshape(1)
     proto_place = lax.axis_index("proto").reshape(1)
-    block = 512
+    block = 1024
 
     teacher_parts = [teacher_feats] + [swap(teacher_feats, "image", k) for k in range(1, image_devices)]
     feats = student_feats.reshape(crops * images, width)

time: 54.7 us -> 54.8 us (level)
  Pallas kernels: 16 us -> 15.3 us
  waiting for transfers between devices: 18.6 us -> 19.3 us
    ppermute x17, waiting for transfers between devices: 18.6 us -> 19.3 us  [swap(): return lax.ppermute(values, axis, [(i, i ^ distance) for i in range(count)])]
    pallas_call x13, Pallas kernels: 16 us -> 15.3 us  [run(): pl.pallas_call(body, in_specs=[IN_SMEM] * scalars + [IN_HBM if i in far e...]
  transfers between devices with their start and end apart: 17 -> 17, of which waited for: 11 -> 11; matrix products, arithmetic and copies ran while one was open for 0% -> 0% of each run, Pallas kernels for 16% -> 14%
where the time goes in v9:
time: 54.8 us; the launch traced here: 54.6 us
  waiting for transfers between devices  19.3 us (35%)
  starting transfers between devices  18.3 us (33%)
  Pallas kernels  15.3 us (28%)
  local copies, waits for them, and re-layouts  0.97 us (2%)
  between operations  0.79 us (1%)
    ppermute x17, waiting for transfers between devices, swap(): return lax.ppermute(values, axis, [(i, i ^ distance) for i in range(count)])  19.3 us
    ppermute x17, starting transfers between devices, swap(): return lax.ppermute(values, axis, [(i, i ^ distance) for i in range(count)])  18.3 us
    pallas_call x13, Pallas kernels, run(): pl.pallas_call(body, in_specs=[IN_SMEM] * scalars + [IN_HBM if i in far e...  15.3 us
  transfers between devices with their start and end apart: 17, of which 11 were waited for; matrix products, arithmetic and copies ran while one was open for 0% of the time, Pallas kernels for 14%

profile of v9, /device:TPU:0, one launch (start us, length us, event | category | flops | bytes accessed | tf_op | source)
XLA Modules:
  0.0 54.6 jit_solution(8992812309584294572)
XLA Ops:
  0.6 0.5 collective-permute-start.3
  1.1 2.6 %collective-permute-start.1 = (bf16[64,2,512]{2,1,0:T(2,128)(2,1)}, bf16[64,2,512]{2,1,0:T(2,128)(2,1)S(1)}, u32[]{:S(2)}, u32[]{:S(2)}) collective-permute-start(bf16[64,2,512]{2,1,0:T(2,128)(2,1)} %refs_0_.1), channel_id=1, source_target_pairs={{0,16},{8,24},{16,0},{24,8},{1,17},{9,25},{17,1},{25,9},{2,18},{10... | collective-permute-start | bytes 393224 | tf_op jit(solution)/shard_map/ppermute | solution.py:188
  3.7 1.5 %collective-permute-start = (bf16[64,2,512]{2,1,0:T(2,128)(2,1)}, bf16[64,2,512]{2,1,0:T(2,128)(2,1)S(1)}, u32[]{:S(2)}, u32[]{:S(2)}) collective-permute-start(bf16[64,2,512]{2,1,0:T(2,128)(2,1)} %refs_0_.1), channel_id=1, source_target_pairs={{0,8},{8,0},{16,24},{24,16},{1,9},{9,1},{17,25},{25,17},{2,10},{10... | collective-permute-start | bytes 393224 | tf_op jit(solution)/shard_map/ppermute | solution.py:188
  5.3 0.9 %copy-done = bf16[4,64,512]{2,1,0:T(8,128)(2,1)S(1)} copy-done((bf16[4,64,512]{2,1,0:T(8,128)(2,1)S(1)}, bf16[4,64,512]{2,1,0:T(8,128)(2,1)}, u32[]{:S(2)}) %copy-start) | copy-done | bytes 262168
  6.2 3.8 %student_own.1 = (bf16[512,2048]{1,0:T(8,128)(2,1)S(1)}, bf16[512,2048]{1,0:T(8,128)(2,1)S(1)}, bf16[256,512]{1,0:T(8,128)(2,1)S(1)}, f32[256,640]{1,0:T(8,128)S(1)}) custom-call(s32[1]{0:T(128)} %bitcast.refs_0_, s32[1]{0:T(128)} %bitcast.1.refs_1_.refs_0_, bf16[256,512]{1,0:T(8,128)(2,1)S(1)} %bitcast.3, bf16[512,2048]{1,0:T(8,128)(2,1)} %refs_3_.2, ...), custom_call_target="tpu_custom_call" | custom-call | flops 1073741824 | tf_op jit(solution)/shard_map/student_own/pallas_call | solution.py:36
  10.1 1.0 %student_begin.1.refs_5_.refs_2_ = f32[256,640]{1,0:T(8,128)S(1)} custom-call(bf16[256,512]{1,0:T(8,128)(2,1)S(1)} %get-tuple-element.23.refs_0_.refs_1_, f32[256,640]{1,0:T(8,128)S(1)} %get-tuple-element.24.refs_1_, bf16[512,2048]{1,0:T(8,128)(2,1)S(1)} %collective-permute-done.3.refs_2_.refs_3_), custom_call_target="tpu_custom_call" | custom-call | flops 536870912 | tf_op jit(solution)/shard_map/student_begin/pallas_call | solution.py:36
  11.1 0.9 %collective-permute-done.2.refs_3_ = bf16[64,2,512]{2,1,0:T(2,128)(2,1)S(1)} collective-permute-done((bf16[64,2,512]{2,1,0:T(2,128)(2,1)}, bf16[64,2,512]{2,1,0:T(2,128)(2,1)S(1)}, u32[]{:S(2)}, u32[]{:S(2)}) %collective-permute-start.2) | collective-permute-done | bytes 131104 | tf_op jit(solution)/shard_map/ppermute | solution.py:188
  12.1 2.6 %first_sweep.1 = (f32[512,2048]{1,0:T(8,128)S(1)}, f32[1,1,512]{2,1,0:T(1,128)S(1)}) custom-call(bf16[64,2,512]{2,1,0:T(2,128)(2,1)S(1)} %copy-done.1, bf16[64,2,512]{2,1,0:T(2,128)(2,1)S(1)} %collective-permute-done.refs_1_, bf16[64,2,512]{2,1,0:T(2,128)(2,1)S(1)} %collective-permute-done.1.refs_2_, bf16[64,2,512]{2,1,0:T(2,128)(2,1)S(1)} %collective-permute-done.2.refs_3_, ...), custom_call_target="tpu_custom_call" | custom-call | flops 4294967296 | tf_op jit(solution)/shard_map/first_sweep/pallas_call | solution.py:36
  14.8 1.4 %student_other.1 = (s16[272,128]{1,0:T(8,128)(2,1)S(1)}, s16[272,128]{1,0:T(8,128)(2,1)S(1)}, s16[272,128]{1,0:T(8,128)(2,1)S(1)}, s16[272,128]{1,0:T(8,128)(2,1)S(1)}) custom-call(s32[1]{0:T(128)} %bitcast.1.refs_1_.refs_0_, bf16[256,512]{1,0:T(8,128)(2,1)S(1)} %get-tuple-element.23.refs_0_.refs_1_, f32[256,640]{1,0:T(8,128)S(1)} %student_begin.1.refs_5_.refs_2_, ...), custom_call_target="tpu_custom_call" | custom-call | flops 1073741824 | tf_op jit(solution)/shard_map/student_other/pallas_call | solution.py:36
  16.3 1.9 %collective-permute-start.5 = (s16[272,128]{1,0:T(8,128)(2,1)S(1)}, s16[272,128]{1,0:T(8,128)(2,1)S(1)}, u32[]{:S(2)}, u32[]{:S(2)}) collective-permute-start(s16[272,128]{1,0:T(8,128)(2,1)S(1)} %get-tuple-element.32), channel_id=1, source_target_pairs={{0,1},{1,0},{2,3},{3,2},{4,5},{5,4},{6,7},{7,6},{8,9},{9,8},{10,11... | collective-permute-start | bytes 208904 | tf_op jit(solution)/shard_map/ppermute | solution.py:188
  18.2 2.6 %collective-permute-start.6 = (s16[272,128]{1,0:T(8,128)(2,1)S(1)}, s16[272,128]{1,0:T(8,128)(2,1)S(1)}, u32[]{:S(2)}, u32[]{:S(2)}) collective-permute-start(s16[272,128]{1,0:T(8,128)(2,1)S(1)} %get-tuple-element.33), channel_id=1, source_target_pairs={{0,2},{1,3},{2,0},{3,1},{4,6},{5,7},{6,4},{7,5},{8,10},{9,11},{10,... | collective-permute-start | bytes 208904 | tf_op jit(solution)/shard_map/ppermute | solution.py:188
  20.8 0.2 collective-permute-done.5.refs_2_.refs_1_
  21.0 5.1 %collective-permute-done.6.refs_3_.refs_2_ = s16[272,128]{1,0:T(8,128)(2,1)S(1)} collective-permute-done((s16[272,128]{1,0:T(8,128)(2,1)S(1)}, s16[272,128]{1,0:T(8,128)(2,1)S(1)}, u32[]{:S(2)}, u32[]{:S(2)}) %collective-permute-start.6) | collective-permute-done | bytes 69664 | tf_op jit(solution)/shard_map/ppermute | solution.py:188
  26.0 0.9 %collective-permute-done.7.refs_4_.refs_3_ = s16[272,128]{1,0:T(8,128)(2,1)S(1)} collective-permute-done((s16[272,128]{1,0:T(8,128)(2,1)S(1)}, s16[272,128]{1,0:T(8,128)(2,1)S(1)}, u32[]{:S(2)}, u32[]{:S(2)}) %collective-permute-start.7) | collective-permute-done | bytes 69664 | tf_op jit(solution)/shard_map/ppermute | solution.py:188
  26.9 1.0 %sweep.1 = (f32[1,1,512]{2,1,0:T(1,128)S(1)}, f32[512,2048]{1,0:T(8,128)S(1)}) custom-call(f32[512,2048]{1,0:T(8,128)S(1)} %get-tuple-element.25.refs_0_, s16[272,128]{1,0:T(8,128)(2,1)S(1)} %get-tuple-element.31.refs_1_.refs_0_, s16[272,128]{1,0:T(8,128)(2,1)S(1)} %collective-permute-done.5.refs_2_.refs_1_, ...), custom_call_target="tpu_custom_call", output_to_operand_aliasing={{1}: (0, {})} | custom-call | flops 1000000000 | tf_op jit(solution)/shard_map/sweep/pallas_call | solution.py:36
  28.0 0.5 %student_totals.1.refs_2_ = s16[272,128]{1,0:T(8,128)(2,1)S(1)} custom-call(s16[272,128]{1,0:T(8,128)(2,1)S(1)} %get-tuple-element.31.refs_1_.refs_0_, s16[272,128]{1,0:T(8,128)(2,1)S(1)} %collective-permute-done.5.refs_2_.refs_1_, s16[272,128]{1,0:T(8,128)(2,1)S(1)} %collective-permute-done.6.refs_3_.refs_2_, ...), custom_call_target="tpu_custom_call" | custom-call | flops 1000000000 | tf_op jit(solution)/shard_map/student_totals/pallas_call | solution.py:36
  28.5 0.6 %collective-permute-done.8.refs_1_ = f32[1,1,512]{2,1,0:T(1,128)S(1)} collective-permute-done((f32[1,1,512]{2,1,0:T(1,128)S(1)}, f32[1,1,512]{2,1,0:T(1,128)S(1)}, u32[]{:S(2)}, u32[]{:S(2)}) %collective-permute-start.8) | collective-permute-done | bytes 2080 | tf_op jit(solution)/shard_map/ppermute | solution.py:188
  29.2 2.7 %collective-permute-start.11 = (s16[272,128]{1,0:T(8,128)(2,1)S(1)}, s16[272,128]{1,0:T(8,128)(2,1)S(1)}, u32[]{:S(2)}, u32[]{:S(2)}) collective-permute-start(s16[272,128]{1,0:T(8,128)(2,1)S(1)} %pack_sums.3.refs_3_.refs_4_), channel_id=1, source_target_pairs={{0,3},{1,2},{2,1},{3,0},{4,7},{5,6},{6,5},{7,4},{8,11},{9,10},{10,... | collective-permute-start | bytes 208904 | tf_op jit(solution)/shard_map/ppermute | solution.py:188
  31.8 0.3 collective-permute-start.10
  32.2 1.4 %collective-permute-start.9 = (s16[272,128]{1,0:T(8,128)(2,1)S(1)}, s16[272,128]{1,0:T(8,128)(2,1)S(1)}, u32[]{:S(2)}, u32[]{:S(2)}) collective-permute-start(s16[272,128]{1,0:T(8,128)(2,1)S(1)} %pack_sums.3.refs_3_.refs_4_), channel_id=1, source_target_pairs={{0,1},{1,0},{2,3},{3,2},{4,5},{5,4},{6,7},{7,6},{8,9},{9,8},{10,11... | collective-permute-start | bytes 208904 | tf_op jit(solution)/shard_map/ppermute | solution.py:188
  33.6 2.1 %collective-permute-done.11.refs_6_.refs_7_ = s16[272,128]{1,0:T(8,128)(2,1)S(1)} collective-permute-done((s16[272,128]{1,0:T(8,128)(2,1)S(1)}, s16[272,128]{1,0:T(8,128)(2,1)S(1)}, u32[]{:S(2)}, u32[]{:S(2)}) %collective-permute-start.11) | collective-permute-done | bytes 69664 | tf_op jit(solution)/shard_map/ppermute | solution.py:188
  35.7 3.2 %collective-permute-done.10.refs_5_.refs_6_ = s16[272,128]{1,0:T(8,128)(2,1)S(1)} collective-permute-done((s16[272,128]{1,0:T(8,128)(2,1)S(1)}, s16[272,128]{1,0:T(8,128)(2,1)S(1)}, u32[]{:S(2)}, u32[]{:S(2)}) %collective-permute-start.10) | collective-permute-done | bytes 69664 | tf_op jit(solution)/shard_map/ppermute | solution.py:188
  38.9 1.4 %last_sweep.1 = (f32[64,640]{1,0:T(8,128)S(1)}, f32[64,640]{1,0:T(8,128)S(1)}) custom-call(s32[1]{0:T(128)} %bitcast.refs_0_, f32[512,2048]{1,0:T(8,128)S(1)} %get-tuple-element.36.refs_1_, bf16[512,2048]{1,0:T(8,128)(2,1)S(1)} %get-tuple-element.37.refs_2_, s16[272,128]{1,0:T(8,128)(2,1)S(1)} %pack_sums.3.refs_3_.refs_4_, ...), custom_call_target="tpu_custom_call" | custom-call | flops 1000000000 | tf_op jit(solution)/shard_map/last_sweep/pallas_call | solution.py:36
  40.5 1.4 %collective-permute-done.12.refs_1_ = f32[64,640]{1,0:T(8,128)S(1)} collective-permute-done((f32[64,640]{1,0:T(8,128)S(1)}, f32[64,640]{1,0:T(8,128)S(1)}, u32[]{:S(2)}, u32[]{:S(2)}) %collective-permute-start.12) | collective-permute-done | bytes 163872 | tf_op jit(solution)/shard_map/ppermute | solution.py:188
  42.1 2.5 %collective-permute-start.15 = (s16[272,128]{1,0:T(8,128)(2,1)S(1)}, s16[272,128]{1,0:T(8,128)(2,1)S(1)}, u32[]{:S(2)}, u32[]{:S(2)}) collective-permute-start(s16[272,128]{1,0:T(8,128)(2,1)S(1)} %code_mixed.1.refs_8_.refs_0_), channel_id=1, source_target_pairs={{0,3},{1,2},{2,1},{3,0},{4,7},{5,6},{6,5},{7,4},{8,11},{9,10},{10,... | collective-permute-start | bytes 208904 | tf_op jit(solution)/shard_map/ppermute | solution.py:188
  44.5 2.0 %collective-permute-start.13 = (s16[272,128]{1,0:T(8,128)(2,1)S(1)}, s16[272,128]{1,0:T(8,128)(2,1)S(1)}, u32[]{:S(2)}, u32[]{:S(2)}) collective-permute-start(s16[272,128]{1,0:T(8,128)(2,1)S(1)} %code_mixed.1.refs_8_.refs_0_), channel_id=1, source_target_pairs={{0,1},{1,0},{2,3},{3,2},{4,5},{5,4},{6,7},{7,6},{8,9},{9,8},{10,11... | collective-permute-start | bytes 208904 | tf_op jit(solution)/shard_map/ppermute | solution.py:188
  46.5 1.0 %prepare.1 = (f32[256,512]{1,0:T(8,128)S(1)}, f32[256,128]{1,0:T(8,128)S(1)}) custom-call(s32[1]{0:T(128)} %bitcast.1.refs_1_.refs_0_, bf16[4,64,512]{2,1,0:T(8,128)(2,1)S(1)} %copy-done, s32[4,64]{1,0:T(4,128)S(1)} %copy-done.2, bf16[4,64]{1,0:T(4,128)(2,1)S(1)} %copy-done.3, s16[272,128]{1,0:T(8,128)(2,1)S(1)} %pack_sums.3.refs_3_.refs_4_, ...), custom_call_target="tpu_custom_call" | custom-call | flops 1000000000 | tf_op jit(solution)/shard_map/prepare/pallas_call | solution.py:36
  47.5 1.4 %collective-permute-done.15.refs_3_ = s16[272,128]{1,0:T(8,128)(2,1)S(1)} collective-permute-done((s16[272,128]{1,0:T(8,128)(2,1)S(1)}, s16[272,128]{1,0:T(8,128)(2,1)S(1)}, u32[]{:S(2)}, u32[]{:S(2)}) %collective-permute-start.15) | collective-permute-done | bytes 69664 | tf_op jit(solution)/shard_map/ppermute | solution.py:188
  49.0 2.1 %collective-permute-done.14.refs_2_ = s16[272,128]{1,0:T(8,128)(2,1)S(1)} collective-permute-done((s16[272,128]{1,0:T(8,128)(2,1)S(1)}, s16[272,128]{1,0:T(8,128)(2,1)S(1)}, u32[]{:S(2)}, u32[]{:S(2)}) %collective-permute-start.14) | collective-permute-done | bytes 69664 | tf_op jit(solution)/shard_map/ppermute | solution.py:188
  51.1 0.4 mean_protos.1.refs_4_
  51.6 1.3 %collective-permute-done.16.refs_5_ = f32[64,512]{1,0:T(8,128)S(1)} collective-permute-done((f32[64,512]{1,0:T(8,128)S(1)}, f32[64,512]{1,0:T(8,128)S(1)}, u32[]{:S(2)}, u32[]{:S(2)}) %collective-permute-start.16) | collective-permute-done | bytes 131104 | tf_op jit(solution)/shard_map/ppermute | solution.py:188
  52.9 1.7 %finish.1 = (f32[4,64,512]{2,1,0:T(8,128)}, f32[4,64]{1,0:T(4,128)}) custom-call(s32[1]{0:T(128)} %bitcast.refs_0_, bf16[4,64,512]{2,1,0:T(8,128)(2,1)S(1)} %copy-done, f32[256,512]{1,0:T(8,128)S(1)} %get-tuple-element.40.refs_4_.refs_2_, f32[256,128]{1,0:T(8,128)S(1)} %get-tuple-element.41.refs_3_, f32[64,512]{1,0:T(8,128)S(1)} %mean_protos.1.refs_4_, ...), custom_call_target="tpu_custom_call" | custom-call | flops 1000000000 | tf_op jit(solution)/shard_map/finish/pallas_call | solution.py:36
  (23 shorter events, 0.7 us)
Async XLA Ops:
  0.6 9.4 %collective-permute-start.3 = (bf16[512,2048]{1,0:T(8,128)(2,1)}, bf16[512,2048]{1,0:T(8,128)(2,1)S(1)}, u32[]{:S(2)}, u32[]{:S(2)}) collective-permute-start(bf16[512,2048]{1,0:T(8,128)(2,1)} %refs_3_.2), channel_id=1, source_target_pairs={{0,4},{4,0},{1,5},{5,1},{2,6},{6,2},{3,7},{7,3},{8,12},{12,8},{9,1... | collective-permute-start | bytes 6291464 | tf_op jit(solution)/shard_map/ppermute | solution.py:188
  1.1 10.0 %collective-permute-start.1 = (bf16[64,2,512]{2,1,0:T(2,128)(2,1)}, bf16[64,2,512]{2,1,0:T(2,128)(2,1)S(1)}, u32[]{:S(2)}, u32[]{:S(2)}) collective-permute-start(bf16[64,2,512]{2,1,0:T(2,128)(2,1)} %refs_0_.1), channel_id=1, source_target_pairs={{0,16},{8,24},{16,0},{24,8},{1,17},{9,25},{17,1},{25,9},{2,18},{10... | collective-permute-start | bytes 393224 | tf_op jit(solution)/shard_map/ppermute | solution.py:188
  3.7 7.4 %collective-permute-start = (bf16[64,2,512]{2,1,0:T(2,128)(2,1)}, bf16[64,2,512]{2,1,0:T(2,128)(2,1)S(1)}, u32[]{:S(2)}, u32[]{:S(2)}) collective-permute-start(bf16[64,2,512]{2,1,0:T(2,128)(2,1)} %refs_0_.1), channel_id=1, source_target_pairs={{0,8},{8,0},{16,24},{24,16},{1,9},{9,1},{17,25},{25,17},{2,10},{10... | collective-permute-start | bytes 393224 | tf_op jit(solution)/shard_map/ppermute | solution.py:188
  5.2 6.8 %collective-permute-start.2 = (bf16[64,2,512]{2,1,0:T(2,128)(2,1)}, bf16[64,2,512]{2,1,0:T(2,128)(2,1)S(1)}, u32[]{:S(2)}, u32[]{:S(2)}) collective-permute-start(bf16[64,2,512]{2,1,0:T(2,128)(2,1)} %refs_0_.1), channel_id=1, source_target_pairs={{0,24},{8,16},{16,8},{24,0},{1,25},{9,17},{17,9},{25,1},{2,26},{10... | collective-permute-start | bytes 393224 | tf_op jit(solution)/shard_map/ppermute | solution.py:188
  5.3 0.9 %copy-start = (bf16[4,64,512]{2,1,0:T(8,128)(2,1)S(1)}, bf16[4,64,512]{2,1,0:T(8,128)(2,1)}, u32[]{:S(2)}) copy-start(bf16[4,64,512]{2,1,0:T(8,128)(2,1)} %refs_1_.3) | copy-start | bytes 786436
  10.0 2.0 %copy-start.1 = (bf16[64,2,512]{2,1,0:T(2,128)(2,1)S(1)}, bf16[64,2,512]{2,1,0:T(2,128)(2,1)}, u32[]{:S(2)}) copy-start(bf16[64,2,512]{2,1,0:T(2,128)(2,1)} %refs_0_.1) | copy-start | bytes 393220
  14.7 1.5 %collective-permute-start.4 = (f32[1,1,512]{2,1,0:T(1,128)S(1)}, f32[1,1,512]{2,1,0:T(1,128)S(1)}, u32[]{:S(2)}, u32[]{:S(2)}) collective-permute-start(f32[1,1,512]{2,1,0:T(1,128)S(1)} %get-tuple-element.26.refs_0_), channel_id=1, source_target_pairs={{0,4},{4,0},{1,5},{5,1},{2,6},{6,2},{3,7},{7,3},{8,12},{12,8},{9,1... | collective-permute-start | bytes 6152 | tf_op jit(solution)/shard_map/ppermute | solution.py:188
  16.3 4.7 %collective-permute-start.5 = (s16[272,128]{1,0:T(8,128)(2,1)S(1)}, s16[272,128]{1,0:T(8,128)(2,1)S(1)}, u32[]{:S(2)}, u32[]{:S(2)}) collective-permute-start(s16[272,128]{1,0:T(8,128)(2,1)S(1)} %get-tuple-element.32), channel_id=1, source_target_pairs={{0,1},{1,0},{2,3},{3,2},{4,5},{5,4},{6,7},{7,6},{8,9},{9,8},{10,11... | collective-permute-start | bytes 208904 | tf_op jit(solution)/shard_map/ppermute | solution.py:188
  18.2 7.9 %collective-permute-start.6 = (s16[272,128]{1,0:T(8,128)(2,1)S(1)}, s16[272,128]{1,0:T(8,128)(2,1)S(1)}, u32[]{:S(2)}, u32[]{:S(2)}) collective-permute-start(s16[272,128]{1,0:T(8,128)(2,1)S(1)} %get-tuple-element.33), channel_id=1, source_target_pairs={{0,2},{1,3},{2,0},{3,1},{4,6},{5,7},{6,4},{7,5},{8,10},{9,11},{10,... | collective-permute-start | bytes 208904 | tf_op jit(solution)/shard_map/ppermute | solution.py:188
  20.8 6.2 %collective-permute-start.7 = (s16[272,128]{1,0:T(8,128)(2,1)S(1)}, s16[272,128]{1,0:T(8,128)(2,1)S(1)}, u32[]{:S(2)}, u32[]{:S(2)}) collective-permute-start(s16[272,128]{1,0:T(8,128)(2,1)S(1)} %get-tuple-element.34), channel_id=1, source_target_pairs={{0,3},{1,2},{2,1},{3,0},{4,7},{5,6},{6,5},{7,4},{8,11},{9,10},{10,... | collective-permute-start | bytes 208904 | tf_op jit(solution)/shard_map/ppermute | solution.py:188
  27.9 1.2 %collective-permute-start.8 = (f32[1,1,512]{2,1,0:T(1,128)S(1)}, f32[1,1,512]{2,1,0:T(1,128)S(1)}, u32[]{:S(2)}, u32[]{:S(2)}) collective-permute-start(f32[1,1,512]{2,1,0:T(1,128)S(1)} %get-tuple-element.35.refs_4_.refs_0_), channel_id=1, source_target_pairs={{0,4},{4,0},{1,5},{5,1},{2,6},{6,2},{3,7},{7,3},{8,12},{12,8},{9,1... | collective-permute-start | bytes 6152 | tf_op jit(solution)/shard_map/ppermute | solution.py:188
  29.2 6.6 %collective-permute-start.11 = (s16[272,128]{1,0:T(8,128)(2,1)S(1)}, s16[272,128]{1,0:T(8,128)(2,1)S(1)}, u32[]{:S(2)}, u32[]{:S(2)}) collective-permute-start(s16[272,128]{1,0:T(8,128)(2,1)S(1)} %pack_sums.3.refs_3_.refs_4_), channel_id=1, source_target_pairs={{0,3},{1,2},{2,1},{3,0},{4,7},{5,6},{6,5},{7,4},{8,11},{9,10},{10,... | collective-permute-start | bytes 208904 | tf_op jit(solution)/shard_map/ppermute | solution.py:188
  31.8 7.1 %collective-permute-start.10 = (s16[272,128]{1,0:T(8,128)(2,1)S(1)}, s16[272,128]{1,0:T(8,128)(2,1)S(1)}, u32[]{:S(2)}, u32[]{:S(2)}) collective-permute-start(s16[272,128]{1,0:T(8,128)(2,1)S(1)} %pack_sums.3.refs_3_.refs_4_), channel_id=1, source_target_pairs={{0,2},{1,3},{2,0},{3,1},{4,6},{5,7},{6,4},{7,5},{8,10},{9,11},{10,... | collective-permute-start | bytes 208904 | tf_op jit(solution)/shard_map/ppermute | solution.py:188
  32.2 6.8 %collective-permute-start.9 = (s16[272,128]{1,0:T(8,128)(2,1)S(1)}, s16[272,128]{1,0:T(8,128)(2,1)S(1)}, u32[]{:S(2)}, u32[]{:S(2)}) collective-permute-start(s16[272,128]{1,0:T(8,128)(2,1)S(1)} %pack_sums.3.refs_3_.refs_4_), channel_id=1, source_target_pairs={{0,1},{1,0},{2,3},{3,2},{4,5},{5,4},{6,7},{7,6},{8,9},{9,8},{10,11... | collective-permute-start | bytes 208904 | tf_op jit(solution)/shard_map/ppermute | solution.py:188
  40.4 6.1 %copy-start.2 = (s32[4,64]{1,0:T(4,128)S(1)}, s32[4,64]{1,0:T(4,128)}, u32[]{:S(2)}) copy-start(s32[4,64]{1,0:T(4,128)} %refs_2_.1) | copy-start | bytes 3076
  40.4 6.1 %copy-start.3 = (bf16[4,64]{1,0:T(4,128)(2,1)S(1)}, bf16[4,64]{1,0:T(4,128)(2,1)}, u32[]{:S(2)}) copy-start(bf16[4,64]{1,0:T(4,128)(2,1)} %refs_3_.3) | copy-start | bytes 1540
  40.4 1.5 %collective-permute-start.12 = (f32[64,640]{1,0:T(8,128)S(1)}, f32[64,640]{1,0:T(8,128)S(1)}, u32[]{:S(2)}, u32[]{:S(2)}) collective-permute-start(f32[64,640]{1,0:T(8,128)S(1)} %get-tuple-element.39), channel_id=1, source_target_pairs={{0,4},{4,0},{1,5},{5,1},{2,6},{6,2},{3,7},{7,3},{8,12},{12,8},{9,1... | collective-permute-start | bytes 491528 | tf_op jit(solution)/shard_map/ppermute | solution.py:188
  42.1 6.9 %collective-permute-start.15 = (s16[272,128]{1,0:T(8,128)(2,1)S(1)}, s16[272,128]{1,0:T(8,128)(2,1)S(1)}, u32[]{:S(2)}, u32[]{:S(2)}) collective-permute-start(s16[272,128]{1,0:T(8,128)(2,1)S(1)} %code_mixed.1.refs_8_.refs_0_), channel_id=1, source_target_pairs={{0,3},{1,2},{2,1},{3,0},{4,7},{5,6},{6,5},{7,4},{8,11},{9,10},{10,... | collective-permute-start | bytes 208904 | tf_op jit(solution)/shard_map/ppermute | solution.py:188
  44.5 6.6 %collective-permute-start.14 = (s16[272,128]{1,0:T(8,128)(2,1)S(1)}, s16[272,128]{1,0:T(8,128)(2,1)S(1)}, u32[]{:S(2)}, u32[]{:S(2)}) collective-permute-start(s16[272,128]{1,0:T(8,128)(2,1)S(1)} %code_mixed.1.refs_8_.refs_0_), channel_id=1, source_target_pairs={{0,2},{1,3},{2,0},{3,1},{4,6},{5,7},{6,4},{7,5},{8,10},{9,11},{10,... | collective-permute-start | bytes 208904 | tf_op jit(solution)/shard_map/ppermute | solution.py:188
  44.5 6.6 %collective-permute-start.13 = (s16[272,128]{1,0:T(8,128)(2,1)S(1)}, s16[272,128]{1,0:T(8,128)(2,1)S(1)}, u32[]{:S(2)}, u32[]{:S(2)}) collective-permute-start(s16[272,128]{1,0:T(8,128)(2,1)S(1)} %code_mixed.1.refs_8_.refs_0_), channel_id=1, source_target_pairs={{0,1},{1,0},{2,3},{3,2},{4,5},{5,4},{6,7},{7,6},{8,9},{9,8},{10,11... | collective-permute-start | bytes 208904 | tf_op jit(solution)/shard_map/ppermute | solution.py:188
  51.5 1.4 %collective-permute-start.16 = (f32[64,512]{1,0:T(8,128)S(1)}, f32[64,512]{1,0:T(8,128)S(1)}, u32[]{:S(2)}, u32[]{:S(2)}) collective-permute-start(f32[64,512]{1,0:T(8,128)S(1)} %mean_protos.1.refs_4_), channel_id=1, source_target_pairs={{0,4},{4,0},{1,5},{5,1},{2,6},{6,2},{3,7},{7,3},{8,12},{12,8},{9,1... | collective-permute-start | bytes 393224 | tf_op jit(solution)/shard_map/ppermute | solution.py:188
